TPU v7x, 512 devices: a whole 4x8x8 slice. The times are simulated.
512 devices in a mesh: lon: 32 (over z_hi, x, core), lat: 16 (over y, z_lo).
Axes of the slice: x: 4, y: 8, z: 8 (z_hi: 4, z_lo: 2; z = z_hi * 2 + z_lo), core: 2. Of those that a mesh axis runs over, the one named last changes fastest.
Arguments:
- fields: bfloat16 [96, 128, 8192], P(None, 'lat', 'lon'), may hold values from -6 to 6
- land_mask: int32 [128, 8192], P('lat', 'lon'), may hold values from 0 to 1, as said below
- dw_kernel: float32 [96, 7, 7], replicated, may hold values from -0.875 to 0.875
- gain: float32 [96], replicated, may hold values from 0.1 to 1.9
- w_in: bfloat16 [96, 192], replicated, may hold values from -0.625 to 0.625
- b_in: float32 [192], replicated, may hold values from -3 to 3
- w_out: bfloat16 [192, 96], replicated, may hold values from -0.4375 to 0.4375
- cotangent: bfloat16 [96, 128, 8192], P(None, 'lat', 'lon'), may hold values from -6 to 6
Outputs:
- output: bfloat16 [96, 128, 8192], P(None, 'lat', 'lon')
- input_grad: bfloat16 [96, 128, 8192], P(None, 'lat', 'lon')
- kernel_grad: float32 [96, 7, 7], replicated
- gain_grad: float32 [96], replicated
- w_in_grad: float32 [96, 192], replicated
- b_in_grad: float32 [192], replicated
- w_out_grad: float32 [192, 96], replicated
Inputs may be any that keep to these rules, and one draw needn't show every extreme that they name: `land_mask`: 1 marks a sea cell and 0 a land cell.
All inputs are finite; a program needn't handle non-finite values.
Results may differ from a plain program's by a relative error of at most 0.009.
Values may be sent and summed in bfloat16 or wider, within the bound.
No kernel may reach another device: no remote copies, remote signals or barrier semaphores. Data moves between devices by JAX's collectives and lax.ppermute only.
A program may use at most 192 MiB of HBM per device.

v0:
```python
import jax
import jax.numpy as jnp
from jax import lax
from jax.sharding import PartitionSpec as P


def from_partner(block, axis, stride):
    count = lax.axis_size(axis)
    route = []
    for low in range(count):
        high = low | 1 << stride
        if high != low and high < count:
            route += [(low, high), (high, low)]
    return lax.ppermute(block, axis, route)


def extended(shard, sides, width, wrap):
    for axis, dim in sides:
        size, length = (lax.axis_size(axis), shard.shape[dim])
        up = [(i, (i + 1) % size) for i in range(size if wrap else size - 1)]
        down = [(j, i) for i, j in up]
        last = lax.slice_in_dim(shard, length - width, length, axis=dim)
        first = lax.slice_in_dim(shard, 0, width, axis=dim)
        before = lax.ppermute(last, axis, up)
        after = lax.ppermute(first, axis, down)
        shard = jnp.concatenate([before, shard, after], axis=dim)
    return shard


def mirror_forward(values):
    steps_count = lax.axis_size("lon").bit_length() - 1
    for bit_pos in range(steps_count):
        values = from_partner(values, "lon", bit_pos)
    return values[:, ::-1, ::-1]


def mirror_backward(values):
    steps_count = lax.axis_size("lon").bit_length() - 1
    for bit_pos in range(steps_count):
        values = from_partner(values.astype(jnp.bfloat16), "lon", bit_pos).astype(values.dtype)
    return values[:, ::-1, ::-1]


def convolve(padded, kernel, tile_rows, tile_cols):
    summed = jnp.zeros((padded.shape[0], tile_rows, tile_cols), jnp.float32)
    for row_off in range(7):
        for col_off in range(7):
            window = padded[:, row_off : row_off + tile_rows, col_off : col_off + tile_cols].astype(
                jnp.float32
            )
            summed = summed + kernel[:, row_off, col_off][:, None, None] * window
    return summed


def spread_back(conv_grad, kernel):
    channels, tile_rows, tile_cols = conv_grad.shape
    bordered = jnp.pad(conv_grad, ((0, 0), (6, 6), (6, 6)))
    summed = jnp.zeros((channels, tile_rows + 6, tile_cols + 6), jnp.float32)
    for row_off in range(7):
        for col_off in range(7):
            window = bordered[
                :, 6 - row_off : 12 - row_off + tile_rows, 6 - col_off : 12 - col_off + tile_cols
            ]
            summed = summed + kernel[:, row_off, col_off][:, None, None] * window
    return summed


def kernel_terms(conv_grad, padded):
    channels, tile_rows, tile_cols = conv_grad.shape
    terms = []
    for row_off in range(7):
        for col_off in range(7):
            window = padded[:, row_off : row_off + tile_rows, col_off : col_off + tile_cols].astype(
                jnp.float32
            )
            terms.append(jnp.sum(conv_grad * window, axis=(1, 2)))
    return jnp.stack(terms, axis=1).reshape(channels, 7, 7)


def shards(fields, land_mask, dw_kernel, gain, w_in, b_in, w_out, cotangent):
    channels, tile_rows, tile_cols = fields.shape
    sea_mask = land_mask.astype(jnp.bfloat16)[None]
    masked = fields * sea_mask
    back_sea = cotangent * sea_mask
    lat_pos = lax.axis_index("lat")
    is_bottom = lat_pos == 0
    is_top = lat_pos == lax.axis_size("lat") - 1
    padded = extended(masked, (("lon", 2), ("lat", 1)), 3, True)
    folded = mirror_forward(padded[:, tile_rows : tile_rows + 3, :])
    south = jnp.where(is_bottom, jnp.zeros_like(padded[:, :3, :]), padded[:, :3, :])
    north = jnp.where(is_top, folded, padded[:, tile_rows + 3 :, :])
    padded = jnp.concatenate([south, padded[:, 3 : tile_rows + 3, :], north], axis=1)
    conv_out = convolve(padded, dw_kernel, tile_rows, tile_cols)
    centred = conv_out - jnp.mean(conv_out, axis=0, keepdims=True)
    inv_std = lax.rsqrt(jnp.mean(centred * centred, axis=0, keepdims=True) + 1e-06)
    normed = centred * inv_std
    scaled = (normed * gain[:, None, None]).astype(jnp.bfloat16)
    hidden_pre = (
        jnp.einsum("ch,cxy->hxy", w_in, scaled, preferred_element_type=jnp.float32)
        + b_in[:, None, None]
    )
    activated, gelu_pull = jax.vjp(jax.nn.gelu, hidden_pre)
    activated = activated.astype(jnp.bfloat16)
    mixed = jnp.einsum("hc,hxy->cxy", w_out, activated, preferred_element_type=jnp.float32)
    centre = padded[:, 3 : tile_rows + 3, 3 : tile_cols + 3].astype(jnp.float32)
    output = (sea_mask * (centre + mixed)).astype(jnp.bfloat16)
    w_out_part = jnp.einsum("hxy,cxy->hc", activated, back_sea, preferred_element_type=jnp.float32)
    act_grad = jnp.einsum("hc,cxy->hxy", w_out, back_sea, preferred_element_type=jnp.float32)
    pre_grad = gelu_pull(act_grad)[0].astype(jnp.bfloat16)
    output, w_out_part, pre_grad, scaled, normed, inv_std = (
        output,
        w_out_part,
        pre_grad,
        scaled,
        normed,
        inv_std,
    )
    b_part = jnp.sum(pre_grad.astype(jnp.float32), axis=(1, 2))
    w_in_part = jnp.einsum("cxy,hxy->ch", scaled, pre_grad, preferred_element_type=jnp.float32)
    scaled_grad = jnp.einsum("ch,hxy->cxy", w_in, pre_grad, preferred_element_type=jnp.float32)
    gain_part = jnp.sum(scaled_grad * normed, axis=(1, 2))
    norm_grad = scaled_grad * gain[:, None, None]
    conv_grad = inv_std * (
        norm_grad
        - jnp.mean(norm_grad, axis=0, keepdims=True)
        - normed * jnp.mean(norm_grad * normed, axis=0, keepdims=True)
    )
    kernel_part = kernel_terms(conv_grad, padded)
    ext_grad = spread_back(conv_grad, dw_kernel)
    kernel_part, gain_part, w_in_part, b_part, ext_grad = (
        kernel_part,
        gain_part,
        w_in_part,
        b_part,
        ext_grad,
    )
    kernel_sum, gain_sum, w_in_sum, b_sum, w_out_sum = lax.psum(
        (kernel_part, gain_part, w_in_part, b_part, w_out_part), ("lon", "lat")
    )
    returned = mirror_backward(ext_grad[:, tile_rows + 3 :, :])
    ext_grad = ext_grad.at[:, tile_rows : tile_rows + 3, :].add(
        jnp.where(is_top, returned, jnp.zeros_like(returned))
    )
    rims = jnp.concatenate([ext_grad[:, :3, :], ext_grad[:, tile_rows + 3 :, :]], axis=1)
    got_rows = extended(rims.astype(jnp.bfloat16), (("lat", 1),), 3, False).astype(rims.dtype)
    inner = ext_grad[:, 3 : tile_rows + 3, :]
    inner = inner.at[:, :3, :].add(got_rows[:, :3, :])
    inner = inner.at[:, tile_rows - 3 :, :].add(got_rows[:, 9:, :])
    sides = jnp.concatenate([inner[:, :, :3], inner[:, :, tile_cols + 3 :]], axis=2)
    sides = jnp.transpose(sides, (2, 0, 1)).reshape(6, channels * tile_rows)
    got_cols = extended(sides, (("lon", 0),), 3, True)
    from_left = jnp.transpose(got_cols[:3].reshape(3, channels, tile_rows), (1, 2, 0))
    from_right = jnp.transpose(got_cols[9:].reshape(3, channels, tile_rows), (1, 2, 0))
    core = inner[:, :, 3 : tile_cols + 3]
    core = core.at[:, :, :3].add(from_left)
    core = core.at[:, :, tile_cols - 3 :].add(from_right)
    input_grad = (sea_mask * (core + back_sea.astype(jnp.float32))).astype(jnp.bfloat16)
    scale_factor = float(tile_rows * tile_cols * lax.axis_size("lat") * lax.axis_size("lon")) ** (
        -0.5
    )
    return (
        output,
        input_grad,
        kernel_sum * scale_factor,
        gain_sum * scale_factor,
        w_in_sum * scale_factor,
        b_sum * scale_factor,
        w_out_sum * scale_factor,
    )


def solution(mesh):
    return jax.shard_map(
        shards,
        mesh=mesh,
        in_specs=(
            P(None, "lat", "lon"),
            P("lat", "lon"),
            P(),
            P(),
            P(),
            P(),
            P(),
            P(None, "lat", "lon"),
        ),
        out_specs=(P(None, "lat", "lon"), P(None, "lat", "lon"), P(), P(), P(), P(), P()),
        check_vma=False,
    )
```

profile of v0, /device:TPU:1, one launch (start us, length us, event | category | flops | bytes accessed | tf_op | source)
XLA Modules:
  0.0 447.0 jit_solution(8596428200641927452)
XLA Ops:
  7.2 0.7 fusion.225
  7.9 1.1 copy_multiply_fusion.1
  9.1 4.5 %collective-permute-start = (bf16[96,8,3]{2,0,1:T(8,128)(2,1)S(1)}, bf16[96,8,3]{2,0,1:T(8,128)(2,1)S(1)}, u32[]{:S(2)}, u32[]{:S(2)}) collective-permute-start(bf16[96,8,3]{2,0,1:T(8,128)(2,1)S(1)} %get-tuple-element.168), channel_id=1, source_target_pairs={{0,16},{16,32},{32,48},{48,64},{64,80},{80,96},{96,112},{112,128},... | collective-permute-start | bytes 13832 | tf_op jit(solution)/shard_map/ppermute | solution.py:24
  13.7 6.2 %collective-permute-start.1 = (bf16[96,8,3]{2,0,1:T(8,128)(2,1)S(1)}, bf16[96,8,3]{2,0,1:T(8,128)(2,1)S(1)}, u32[]{:S(2)}, u32[]{:S(2)}) collective-permute-start(bf16[96,8,3]{2,0,1:T(8,128)(2,1)S(1)} %get-tuple-element.169), channel_id=1, source_target_pairs={{16,0},{32,16},{48,32},{64,48},{80,64},{96,80},{112,96},{128,112},... | collective-permute-start | bytes 13832 | tf_op jit(solution)/shard_map/ppermute | solution.py:25
  19.9 1.0 collective-permute-done.1
  21.2 12.1 %collective-permute-start.3 = (bf16[96,3,262]{2,0,1:T(8,128)(2,1)S(1)}, bf16[96,3,262]{2,0,1:T(8,128)(2,1)S(1)}, u32[]{:S(2)}, u32[]{:S(2)}) collective-permute-start(bf16[96,3,262]{2,0,1:T(8,128)(2,1)S(1)} %get-tuple-element.167), channel_id=1, source_target_pairs={{0,16},{16,0},{32,48},{48,32},{64,80},{80,64},{96,112},{112,96},{1... | collective-permute-start | bytes 452744 | tf_op jit(solution)/shard_map/ppermute | solution.py:14
  33.3 1.1 collective-permute-done.3
  34.4 1.9 collective-permute-start.4
  36.4 6.4 %collective-permute-done.4 = bf16[96,3,262]{2,0,1:T(8,128)(2,1)S(1)} collective-permute-done((bf16[96,3,262]{2,0,1:T(8,128)(2,1)S(1)}, bf16[96,3,262]{2,0,1:T(8,128)(2,1)S(1)}, u32[]{:S(2)}, u32[]{:S(2)}) %collective-permute-start.4) | collective-permute-done | bytes 150944 | tf_op jit(solution)/shard_map/ppermute | solution.py:14
  42.9 2.3 collective-permute-start.5
  45.4 1.9 collective-permute-start.2
  47.4 4.6 %collective-permute-done.5 = bf16[96,3,262]{2,0,1:T(8,128)(2,1)S(1)} collective-permute-done((bf16[96,3,262]{2,0,1:T(8,128)(2,1)S(1)}, bf16[96,3,262]{2,0,1:T(8,128)(2,1)S(1)}, u32[]{:S(2)}, u32[]{:S(2)}) %collective-permute-start.5) | collective-permute-done | bytes 150944 | tf_op jit(solution)/shard_map/ppermute | solution.py:14
  52.0 6.5 %collective-permute-start.6 = (bf16[96,3,262]{2,0,1:T(8,128)(2,1)S(1)}, bf16[96,3,262]{2,0,1:T(8,128)(2,1)S(1)}, u32[]{:S(2)}, u32[]{:S(2)}) collective-permute-start(bf16[96,3,262]{2,0,1:T(8,128)(2,1)S(1)} %collective-permute-done.5), channel_id=1, source_target_pairs={{0,128},{128,0},{16,144},{144,16},{32,160},{160,32},{48,176},{176,... | collective-permute-start | bytes 452744 | tf_op jit(solution)/shard_map/ppermute | solution.py:14
  58.5 0.5 slice_bitcast_fusion.46
  59.0 5.2 %collective-permute-start.8 = (bf16[96,3,262]{2,0,1:T(8,128)(2,1)S(1)}, bf16[96,3,262]{2,0,1:T(8,128)(2,1)S(1)}, u32[]{:S(2)}, u32[]{:S(2)}) collective-permute-start(bf16[96,3,262]{2,0,1:T(8,128)(2,1)S(1)} %get-tuple-element.166), channel_id=1, source_target_pairs={{1,0},{2,1},{3,2},{4,3},{5,4},{6,5},{7,6},{8,7},{9,8},{10,9},{11,1... | collective-permute-start | bytes 452744 | tf_op jit(solution)/shard_map/ppermute | solution.py:25
  64.2 3.5 collective-permute-done.6
  67.7 5.5 %collective-permute-start.7 = (bf16[96,3,262]{2,0,1:T(8,128)(2,1)S(1)}, bf16[96,3,262]{2,0,1:T(8,128)(2,1)S(1)}, u32[]{:S(2)}, u32[]{:S(2)}) collective-permute-start(bf16[96,3,262]{2,0,1:T(8,128)(2,1)S(1)} %collective-permute-done.6), channel_id=1, source_target_pairs={{0,256},{256,0},{16,272},{272,16},{32,288},{288,32},{48,304},{304,... | collective-permute-start | bytes 452744 | tf_op jit(solution)/shard_map/ppermute | solution.py:14
  73.3 8.0 %collective-permute-done.7 = bf16[96,3,262]{2,0,1:T(8,128)(2,1)S(1)} collective-permute-done((bf16[96,3,262]{2,0,1:T(8,128)(2,1)S(1)}, bf16[96,3,262]{2,0,1:T(8,128)(2,1)S(1)}, u32[]{:S(2)}, u32[]{:S(2)}) %collective-permute-start.7) | collective-permute-done | bytes 150944 | tf_op jit(solution)/shard_map/ppermute | solution.py:14
  81.3 0.9 reverse
  82.3 0.5 maximum_maximum_fusion
  83.3 8.7 %fusion.223 = (f32[8,256]{1,0:T(8,128)S(1)}, f32[96,8,256]{2,0,1:T(8,128)S(1)}) fusion(bf16[96,11,262]{2,0,1:T(8,128)(2,1)S(1)} %get-tuple-element.165, f32[96]{0:T(128)} %get-tuple-element.217, f32[96]{0:T(128)} %get-tuple-element.218, f32[96]{0:T(128)S(1)} %get-tuple-element.171, f32[96]{0:T(128)S(1)} %get-tuple-element.172, ...), kind=kLoop, calls=%fused_computation.474 | loop fusion | flops 32438272 | bytes 17730944 | tf_op jit(solution)/shard_map/reduce_sum | solution.py:94
  92.1 0.5 convolution_add_fusion
  92.6 0.4 copy-done.6
  92.9 1.9 convert_reduce_fusion
  94.8 1.0 multiply_reduce_fusion
  95.8 3.5 fusion.206
  99.4 1.1 fusion.138
  100.8 3.3 fusion.156
  104.4 17.7 %fusion.93 = f32[96,14,262]{2,0,1:T(8,128)S(1)} fusion(f32[96,8,256]{2,0,1:T(8,128)S(1)} %get-tuple-element.155, f32[96]{0:T(128)} %get-tuple-element.217, f32[96]{0:T(128)} %get-tuple-element.218, f32[96]{0:T(128)S(1)} %get-tuple-element.171, f32[96]{0:T(128)S(1)} %get-tuple-element.172, f32[96]{0:T(128)S(1)} %get-tuple-element.173, ...), kind=kLoop, calls=%fused_computation.144 | loop fusion | flops 34156416 | bytes 2213760 | tf_op jit(solution)/shard_map/add | solution.py:64
  122.2 0.7 fusion.110
  123.0 1.0 copy.41
  123.9 2.6 fusion.188
  126.6 4.3 stack.199
  130.9 4.4 collective-permute-start.9
  135.4 2.8 convolution_bitcast_fusion.2
  138.2 1.9 collective-permute-start.10
  140.1 1.1 convolution_bitcast_fusion.3
  141.2 107.6 %all-reduce.1 = (f32[96,7,7]{0,2,1:T(8,128)S(1)}, f32[96]{0:T(128)S(1)}, f32[192]{0:T(256)S(1)}) all-reduce(f32[96,7,7]{0,2,1:T(8,128)S(1)} %reshape.198, f32[96]{0:T(128)S(1)} %copy-done.87, f32[192]{0:T(256)S(1)} %copy-done.97), channel_id=1, replica_groups=mesh['lon'=32,'lat'=16] {'lon','lat'}, use_global_device_ids=true, to_apply=%region_53.54 | all-reduce | flops 4992 | bytes 39936 | tf_op jit(solution)/shard_map/psum | solution.py:137
  248.8 2.7 collective-permute-start.11
  251.6 0.6 broadcast_multiply_fusion.2
  252.2 6.3 %collective-permute-done.11 = bf16[96,3,262]{2,0,1:T(8,128)(2,1)S(1)} collective-permute-done((bf16[96,3,262]{2,0,1:T(8,128)(2,1)S(1)}, bf16[96,3,262]{2,0,1:T(8,128)(2,1)S(1)}, u32[]{:S(2)}, u32[]{:S(2)}) %collective-permute-start.11) | collective-permute-done | bytes 150944 | tf_op jit(solution)/shard_map/ppermute | solution.py:14
  258.5 2.4 collective-permute-start.12
  260.9 0.6 broadcast_multiply_fusion.6
  261.5 10.3 %collective-permute-done.12 = bf16[96,3,262]{2,0,1:T(8,128)(2,1)S(1)} collective-permute-done((bf16[96,3,262]{2,0,1:T(8,128)(2,1)S(1)}, bf16[96,3,262]{2,0,1:T(8,128)(2,1)S(1)}, u32[]{:S(2)}, u32[]{:S(2)}) %collective-permute-start.12) | collective-permute-done | bytes 150944 | tf_op jit(solution)/shard_map/ppermute | solution.py:14
  271.8 4.0 collective-permute-start.13
  275.8 0.5 broadcast_multiply_fusion.7
  276.3 12.6 %collective-permute-done.13 = bf16[96,3,262]{2,0,1:T(8,128)(2,1)S(1)} collective-permute-done((bf16[96,3,262]{2,0,1:T(8,128)(2,1)S(1)}, bf16[96,3,262]{2,0,1:T(8,128)(2,1)S(1)}, u32[]{:S(2)}, u32[]{:S(2)}) %collective-permute-start.13) | collective-permute-done | bytes 150944 | tf_op jit(solution)/shard_map/ppermute | solution.py:14
  289.0 0.8 reverse.1
  290.1 0.7 fusion.227
  290.8 2.0 collective-permute-start.14
  292.8 1.3 collective-permute-start.15
  294.1 119.6 %all-reduce.5.cloned.1.call-done = (f32[96,192]{1,0:T(8,128)}, f32[192,96]{1,0:T(8,128)}) async-done(((f32[96,192]{1,0:T(8,128)}, f32[192,96]{1,0:T(8,128)}), (f32[96,192]{1,0:T(8,128)}, f32[192,96]{1,0:T(8,128)})) %all-reduce.5.cloned.1.call-update) | async-done | bytes 147472 | tf_op jit(solution)/shard_map/psum | solution.py:137
  413.7 1.5 broadcast_multiply_fusion.1
  415.4 1.0 fusion.209
  416.4 1.1 fusion.208
  418.2 2.3 collective-permute-start.16
  420.5 0.6 broadcast_multiply_fusion
  421.7 2.0 collective-permute-start.17
  423.9 0.7 copy.38
  424.7 2.0 collective-permute-done.17
  426.8 0.7 copy.40
  427.5 6.0 %scatter-add.21 = f32[96,8,256]{2,0,1:T(8,128)S(1)} dynamic-update-slice(f32[96,8,256]{2,0,1:T(8,128)S(1)} %slice.989, f32[96,8,3]{2,0,1:T(8,128)S(1)} %slice_add_fusion.3, s32[]{:T(128)} %constant.159.clone.1, s32[]{:T(128)} %constant.159.clone.1, s32[]{:T(128)} %constant.159.clone.1) | dynamic-update-slice | bytes 18436 | tf_op jit(solution)/shard_map/scatter-add | solution.py:155
  433.7 5.3 %scatter-add.24 = f32[96,8,256]{2,0,1:T(8,128)S(1)} dynamic-update-slice(f32[96,8,256]{2,0,1:T(8,128)S(1)} %scatter-add.21, f32[96,8,3]{2,0,1:T(8,128)S(1)} %slice_add_fusion.2, s32[]{:T(128)} %constant.159.clone.1, s32[]{:T(128)} %constant.159.clone.1, s32[]{:T(128)} %constant.173.clone.1) | dynamic-update-slice | bytes 18436 | tf_op jit(solution)/shard_map/scatter-add | solution.py:156
  439.2 1.0 copy.42
  (238 shorter events, 3.7 us)
Async XLA Ops:
  7.2 84.9 %copy-start = (bf16[96,192]{1,0:T(8,128)(2,1)S(1)}, bf16[96,192]{1,0:T(8,128)(2,1)}, u32[]{:S(2)}) copy-start(bf16[96,192]{1,0:T(8,128)(2,1)} %param.22) | copy-start | bytes 110596
  7.2 29.1 %copy-start.9 = (f32[96,7,7]{0,2,1:T(8,128)S(1)}, f32[96,7,7]{0,2,1:T(8,128)}, u32[]{:S(2)}) copy-start(f32[96,7,7]{0,2,1:T(8,128)} %param.20) | copy-start | bytes 56452
  7.2 406.5 %all-reduce.5.cloned.1.call-start = ((), (), s32[]{:S(2)}) async-start(), calls=%async_computation | async-start | bytes 393216 | tf_op jit(solution)/shard_map/psum | solution.py:137
  9.1 10.7 %collective-permute-start = (bf16[96,8,3]{2,0,1:T(8,128)(2,1)S(1)}, bf16[96,8,3]{2,0,1:T(8,128)(2,1)S(1)}, u32[]{:S(2)}, u32[]{:S(2)}) collective-permute-start(bf16[96,8,3]{2,0,1:T(8,128)(2,1)S(1)} %get-tuple-element.168), channel_id=1, source_target_pairs={{0,16},{16,32},{32,48},{48,64},{64,80},{80,96},{96,112},{112,128},... | collective-permute-start | bytes 13832 | tf_op jit(solution)/shard_map/ppermute | solution.py:24
  13.7 7.3 %collective-permute-start.1 = (bf16[96,8,3]{2,0,1:T(8,128)(2,1)S(1)}, bf16[96,8,3]{2,0,1:T(8,128)(2,1)S(1)}, u32[]{:S(2)}, u32[]{:S(2)}) collective-permute-start(bf16[96,8,3]{2,0,1:T(8,128)(2,1)S(1)} %get-tuple-element.169), channel_id=1, source_target_pairs={{16,0},{32,16},{48,32},{64,48},{80,64},{96,80},{112,96},{128,112},... | collective-permute-start | bytes 13832 | tf_op jit(solution)/shard_map/ppermute | solution.py:25
  20.9 61.9 %copy-start.1 = (bf16[96,8,3]{2,0,1:T(8,128)(2,1)}, bf16[96,8,3]{2,0,1:T(8,128)(2,1)S(1)}, u32[]{:S(2)}) copy-start(bf16[96,8,3]{2,0,1:T(8,128)(2,1)S(1)} %collective-permute-done.1) | copy-start | bytes 13828
  21.2 13.2 %collective-permute-start.3 = (bf16[96,3,262]{2,0,1:T(8,128)(2,1)S(1)}, bf16[96,3,262]{2,0,1:T(8,128)(2,1)S(1)}, u32[]{:S(2)}, u32[]{:S(2)}) collective-permute-start(bf16[96,3,262]{2,0,1:T(8,128)(2,1)S(1)} %get-tuple-element.167), channel_id=1, source_target_pairs={{0,16},{16,0},{32,48},{48,32},{64,80},{80,64},{96,112},{112,96},{1... | collective-permute-start | bytes 452744 | tf_op jit(solution)/shard_map/ppermute | solution.py:14
  34.4 8.5 %collective-permute-start.4 = (bf16[96,3,262]{2,0,1:T(8,128)(2,1)S(1)}, bf16[96,3,262]{2,0,1:T(8,128)(2,1)S(1)}, u32[]{:S(2)}, u32[]{:S(2)}) collective-permute-start(bf16[96,3,262]{2,0,1:T(8,128)(2,1)S(1)} %collective-permute-done.3), channel_id=1, source_target_pairs={{0,32},{32,0},{16,48},{48,16},{64,96},{96,64},{80,112},{112,80},{1... | collective-permute-start | bytes 452744 | tf_op jit(solution)/shard_map/ppermute | solution.py:14
  36.3 46.5 %copy-start.11 = (f32[96]{0:T(128)}, f32[96]{0:T(128)S(1)}, u32[]{:S(2)}) copy-start(f32[96]{0:T(128)S(1)} %get-tuple-element.176) | copy-start | bytes 1156
  36.3 46.5 %copy-start.13 = (f32[96]{0:T(128)}, f32[96]{0:T(128)S(1)}, u32[]{:S(2)}) copy-start(f32[96]{0:T(128)S(1)} %get-tuple-element.177) | copy-start | bytes 1156
  36.3 46.5 %copy-start.15 = (f32[96]{0:T(128)}, f32[96]{0:T(128)S(1)}, u32[]{:S(2)}) copy-start(f32[96]{0:T(128)S(1)} %get-tuple-element.178) | copy-start | bytes 1156
  36.3 46.5 %copy-start.17 = (f32[96]{0:T(128)}, f32[96]{0:T(128)S(1)}, u32[]{:S(2)}) copy-start(f32[96]{0:T(128)S(1)} %get-tuple-element.179) | copy-start | bytes 1156
  36.3 46.5 %copy-start.19 = (f32[96]{0:T(128)}, f32[96]{0:T(128)S(1)}, u32[]{:S(2)}) copy-start(f32[96]{0:T(128)S(1)} %get-tuple-element.180) | copy-start | bytes 1156
  36.4 46.5 %copy-start.21 = (f32[96]{0:T(128)}, f32[96]{0:T(128)S(1)}, u32[]{:S(2)}) copy-start(f32[96]{0:T(128)S(1)} %get-tuple-element.181) | copy-start | bytes 1156
  36.4 46.5 %copy-start.23 = (f32[96]{0:T(128)}, f32[96]{0:T(128)S(1)}, u32[]{:S(2)}) copy-start(f32[96]{0:T(128)S(1)} %get-tuple-element.182) | copy-start | bytes 1156
  36.4 46.5 %copy-start.25 = (f32[96]{0:T(128)}, f32[96]{0:T(128)S(1)}, u32[]{:S(2)}) copy-start(f32[96]{0:T(128)S(1)} %get-tuple-element.183) | copy-start | bytes 1156
  36.4 46.5 %copy-start.27 = (f32[96]{0:T(128)}, f32[96]{0:T(128)S(1)}, u32[]{:S(2)}) copy-start(f32[96]{0:T(128)S(1)} %get-tuple-element.184) | copy-start | bytes 1156
  36.4 46.5 %copy-start.29 = (f32[96]{0:T(128)}, f32[96]{0:T(128)S(1)}, u32[]{:S(2)}) copy-start(f32[96]{0:T(128)S(1)} %get-tuple-element.185) | copy-start | bytes 1156
  36.4 46.5 %copy-start.31 = (f32[96]{0:T(128)}, f32[96]{0:T(128)S(1)}, u32[]{:S(2)}) copy-start(f32[96]{0:T(128)S(1)} %get-tuple-element.186) | copy-start | bytes 1156
  36.4 46.5 %copy-start.33 = (f32[96]{0:T(128)}, f32[96]{0:T(128)S(1)}, u32[]{:S(2)}) copy-start(f32[96]{0:T(128)S(1)} %get-tuple-element.187) | copy-start | bytes 1156
  36.4 46.5 %copy-start.35 = (f32[96]{0:T(128)}, f32[96]{0:T(128)S(1)}, u32[]{:S(2)}) copy-start(f32[96]{0:T(128)S(1)} %get-tuple-element.188) | copy-start | bytes 1156
  42.9 9.1 %collective-permute-start.5 = (bf16[96,3,262]{2,0,1:T(8,128)(2,1)S(1)}, bf16[96,3,262]{2,0,1:T(8,128)(2,1)S(1)}, u32[]{:S(2)}, u32[]{:S(2)}) collective-permute-start(bf16[96,3,262]{2,0,1:T(8,128)(2,1)S(1)} %collective-permute-done.4), channel_id=1, source_target_pairs={{0,64},{64,0},{16,80},{80,16},{32,96},{96,32},{48,112},{112,48},{1... | collective-permute-start | bytes 452744 | tf_op jit(solution)/shard_map/ppermute | solution.py:14
  45.3 37.7 %copy-start.37 = (f32[96]{0:T(128)}, f32[96]{0:T(128)S(1)}, u32[]{:S(2)}) copy-start(f32[96]{0:T(128)S(1)} %get-tuple-element.189) | copy-start | bytes 1156
  45.3 37.7 %copy-start.39 = (f32[96]{0:T(128)}, f32[96]{0:T(128)S(1)}, u32[]{:S(2)}) copy-start(f32[96]{0:T(128)S(1)} %get-tuple-element.190) | copy-start | bytes 1156
  45.3 37.7 %copy-start.41 = (f32[96]{0:T(128)}, f32[96]{0:T(128)S(1)}, u32[]{:S(2)}) copy-start(f32[96]{0:T(128)S(1)} %get-tuple-element.191) | copy-start | bytes 1156
  45.3 37.7 %copy-start.43 = (f32[96]{0:T(128)}, f32[96]{0:T(128)S(1)}, u32[]{:S(2)}) copy-start(f32[96]{0:T(128)S(1)} %get-tuple-element.192) | copy-start | bytes 1156
  45.3 37.7 %copy-start.45 = (f32[96]{0:T(128)}, f32[96]{0:T(128)S(1)}, u32[]{:S(2)}) copy-start(f32[96]{0:T(128)S(1)} %get-tuple-element.193) | copy-start | bytes 1156
  45.3 37.7 %copy-start.47 = (f32[96]{0:T(128)}, f32[96]{0:T(128)S(1)}, u32[]{:S(2)}) copy-start(f32[96]{0:T(128)S(1)} %get-tuple-element.194) | copy-start | bytes 1156
  45.3 37.7 %copy-start.49 = (f32[96]{0:T(128)}, f32[96]{0:T(128)S(1)}, u32[]{:S(2)}) copy-start(f32[96]{0:T(128)S(1)} %get-tuple-element.195) | copy-start | bytes 1156
  45.3 37.7 %copy-start.51 = (f32[96]{0:T(128)}, f32[96]{0:T(128)S(1)}, u32[]{:S(2)}) copy-start(f32[96]{0:T(128)S(1)} %get-tuple-element.196) | copy-start | bytes 1156
  45.3 37.7 %copy-start.53 = (f32[96]{0:T(128)}, f32[96]{0:T(128)S(1)}, u32[]{:S(2)}) copy-start(f32[96]{0:T(128)S(1)} %get-tuple-element.197) | copy-start | bytes 1156
  45.3 37.7 %copy-start.55 = (f32[96]{0:T(128)}, f32[96]{0:T(128)S(1)}, u32[]{:S(2)}) copy-start(f32[96]{0:T(128)S(1)} %get-tuple-element.198) | copy-start | bytes 1156
  45.4 37.7 %copy-start.57 = (f32[96]{0:T(128)}, f32[96]{0:T(128)S(1)}, u32[]{:S(2)}) copy-start(f32[96]{0:T(128)S(1)} %get-tuple-element.199) | copy-start | bytes 1156
  45.4 37.7 %copy-start.59 = (f32[96]{0:T(128)}, f32[96]{0:T(128)S(1)}, u32[]{:S(2)}) copy-start(f32[96]{0:T(128)S(1)} %get-tuple-element.200) | copy-start | bytes 1156
  45.4 37.7 %copy-start.61 = (f32[96]{0:T(128)}, f32[96]{0:T(128)S(1)}, u32[]{:S(2)}) copy-start(f32[96]{0:T(128)S(1)} %get-tuple-element.201) | copy-start | bytes 1156
  45.4 37.7 %copy-start.63 = (f32[96]{0:T(128)}, f32[96]{0:T(128)S(1)}, u32[]{:S(2)}) copy-start(f32[96]{0:T(128)S(1)} %get-tuple-element.202) | copy-start | bytes 1156
  45.4 37.7 %copy-start.65 = (f32[96]{0:T(128)}, f32[96]{0:T(128)S(1)}, u32[]{:S(2)}) copy-start(f32[96]{0:T(128)S(1)} %get-tuple-element.203) | copy-start | bytes 1156
  45.4 37.7 %copy-start.67 = (f32[96]{0:T(128)}, f32[96]{0:T(128)S(1)}, u32[]{:S(2)}) copy-start(f32[96]{0:T(128)S(1)} %get-tuple-element.204) | copy-start | bytes 1156
  45.4 37.7 %copy-start.69 = (f32[96]{0:T(128)}, f32[96]{0:T(128)S(1)}, u32[]{:S(2)}) copy-start(f32[96]{0:T(128)S(1)} %get-tuple-element.205) | copy-start | bytes 1156
  45.4 37.7 %copy-start.71 = (f32[96]{0:T(128)}, f32[96]{0:T(128)S(1)}, u32[]{:S(2)}) copy-start(f32[96]{0:T(128)S(1)} %get-tuple-element.206) | copy-start | bytes 1156
  45.4 37.7 %copy-start.73 = (f32[96]{0:T(128)}, f32[96]{0:T(128)S(1)}, u32[]{:S(2)}) copy-start(f32[96]{0:T(128)S(1)} %get-tuple-element.207) | copy-start | bytes 1156
  45.4 27.8 %collective-permute-start.2 = (bf16[96,3,262]{2,0,1:T(8,128)(2,1)S(1)}, bf16[96,3,262]{2,0,1:T(8,128)(2,1)S(1)}, u32[]{:S(2)}, u32[]{:S(2)}) collective-permute-start(bf16[96,3,262]{2,0,1:T(8,128)(2,1)S(1)} %get-tuple-element.167), channel_id=1, source_target_pairs={{0,1},{1,2},{2,3},{3,4},{4,5},{5,6},{6,7},{7,8},{8,9},{9,10},{10,1... | collective-permute-start | bytes 452744 | tf_op jit(solution)/shard_map/ppermute | solution.py:24
  52.0 15.7 %collective-permute-start.6 = (bf16[96,3,262]{2,0,1:T(8,128)(2,1)S(1)}, bf16[96,3,262]{2,0,1:T(8,128)(2,1)S(1)}, u32[]{:S(2)}, u32[]{:S(2)}) collective-permute-start(bf16[96,3,262]{2,0,1:T(8,128)(2,1)S(1)} %collective-permute-done.5), channel_id=1, source_target_pairs={{0,128},{128,0},{16,144},{144,16},{32,160},{160,32},{48,176},{176,... | collective-permute-start | bytes 452744 | tf_op jit(solution)/shard_map/ppermute | solution.py:14
  59.0 24.2 %copy-start.75 = (f32[96]{0:T(128)}, f32[96]{0:T(128)S(1)}, u32[]{:S(2)}) copy-start(f32[96]{0:T(128)S(1)} %get-tuple-element.208) | copy-start | bytes 1156
  59.0 24.2 %copy-start.77 = (f32[96]{0:T(128)}, f32[96]{0:T(128)S(1)}, u32[]{:S(2)}) copy-start(f32[96]{0:T(128)S(1)} %get-tuple-element.209) | copy-start | bytes 1156
  59.0 24.2 %copy-start.79 = (f32[96]{0:T(128)}, f32[96]{0:T(128)S(1)}, u32[]{:S(2)}) copy-start(f32[96]{0:T(128)S(1)} %get-tuple-element.210) | copy-start | bytes 1156
  59.0 24.2 %copy-start.81 = (f32[96]{0:T(128)}, f32[96]{0:T(128)S(1)}, u32[]{:S(2)}) copy-start(f32[96]{0:T(128)S(1)} %get-tuple-element.211) | copy-start | bytes 1156
  59.0 24.2 %copy-start.83 = (f32[96]{0:T(128)}, f32[96]{0:T(128)S(1)}, u32[]{:S(2)}) copy-start(f32[96]{0:T(128)S(1)} %get-tuple-element.212) | copy-start | bytes 1156
  59.0 24.2 %copy-start.85 = (f32[96]{0:T(128)}, f32[96]{0:T(128)S(1)}, u32[]{:S(2)}) copy-start(f32[96]{0:T(128)S(1)} %get-tuple-element.213) | copy-start | bytes 1156
  59.0 23.1 %collective-permute-start.8 = (bf16[96,3,262]{2,0,1:T(8,128)(2,1)S(1)}, bf16[96,3,262]{2,0,1:T(8,128)(2,1)S(1)}, u32[]{:S(2)}, u32[]{:S(2)}) collective-permute-start(bf16[96,3,262]{2,0,1:T(8,128)(2,1)S(1)} %get-tuple-element.166), channel_id=1, source_target_pairs={{1,0},{2,1},{3,2},{4,3},{5,4},{6,5},{7,6},{8,7},{9,8},{10,9},{11,1... | collective-permute-start | bytes 452744 | tf_op jit(solution)/shard_map/ppermute | solution.py:25
  67.7 13.5 %collective-permute-start.7 = (bf16[96,3,262]{2,0,1:T(8,128)(2,1)S(1)}, bf16[96,3,262]{2,0,1:T(8,128)(2,1)S(1)}, u32[]{:S(2)}, u32[]{:S(2)}) collective-permute-start(bf16[96,3,262]{2,0,1:T(8,128)(2,1)S(1)} %collective-permute-done.6), channel_id=1, source_target_pairs={{0,256},{256,0},{16,272},{272,16},{32,288},{288,32},{48,304},{304,... | collective-permute-start | bytes 452744 | tf_op jit(solution)/shard_map/ppermute | solution.py:14
  92.9 29.2 %copy-start.5 = (f32[8,256,192]{1,2,0:T(8,128)}, f32[8,256,192]{1,2,0:T(8,128)S(1)}, u32[]{:S(2)}) copy-start(f32[8,256,192]{1,2,0:T(8,128)S(1)} %convolution_add_fusion) | copy-start | bytes 4718596
  130.9 10.3 %copy-start.87 = (f32[96]{0:T(128)S(1)}, f32[96]{0:T(128)}, u32[]{:S(2)}) copy-start(f32[96]{0:T(128)} %get-tuple-element.130) | copy-start | bytes 1156
  130.9 10.3 %copy-start.97 = (f32[192]{0:T(256)S(1)}, f32[192]{0:T(256)}, u32[]{:S(2)}) copy-start(f32[192]{0:T(256)} %get-tuple-element.222) | copy-start | bytes 2308
  130.9 7.3 %collective-permute-start.9 = (bf16[96,3,262]{2,0,1:T(8,128)(2,1)S(1)}, bf16[96,3,262]{2,0,1:T(8,128)(2,1)}, u32[]{:S(2)}, u32[]{:S(2)}) collective-permute-start(bf16[96,3,262]{2,0,1:T(8,128)(2,1)S(1)} %slice.1622), channel_id=1, source_target_pairs={{0,16},{16,0},{32,48},{48,32},{64,80},{80,64},{96,112},{112,96},{1... | collective-permute-start | bytes 452744 | tf_op jit(solution)/shard_map/ppermute | solution.py:14
  138.2 110.7 %collective-permute-start.10 = (bf16[96,3,262]{2,0,1:T(8,128)(2,1)}, bf16[96,3,262]{2,0,1:T(8,128)(2,1)S(1)}, u32[]{:S(2)}, u32[]{:S(2)}) collective-permute-start(bf16[96,3,262]{2,0,1:T(8,128)(2,1)} %collective-permute-done.9), channel_id=1, source_target_pairs={{0,32},{32,0},{16,48},{48,16},{64,96},{96,64},{80,112},{112,80},{1... | collective-permute-start | bytes 452744 | tf_op jit(solution)/shard_map/ppermute | solution.py:14
  248.8 9.7 %collective-permute-start.11 = (bf16[96,3,262]{2,0,1:T(8,128)(2,1)S(1)}, bf16[96,3,262]{2,0,1:T(8,128)(2,1)S(1)}, u32[]{:S(2)}, u32[]{:S(2)}) collective-permute-start(bf16[96,3,262]{2,0,1:T(8,128)(2,1)S(1)} %collective-permute-done.10), channel_id=1, source_target_pairs={{0,64},{64,0},{16,80},{80,16},{32,96},{96,32},{48,112},{112,48},{1... | collective-permute-start | bytes 452744 | tf_op jit(solution)/shard_map/ppermute | solution.py:14
  258.5 13.3 %collective-permute-start.12 = (bf16[96,3,262]{2,0,1:T(8,128)(2,1)S(1)}, bf16[96,3,262]{2,0,1:T(8,128)(2,1)S(1)}, u32[]{:S(2)}, u32[]{:S(2)}) collective-permute-start(bf16[96,3,262]{2,0,1:T(8,128)(2,1)S(1)} %collective-permute-done.11), channel_id=1, source_target_pairs={{0,128},{128,0},{16,144},{144,16},{32,160},{160,32},{48,176},{176,... | collective-permute-start | bytes 452744 | tf_op jit(solution)/shard_map/ppermute | solution.py:14
  271.8 17.2 %collective-permute-start.13 = (bf16[96,3,262]{2,0,1:T(8,128)(2,1)S(1)}, bf16[96,3,262]{2,0,1:T(8,128)(2,1)S(1)}, u32[]{:S(2)}, u32[]{:S(2)}) collective-permute-start(bf16[96,3,262]{2,0,1:T(8,128)(2,1)S(1)} %collective-permute-done.12), channel_id=1, source_target_pairs={{0,256},{256,0},{16,272},{272,16},{32,288},{288,32},{48,304},{304,... | collective-permute-start | bytes 452744 | tf_op jit(solution)/shard_map/ppermute | solution.py:14
  290.8 124.5 %collective-permute-start.14 = (bf16[96,3,262]{2,0,1:T(8,128)(2,1)S(1)}, bf16[96,3,262]{2,0,1:T(8,128)(2,1)}, u32[]{:S(2)}, u32[]{:S(2)}) collective-permute-start(bf16[96,3,262]{2,0,1:T(8,128)(2,1)S(1)} %get-tuple-element.162), channel_id=1, source_target_pairs={{0,1},{1,2},{2,3},{3,4},{4,5},{5,6},{6,7},{7,8},{8,9},{9,10},{10,1... | collective-permute-start | bytes 452744 | tf_op jit(solution)/shard_map/ppermute | solution.py:24
  292.8 122.5 %collective-permute-start.15 = (bf16[96,3,262]{2,0,1:T(8,128)(2,1)}, bf16[96,3,262]{2,0,1:T(8,128)(2,1)}, u32[]{:S(2)}, u32[]{:S(2)}) collective-permute-start(bf16[96,3,262]{2,0,1:T(8,128)(2,1)} %get-tuple-element.163), channel_id=1, source_target_pairs={{1,0},{2,1},{3,2},{4,3},{5,4},{6,5},{7,6},{8,7},{9,8},{10,9},{11,1... | collective-permute-start | bytes 452744 | tf_op jit(solution)/shard_map/ppermute | solution.py:25
  418.2 5.5 %collective-permute-start.16 = (f32[3,768]{1,0:T(4,128)S(1)}, f32[3,768]{1,0:T(4,128)S(1)}, u32[]{:S(2)}, u32[]{:S(2)}) collective-permute-start(f32[3,768]{1,0:T(4,128)S(1)} %slice.926), channel_id=1, source_target_pairs={{0,16},{16,32},{32,48},{48,64},{64,80},{80,96},{96,112},{112,128},... | collective-permute-start | bytes 27656 | tf_op jit(solution)/shard_map/ppermute | solution.py:24
  421.7 5.0 %collective-permute-start.17 = (f32[3,768]{1,0:T(4,128)S(1)}, f32[3,768]{1,0:T(4,128)S(1)}, u32[]{:S(2)}, u32[]{:S(2)}) collective-permute-start(f32[3,768]{1,0:T(4,128)S(1)} %slice.929), channel_id=1, source_target_pairs={{16,0},{32,16},{48,32},{64,48},{80,64},{96,80},{112,96},{128,112},... | collective-permute-start | bytes 27656 | tf_op jit(solution)/shard_map/ppermute | solution.py:25
  424.7 14.3 %copy-start.7 = (bf16[96,8,256]{2,1,0:T(8,128)(2,1)S(1)}, bf16[96,8,256]{2,1,0:T(8,128)(2,1)}, u32[]{:S(2)}) copy-start(bf16[96,8,256]{2,1,0:T(8,128)(2,1)} %param.25) | copy-start | bytes 1179652
  (54 other events, 202.3 us)
Sparse Core Ops, SparseCore 0:
  141.3 272.3 all-reduce.4
where the time goes:
time: 451 us; the launch traced here: 447 us
  waiting for transfers between devices  176 us (39%)
  blocking collectives  108 us (24%)
  starting transfers between devices  69.2 us (15%)
  other arithmetic  46.5 us (10%)
  local copies, waits for them, and re-layouts  24.3 us (5%)
  between operations  15.9 us (4%)
  matrix products  7.91 us (2%)
    psum x1, waiting for transfers between devices, shards(): lax.psum((kernel_part, gain_part, w_in_part, b_part, w_out_part), ('lon',...  120 us
    psum x1, blocking collectives, shards(): lax.psum((kernel_part, gain_part, w_in_part, b_part, w_out_part), ('lon',...  108 us
    ppermute x10, waiting for transfers between devices, from_partner(): return lax.ppermute(block, axis, route)  52.9 us
    ppermute x10, starting transfers between devices, from_partner(): return lax.ppermute(block, axis, route)  43.8 us
    add x1, other arithmetic, spread_back(): summed = summed + kernel[:, row_off, col_off][:, None, None] * window  17.7 us
    ppermute x4, starting transfers between devices, extended(): after = lax.ppermute(first, axis, down)  14.7 us
    ppermute x4, starting transfers between devices, extended(): before = lax.ppermute(last, axis, up)  10.7 us
    reduce_sum x4, other arithmetic, kernel_terms(): terms.append(jnp.sum(conv_grad * window, axis=(1, 2)))  10.5 us
  transfers between devices with their start and end apart: 19, of which 11 were waited for; matrix products, arithmetic and copies ran while one was open for 3% of the time, Pallas kernels for 0%

commit v1 on v0

v1 whole, which is shorter than its diff:
```python
import functools

import jax
import jax.numpy as jnp
from jax import lax
from jax.experimental import pallas as pl
from jax.experimental.pallas import tpu as pltpu
from jax.sharding import PartitionSpec as P

F32 = jnp.float32
BF16 = jnp.bfloat16
VMEM_LIMIT = 56 * 1024 * 1024
RING = 3


def call(body, outs, *args, scratch=()):
    return pl.pallas_call(
        body,
        out_shape=outs,
        in_specs=[pl.BlockSpec(memory_space=pltpu.VMEM)] * len(args),
        out_specs=[pl.BlockSpec(memory_space=pltpu.VMEM)] * len(outs),
        scratch_shapes=list(scratch),
        compiler_params=pltpu.CompilerParams(vmem_limit_bytes=VMEM_LIMIT),
    )(*args)


def lanes():
    return lax.broadcasted_iota(jnp.int32, (8, 128), 1)


def spread(flat, values):
    channels, rows, cols = values.shape
    for t in range(cols // 128):
        part = values[:, :, t * 128 : t * 128 + 128]
        flat[t] = part.reshape(channels * rows, 128)


def gather(flat, channels, rows):
    parts = [flat[t].reshape(channels, rows, 128) for t in range(flat.shape[0])]
    return jnp.concatenate(parts, axis=2)


def row_of(flat, i, channels, rows):
    parts = [flat[t, pl.ds(i, channels, stride=rows), :] for t in range(flat.shape[0])]
    return jnp.concatenate(parts, axis=1)


def rows_body(f_ref, mask_ref, m_ref, first_ref, last_ref, flat):
    channels, rows, cols = f_ref.shape
    sea = mask_ref[...].astype(F32)
    spread(flat, f_ref[...].astype(F32) * sea[None])
    for i in range(rows):
        row = row_of(flat, i, channels, rows).astype(BF16)
        m_ref[i] = row
        if i < RING:
            first_ref[i] = row
        if i >= rows - RING:
            last_ref[i - (rows - RING)] = row


def strips_body(m_ref, south_ref, north_ref, mirror_ref, flip_ref, halo_ref, left_ref, right_ref):
    rows, channels, cols = m_ref.shape
    for k in range(RING):
        turned = jnp.dot(mirror_ref[RING - 1 - k], flip_ref[...], preferred_element_type=F32)
        halo_ref[k] = (north_ref[k].astype(F32) + turned).astype(BF16)
    lane = lax.broadcasted_iota(jnp.int32, (channels, 128), 1)
    left = jnp.zeros((channels, 128), F32)
    right = jnp.zeros((channels, 128), F32)
    for r in range(rows + 2 * RING):
        if r < RING:
            ref, at = south_ref, r
        elif r < rows + RING:
            ref, at = m_ref, r - RING
        else:
            ref, at = halo_ref, r - RING - rows
        here = (lane >= RING * r) & (lane < RING * r + RING)
        head = ref[at, :, 0:128].astype(F32)
        tail = ref[at, :, cols - 128 : cols].astype(F32)
        if r:
            head = pltpu.roll(head, RING * r, 1)
        tail = pltpu.roll(tail, RING * r + RING, 1)
        left = jnp.where(here, head, left)
        right = jnp.where(here, tail, right)
    left_ref[...] = left.astype(BF16)
    right_ref[...] = right.astype(BF16)


def fill(ext, m_ref, south_ref, halo_ref, before_ref, after_ref):
    rows, channels, cols = m_ref.shape
    lane = lax.broadcasted_iota(jnp.int32, (channels, 128), 1)
    before = before_ref[...].astype(F32)
    after = after_ref[...].astype(F32)
    for r in range(rows + 2 * RING):
        if r < RING:
            row = south_ref[r]
        elif r < rows + RING:
            row = m_ref[r - RING]
        else:
            row = halo_ref[r - RING - rows]
        ext[r, :, 0:cols] = row.astype(F32)
        right = after if r == 0 else pltpu.roll(after, 128 - RING * r, 1)
        left = pltpu.roll(before, 128 - RING - RING * r, 1)
        ext[r, :, cols : cols + 128] = jnp.where(
            lane < RING, right, jnp.where(lane >= 128 - RING, left, 0.0)
        )


def windows(tiles, step, lane):
    if step == 0:
        return tiles[:-1]
    count = len(tiles)
    if step > 0:
        turned = [pltpu.roll(t, 128 - step, 1) for t in tiles]
        keep = lane < 128 - step
        return [jnp.where(keep, turned[t], turned[t + 1]) for t in range(count - 1)]
    turned = [pltpu.roll(t, -step, 1) for t in tiles]
    keep = lane >= -step
    return [jnp.where(keep, turned[t], turned[t - 1]) for t in range(count - 1)]


def tap(weights, index):
    return jnp.broadcast_to(weights[:, index : index + 1], (8, 128))


def correlate(ext, c0, rows, pairs, lane, weights, north):
    summed = [[None] * pairs for _ in range(rows)]
    for b in range(7):
        taps = [tap(weights, a * 7 + b) for a in range(7)]
        far = taps if north is None else [tap(north, a * 7 + b) for a in range(7)]
        for r in range(rows + 2 * RING):
            tiles = [ext[r, pl.ds(c0, 8), t * 128 : t * 128 + 128] for t in range(pairs + 1)]
            wins = windows(tiles, b - RING, lane)
            for a in range(7):
                i = r - a
                if 0 <= i < rows:
                    weight = far[a] if r >= rows + RING else taps[a]
                    for t in range(pairs):
                        term = weight * wins[t]
                        old = summed[i][t]
                        summed[i][t] = term if old is None else old + term
    return summed


def block_body(
    m_ref, south_ref, halo_ref, before_ref, after_ref, ct_ref, mask_ref,
    dw_ref, gain_ref, w_in_ref, w_in_t_ref, b_ref, w_out_ref, w_out_t_ref,
    out_ref, g_ref, first_ref, last_ref, sums_ref,
    ext, conv, flat, act, back, sca, pre, b_acc, gain_acc,
):
    rows, channels, cols = m_ref.shape
    hidden = w_out_ref.shape[0]
    pairs = cols // 128
    fill(ext, m_ref, south_ref, halo_ref, before_ref, after_ref)
    sea = mask_ref[...].astype(F32)
    spread(flat, ct_ref[...].astype(F32) * sea[None])
    for i in range(rows):
        back[:, i * cols : i * cols + cols] = row_of(flat, i, channels, rows).astype(BF16)

    def conv_step(ct, carry):
        c0 = pl.multiple_of(ct * 8, 8)
        lane = lanes()
        summed = correlate(ext, c0, rows, pairs, lane, dw_ref[pl.ds(c0, 8), :], None)
        for i in range(rows):
            for t in range(pairs):
                conv[i, pl.ds(c0, 8), t * 128 : t * 128 + 128] = summed[i][t]
        return carry

    lax.fori_loop(0, channels // 8, conv_step, 0)

    b_acc[...] = jnp.zeros_like(b_acc)
    gain_acc[...] = jnp.zeros_like(gain_acc)
    gain = jnp.broadcast_to(gain_ref[...], (channels, cols))
    bias = jnp.broadcast_to(b_ref[...], (hidden, cols))
    root = 0.7978845608028654
    for i in range(rows):
        span = slice(i * cols, i * cols + cols)
        raw = conv[i]
        centred = raw - jnp.mean(raw, axis=0, keepdims=True)
        inv_std = lax.rsqrt(jnp.mean(centred * centred, axis=0, keepdims=True) + 1e-06)
        normed = centred * inv_std
        scaled = (normed * gain).astype(BF16)
        sca[:, span] = scaled
        v = jnp.dot(w_in_t_ref[...], scaled, preferred_element_type=F32) + bias
        v2 = v * v
        t = jnp.tanh(root * v * (1.0 + 0.044715 * v2))
        half = 0.5 * (1.0 + t)
        activated = (v * half).astype(BF16)
        act[:, span] = activated
        slope = half + 0.5 * v * (1.0 - t * t) * (root * (1.0 + 3 * 0.044715 * v2))
        mixed = jnp.dot(w_out_t_ref[...], activated, preferred_element_type=F32)
        mixed = m_ref[i].astype(F32) + mixed
        for t in range(pairs):
            flat[t, pl.ds(i, channels, stride=rows), :] = mixed[:, t * 128 : t * 128 + 128]
        act_grad = jnp.dot(w_out_ref[...], back[:, span], preferred_element_type=F32)
        pre_grad = (act_grad * slope).astype(BF16)
        pre[:, span] = pre_grad
        wide = pre_grad.astype(F32)
        b_acc[...] += sum(wide[:, t * 128 : t * 128 + 128] for t in range(pairs))
        scaled_grad = jnp.dot(w_in_ref[...], pre_grad, preferred_element_type=F32)
        gains = scaled_grad * normed
        gain_acc[...] += sum(gains[:, t * 128 : t * 128 + 128] for t in range(pairs))
        norm_grad = scaled_grad * gain
        grad = inv_std * (
            norm_grad
            - jnp.mean(norm_grad, axis=0, keepdims=True)
            - normed * jnp.mean(norm_grad * normed, axis=0, keepdims=True)
        )
        conv[i] = grad
        short = grad.astype(BF16)
        g_ref[i] = short
        if i < RING:
            first_ref[i] = short
        if i >= rows - RING:
            last_ref[i - (rows - RING)] = short

    out_ref[...] = (gather(flat, channels, rows) * sea[None]).astype(BF16)
    over_cells = (((1,), (1,)), ((), ()))
    w_in_sum = lax.dot_general(sca[...], pre[...], over_cells, preferred_element_type=F32)
    w_out_sum = lax.dot_general(act[...], back[...], over_cells, preferred_element_type=F32)
    sums_ref[0:channels, :] = w_in_sum[:, 0:128]
    sums_ref[channels : channels + hidden, :] = jnp.zeros((hidden, 128), F32)
    sums_ref[channels : channels + hidden, 0:channels] = w_out_sum
    low = channels + hidden
    sums_ref[low : low + channels, :] = jnp.zeros((channels, 128), F32)
    sums_ref[low : low + channels, 0 : hidden - 128] = w_in_sum[:, 128:hidden]
    shift = hidden - 128

    def kernel_step(ct, carry):
        c0 = pl.multiple_of(ct * 8, 8)
        lane = lanes()
        at = pl.multiple_of(low + c0, 8)
        tile = sums_ref[pl.ds(at, 8), :]
        grads = [
            [conv[i, pl.ds(c0, 8), t * 128 : t * 128 + 128] for t in range(pairs)]
            for i in range(rows)
        ]
        for b in range(7):
            summed = [None] * 7
            for r in range(rows + 2 * RING):
                tiles = [ext[r, pl.ds(c0, 8), t * 128 : t * 128 + 128] for t in range(pairs + 1)]
                wins = windows(tiles, b - RING, lane)
                for a in range(7):
                    i = r - a
                    if 0 <= i < rows:
                        for t in range(pairs):
                            term = grads[i][t] * wins[t]
                            summed[a] = term if summed[a] is None else summed[a] + term
            for a in range(7):
                total = jnp.sum(summed[a], axis=1, keepdims=True)
                tile = jnp.where(lane == shift + a * 7 + b, total, tile)
        total = jnp.sum(gain_acc[pl.ds(c0, 8), :], axis=1, keepdims=True)
        tile = jnp.where(lane == shift + 49, total, tile)
        for part in range(hidden // channels):
            start = pl.multiple_of(part * channels + c0, 8)
            total = jnp.sum(b_acc[pl.ds(start, 8), :], axis=1, keepdims=True)
            tile = jnp.where(lane == shift + 50 + part, total, tile)
        sums_ref[pl.ds(at, 8), :] = tile
        return carry

    lax.fori_loop(0, channels // 8, kernel_step, 0)


def back_body(
    g_ref, south_ref, halo_ref, before_ref, after_ref, ct_ref, mask_ref, dw_ref, north_ref,
    out_ref, ext, flat,
):
    rows, channels, cols = g_ref.shape
    pairs = cols // 128
    fill(ext, g_ref, south_ref, halo_ref, before_ref, after_ref)

    def step(ct, carry):
        c0 = pl.multiple_of(ct * 8, 8)
        lane = lanes()
        summed = correlate(
            ext, c0, rows, pairs, lane, dw_ref[pl.ds(c0, 8), :], north_ref[pl.ds(c0, 8), :]
        )
        for i in range(rows):
            for t in range(pairs):
                flat[t, pl.ds(c0 * rows + i, 8, stride=rows), :] = summed[i][t]
        return carry

    lax.fori_loop(0, channels // 8, step, 0)
    sea = mask_ref[...].astype(F32)[None]
    grad = gather(flat, channels, rows) + ct_ref[...].astype(F32) * sea
    out_ref[...] = (grad * sea).astype(BF16)


def lat_halo(first, last):
    n_lat, n_lon = lax.axis_size("lat"), lax.axis_size("lon")
    tops = [i * n_lat + n_lat - 1 for i in range(n_lon)]
    mirror = lax.ppermute(last, ("lon", "lat"), list(zip(tops, tops[::-1])))
    south = lax.ppermute(last, "lat", [(i, i + 1) for i in range(n_lat - 1)])
    north = lax.ppermute(first, "lat", [(i + 1, i) for i in range(n_lat - 1)])
    return south, north, mirror


def lon_halo(left, right):
    n_lon = lax.axis_size("lon")
    before = lax.ppermute(right, "lon", [(i, (i + 1) % n_lon) for i in range(n_lon)])
    after = lax.ppermute(left, "lon", [(i, (i - 1) % n_lon) for i in range(n_lon)])
    return before, after


def like(shape, dtype):
    return jax.ShapeDtypeStruct(shape, dtype)


def halo(rows_of, first, last, flip):
    rows, channels, cols = rows_of.shape
    south, north, mirror = lat_halo(first, last)
    strip = like((channels, 128), BF16)
    fold, left, right = call(
        strips_body, [like((RING, channels, cols), BF16), strip, strip],
        rows_of, south, north, mirror, flip,
    )
    before, after = lon_halo(left, right)
    return south, fold, before, after


def total(sums):
    n_lat, n_lon = lax.axis_size("lat"), lax.axis_size("lon")
    size = sums.shape[0] // n_lat
    pieces = sums.reshape(n_lat, size, 128)
    pieces = lax.all_to_all(pieces, "lat", 0, 0, tiled=True)
    own = jnp.sum(pieces, axis=0, keepdims=True)
    own = lax.all_to_all(jnp.broadcast_to(own, (n_lon, size, 128)), "lon", 0, 0, tiled=True)
    own = jnp.sum(own, axis=0, keepdims=True)
    own = lax.all_to_all(jnp.broadcast_to(own, (n_lat, size, 128)), "lat", 0, 0, tiled=True)
    return own.reshape(n_lat * size, 128)


def shards(fields, land_mask, dw_kernel, gain, w_in, b_in, w_out, cotangent):
    channels, rows, cols = fields.shape
    hidden = w_out.shape[0]
    flip = jnp.eye(cols, dtype=BF16)[::-1]
    taps = dw_kernel.reshape(channels, 49)
    turned = taps[:, ::-1]
    is_top = lax.axis_index("lat") == lax.axis_size("lat") - 1
    north = jnp.where(is_top, taps, turned)
    ring = like((RING, channels, cols), BF16)
    grid = like((rows, channels, cols), BF16)
    whole = like((channels, rows, cols), BF16)
    flat = pltpu.VMEM((cols // 128, channels * rows, 128), F32)
    ext = pltpu.VMEM((rows + 2 * RING, channels, cols + 128), F32)
    masked, first, last = call(rows_body, [grid, ring, ring], fields, land_mask, scratch=[flat])
    south, fold, before, after = halo(masked, first, last, flip)
    cells = rows * cols
    output, grads, first, last, sums = call(
        block_body,
        [whole, grid, ring, ring, like((2 * channels + hidden, 128), F32)],
        masked, south, fold, before, after, cotangent, land_mask,
        taps, gain[:, None], w_in, w_in.T, b_in[:, None], w_out, w_out.T,
        scratch=[
            ext,
            pltpu.VMEM((rows, channels, cols), F32),
            flat,
            pltpu.VMEM((hidden, cells), BF16),
            pltpu.VMEM((channels, cells), BF16),
            pltpu.VMEM((channels, cells), BF16),
            pltpu.VMEM((hidden, cells), BF16),
            pltpu.VMEM((hidden, 128), F32),
            pltpu.VMEM((channels, 128), F32),
        ],
    )
    south, fold, before, after = halo(grads, first, last, flip)
    (input_grad,) = call(
        back_body, [whole], grads, south, fold, before, after, cotangent, land_mask, turned, north,
        scratch=[ext, flat],
    )
    scale = float(cells * lax.axis_size("lat") * lax.axis_size("lon")) ** -0.5
    sums = total(sums) * scale
    low = channels + hidden
    shift = hidden - 128
    tail = sums[low:, shift:]
    return (
        output,
        input_grad,
        tail[:, :49].reshape(channels, 7, 7),
        tail[:, 49],
        jnp.concatenate([sums[:channels], sums[low:, :shift]], axis=1),
        tail[:, 50 : 50 + hidden // channels].T.reshape(hidden),
        sums[channels:low, :channels],
    )


def solution(mesh):
    tiles = P(None, "lat", "lon")
    return jax.shard_map(
        shards,
        mesh=mesh,
        in_specs=(tiles, P("lat", "lon"), P(), P(), P(), P(), P(), tiles),
        out_specs=(tiles, tiles, P(), P(), P(), P(), P()),
        check_vma=False,
    )
```

time: 451 us -> 136 us (0.30)
  the two profiles are of different devices: /device:TPU:1 before, /device:TPU:15 now
where the time goes in v1:
time: 136 us; the launch traced here: 135 us
  starting transfers between devices  42.3 us (31%)
  Pallas kernels  35.1 us (26%)
  waiting for transfers between devices  20.9 us (15%)
  blocking collectives  20.6 us (15%)
  local copies, waits for them, and re-layouts  13.5 us (10%)
  other arithmetic  1.37 us (1%)
    pallas_call x5, Pallas kernels, call(): pl.pallas_call(body, out_shape=outs, in_specs=[pl.BlockSpec(memory_space=...  35.1 us
    all_to_all x1, blocking collectives, total(): pieces = lax.all_to_all(pieces, 'lat', 0, 0, tiled=True)  20.6 us
    all_to_all x1, waiting for transfers between devices, total(): lax.all_to_all(jnp.broadcast_to(own, (n_lon, size, 128)), 'lon', 0, 0, ti...  10.8 us
    ppermute x2, starting transfers between devices, lon_halo(): lax.ppermute(right, 'lon', [(i, (i + 1) % n_lon) for i in range(n_lon)])  10.6 us
    all_to_all x1, starting transfers between devices, total(): lax.all_to_all(jnp.broadcast_to(own, (n_lon, size, 128)), 'lon', 0, 0, ti...  9.16 us
    ppermute x2, waiting for transfers between devices, lon_halo(): lax.ppermute(left, 'lon', [(i, (i - 1) % n_lon) for i in range(n_lon)])  7.13 us
    ppermute x2, starting transfers between devices, lat_halo(): north = lax.ppermute(first, 'lat', [(i + 1, i) for i in range(n_lat - 1)])  6.3 us
    ppermute x2, starting transfers between devices, lat_halo(): south = lax.ppermute(last, 'lat', [(i, i + 1) for i in range(n_lat - 1)])  6.05 us
  transfers between devices with their start and end apart: 12, of which 4 were waited for; matrix products, arithmetic and copies ran while one was open for 5% of the time, Pallas kernels for 8%

profile of v1, /device:TPU:15, one launch (start us, length us, event | category | flops | bytes accessed | tf_op | source)
XLA Modules:
  0.0 134.7 jit_solution(16610218318343037325)
XLA Ops:
  0.6 2.0 %shard_map.135 = (bf16[8,96,256]{2,1,0:T(8,128)(2,1)}, bf16[3,96,256]{2,1,0:T(8,128)(2,1)}, bf16[3,96,256]{2,1,0:T(8,128)(2,1)}) custom-call(bf16[96,8,256]{2,1,0:T(8,128)(2,1)} %f_ref.1, s32[8,256]{1,0:T(8,128)} %mask_ref.5), custom_call_target="tpu_custom_call" | custom-call | tf_op jit(solution)/shard_map/pallas_call | solution.py:17
  2.6 4.0 %collective-permute-start = (bf16[3,96,256]{2,1,0:T(8,128)(2,1)}, bf16[3,96,256]{2,1,0:T(8,128)(2,1)S(1)}, u32[]{:S(2)}, u32[]{:S(2)}) collective-permute-start(bf16[3,96,256]{2,1,0:T(8,128)(2,1)} %get-tuple-element.22), channel_id=1, source_target_pairs={{0,1},{1,2},{2,3},{3,4},{4,5},{5,6},{6,7},{7,8},{8,9},{9,10},{10,1... | collective-permute-start | bytes 442376 | tf_op jit(solution)/shard_map/ppermute | solution.py:292
  6.6 0.7 collective-permute-start.2
  7.3 2.2 %collective-permute-start.1 = (bf16[3,96,256]{2,1,0:T(8,128)(2,1)}, bf16[3,96,256]{2,1,0:T(8,128)(2,1)S(1)}, u32[]{:S(2)}, u32[]{:S(2)}) collective-permute-start(bf16[3,96,256]{2,1,0:T(8,128)(2,1)} %get-tuple-element.23), channel_id=1, source_target_pairs={{1,0},{2,1},{3,2},{4,3},{5,4},{6,5},{7,6},{8,7},{9,8},{10,9},{11,1... | collective-permute-start | bytes 442376 | tf_op jit(solution)/shard_map/ppermute | solution.py:293
  9.5 1.3 rev.6.flip_ref
  10.8 0.0 collective-permute-done.south_ref
  10.9 0.0 collective-permute-done.2.mirror_ref
  10.9 0.0 copy-start.8
  10.9 2.9 %collective-permute-done.1.north_ref = bf16[3,96,256]{2,1,0:T(8,128)(2,1)S(1)} collective-permute-done((bf16[3,96,256]{2,1,0:T(8,128)(2,1)}, bf16[3,96,256]{2,1,0:T(8,128)(2,1)S(1)}, u32[]{:S(2)}, u32[]{:S(2)}) %collective-permute-start.1) | collective-permute-done | bytes 147488 | tf_op jit(solution)/shard_map/ppermute | solution.py:293
  13.8 0.0 copy-done.2
  13.8 0.7 copy-done.9
  14.5 2.2 %shard_map.136 = (bf16[3,96,256]{2,1,0:T(8,128)(2,1)}, bf16[96,128]{1,0:T(8,128)(2,1)}, bf16[96,128]{1,0:T(8,128)(2,1)}) custom-call(bf16[8,96,256]{2,1,0:T(8,128)(2,1)} %get-tuple-element.21.m_ref, bf16[3,96,256]{2,1,0:T(8,128)(2,1)} %copy-done.2, bf16[3,96,256]{2,1,0:T(8,128)(2,1)} %copy-done.9, bf16[3,96,256]{2,1,0:T(8,128)(2,1)} %copy-done.8, ...), custom_call_target="tpu_custom_call" | custom-call | tf_op jit(solution)/shard_map/pallas_call | solution.py:17
  16.6 7.5 %collective-permute-start.3 = (bf16[96,128]{1,0:T(8,128)(2,1)}, bf16[96,128]{1,0:T(8,128)(2,1)S(1)}, u32[]{:S(2)}, u32[]{:S(2)}) collective-permute-start(bf16[96,128]{1,0:T(8,128)(2,1)} %get-tuple-element.25), channel_id=1, source_target_pairs={{0,16},{16,32},{32,48},{48,64},{64,80},{80,96},{96,112},{112,128},... | collective-permute-start | bytes 73736 | tf_op jit(solution)/shard_map/ppermute | solution.py:299
  24.1 1.9 %collective-permute-start.4 = (bf16[96,128]{1,0:T(8,128)(2,1)}, bf16[96,128]{1,0:T(8,128)(2,1)S(1)}, u32[]{:S(2)}, u32[]{:S(2)}) collective-permute-start(bf16[96,128]{1,0:T(8,128)(2,1)} %get-tuple-element.26), channel_id=1, source_target_pairs={{0,496},{16,0},{32,16},{48,32},{64,48},{80,64},{96,80},{112,96},{1... | collective-permute-start | bytes 73736 | tf_op jit(solution)/shard_map/ppermute | solution.py:300
  26.0 0.7 copy.30.dw_ref
  26.8 0.7 copy-done.15
  27.4 0.8 copy.32.b_ref
  28.2 0.0 copy-done.4
  28.2 0.7 copy.28
  29.0 0.1 copy-done.5
  29.0 0.7 copy.29
  29.7 0.7 copy-done.16
  30.4 0.7 copy.31.gain_ref
  31.1 0.0 collective-permute-done.3.before_ref
  31.1 1.3 collective-permute-done.4.after_ref
  32.5 0.6 copy-done.12
  33.1 20.6 %shard_map.137 = (bf16[96,8,256]{2,1,0:T(8,128)(2,1)}, bf16[8,96,256]{2,1,0:T(8,128)(2,1)}, bf16[3,96,256]{2,1,0:T(8,128)(2,1)}, bf16[3,96,256]{2,1,0:T(8,128)(2,1)}, f32[384,128]{1,0:T(8,128)}) custom-call(bf16[8,96,256]{2,1,0:T(8,128)(2,1)} %get-tuple-element.21.m_ref, bf16[3,96,256]{2,1,0:T(8,128)(2,1)} %copy-done.2, ...), custom_call_target="tpu_custom_call" | custom-call | tf_op jit(solution)/shard_map/pallas_call | solution.py:17
  53.7 20.6 %all_to_all.15 = f32[16,24,128]{2,1,0:T(8,128)S(1)} all-to-all(f32[16,24,128]{2,1,0:T(8,128)} %bitcast.20), channel_id=1, replica_groups=mesh['lon'=32,'lat'=16] {'lat'}, dimensions={0} | all-to-all | bytes 393216 | tf_op jit(solution)/shard_map/all_to_all | solution.py:324
  74.3 0.8 broadcast_in_dim.20
  75.1 9.2 %all-to-all-start.1 = ((f32[32,24,128]{2,1,0:T(8,128)}), f32[32,24,128]{2,1,0:T(8,128)S(1)}, u32[]{:S(2)}, u32[]{:S(2)}) async-start(f32[32,24,128]{2,1,0:T(8,128)} %broadcast_in_dim.20), calls=%async_computation.1 | async-start | bytes 786432 | tf_op jit(solution)/shard_map/all_to_all | solution.py:326
  84.3 2.1 %collective-permute-start.5 = (bf16[3,96,256]{2,1,0:T(8,128)(2,1)S(1)}, bf16[3,96,256]{2,1,0:T(8,128)(2,1)S(1)}, u32[]{:S(2)}, u32[]{:S(2)}) collective-permute-start(bf16[3,96,256]{2,1,0:T(8,128)(2,1)S(1)} %copy-done.18), channel_id=1, source_target_pairs={{0,1},{1,2},{2,3},{3,4},{4,5},{5,6},{6,7},{7,8},{8,9},{9,10},{10,1... | collective-permute-start | bytes 442376 | tf_op jit(solution)/shard_map/ppermute | solution.py:292
  86.3 0.7 collective-permute-start.7
  87.0 4.1 %collective-permute-start.6 = (bf16[3,96,256]{2,1,0:T(8,128)(2,1)S(1)}, bf16[3,96,256]{2,1,0:T(8,128)(2,1)S(1)}, u32[]{:S(2)}, u32[]{:S(2)}) collective-permute-start(bf16[3,96,256]{2,1,0:T(8,128)(2,1)S(1)} %copy-done.17), channel_id=1, source_target_pairs={{1,0},{2,1},{3,2},{4,3},{5,4},{6,5},{7,6},{8,7},{9,8},{10,9},{11,1... | collective-permute-start | bytes 442376 | tf_op jit(solution)/shard_map/ppermute | solution.py:293
  91.1 10.8 %all-to-all-done.1 = f32[32,24,128]{2,1,0:T(8,128)S(1)} async-done(((f32[32,24,128]{2,1,0:T(8,128)}), f32[32,24,128]{2,1,0:T(8,128)S(1)}, u32[]{:S(2)}, u32[]{:S(2)}) %all-to-all-start.1) | async-done | bytes 393248 | tf_op jit(solution)/shard_map/all_to_all | solution.py:326
  102.0 0.7 broadcast_in_dim.21
  102.7 5.0 %all-to-all-start.2 = ((f32[16,24,128]{2,1,0:T(8,128)}), f32[16,24,128]{2,1,0:T(8,128)S(1)}, u32[]{:S(2)}, u32[]{:S(2)}) async-start(f32[16,24,128]{2,1,0:T(8,128)} %broadcast_in_dim.21), calls=%async_computation.2 | async-start | bytes 393216 | tf_op jit(solution)/shard_map/all_to_all | solution.py:328
  107.8 0.1 rev.7.dw_ref
  107.8 0.0 collective-permute-done.5.south_ref
  107.8 0.0 copy-start.1
  107.8 0.0 collective-permute-done.7.mirror_ref
  107.9 0.0 collective-permute-done.6.north_ref
  107.9 0.0 copy-start.7
  107.9 0.6 copy-done.1
  108.5 0.1 copy-done.6
  108.6 0.0 copy-done.7
  108.6 2.1 %shard_map.138 = (bf16[3,96,256]{2,1,0:T(8,128)(2,1)}, bf16[96,128]{1,0:T(8,128)(2,1)}, bf16[96,128]{1,0:T(8,128)(2,1)}) custom-call(bf16[8,96,256]{2,1,0:T(8,128)(2,1)} %get-tuple-element.28.m_ref.g_ref, bf16[3,96,256]{2,1,0:T(8,128)(2,1)} %copy-done.1, bf16[3,96,256]{2,1,0:T(8,128)(2,1)} %copy-done.7, bf16[3,96,256]{2,1,0:T(8,128)(2,1)} %copy-done.6, ...), custom_call_target="tpu_custom_call" | custom-call | tf_op jit(solution)/shard_map/pallas_call | solution.py:17
  110.8 3.1 %collective-permute-start.8 = (bf16[96,128]{1,0:T(8,128)(2,1)}, bf16[96,128]{1,0:T(8,128)(2,1)S(1)}, u32[]{:S(2)}, u32[]{:S(2)}) collective-permute-start(bf16[96,128]{1,0:T(8,128)(2,1)} %get-tuple-element.32), channel_id=1, source_target_pairs={{0,16},{16,32},{32,48},{48,64},{64,80},{80,96},{96,112},{112,128},... | collective-permute-start | bytes 73736 | tf_op jit(solution)/shard_map/ppermute | solution.py:299
  113.9 1.9 %collective-permute-start.9 = (bf16[96,128]{1,0:T(8,128)(2,1)}, bf16[96,128]{1,0:T(8,128)(2,1)S(1)}, u32[]{:S(2)}, u32[]{:S(2)}) collective-permute-start(bf16[96,128]{1,0:T(8,128)(2,1)} %get-tuple-element.33), channel_id=1, source_target_pairs={{0,496},{16,0},{32,16},{48,32},{64,48},{80,64},{96,80},{112,96},{1... | collective-permute-start | bytes 73736 | tf_op jit(solution)/shard_map/ppermute | solution.py:300
  115.9 0.0 copy-done.3
  115.9 0.6 broadcast_select_fusion.north_ref
  116.5 0.0 collective-permute-done.8.before_ref
  116.5 5.8 %collective-permute-done.9.after_ref = bf16[96,128]{1,0:T(8,128)(2,1)S(1)} collective-permute-done((bf16[96,128]{1,0:T(8,128)(2,1)}, bf16[96,128]{1,0:T(8,128)(2,1)S(1)}, u32[]{:S(2)}, u32[]{:S(2)}) %collective-permute-start.9) | collective-permute-done | bytes 24608 | tf_op jit(solution)/shard_map/ppermute | solution.py:300
  122.3 0.6 copy-done.14
  122.9 8.1 %shard_map.139 = bf16[96,8,256]{2,1,0:T(8,128)(2,1)} custom-call(bf16[8,96,256]{2,1,0:T(8,128)(2,1)} %get-tuple-element.28.m_ref.g_ref, bf16[3,96,256]{2,1,0:T(8,128)(2,1)} %copy-done.1, bf16[3,96,256]{2,1,0:T(8,128)(2,1)} %get-tuple-element.31.halo_ref, bf16[96,128]{1,0:T(8,128)(2,1)} %copy-done.13, bf16[96,128]{1,0:T(8,128)(2,1)} %copy-done.14, ...), custom_call_target="tpu_custom_call" | custom-call | tf_op jit(solution)/shard_map/pallas_call | solution.py:17
  131.0 0.0 all-to-all-done.2
  131.1 0.1 slice.32
  131.2 0.7 slice.37
  131.8 0.1 slice_bitcast_fusion
  131.9 0.7 slice_reduce_fusion
  132.6 0.1 copy.35
  132.7 0.6 reshape.34
  133.3 0.1 copy.36
  133.4 0.7 reshape.35
  134.0 0.6 pad_maximum_fusion
  (30 shorter events, 0.2 us)
Async XLA Ops:
  2.6 8.2 %collective-permute-start = (bf16[3,96,256]{2,1,0:T(8,128)(2,1)}, bf16[3,96,256]{2,1,0:T(8,128)(2,1)S(1)}, u32[]{:S(2)}, u32[]{:S(2)}) collective-permute-start(bf16[3,96,256]{2,1,0:T(8,128)(2,1)} %get-tuple-element.22), channel_id=1, source_target_pairs={{0,1},{1,2},{2,3},{3,4},{4,5},{5,6},{6,7},{7,8},{8,9},{9,10},{10,1... | collective-permute-start | bytes 442376 | tf_op jit(solution)/shard_map/ppermute | solution.py:292
  6.6 4.2 %collective-permute-start.2 = (bf16[3,96,256]{2,1,0:T(8,128)(2,1)}, bf16[3,96,256]{2,1,0:T(8,128)(2,1)S(1)}, u32[]{:S(2)}, u32[]{:S(2)}) collective-permute-start(bf16[3,96,256]{2,1,0:T(8,128)(2,1)} %get-tuple-element.22), channel_id=1, source_target_pairs={{15,511},{31,495},{47,479},{63,463},{79,447},{95,431},{111,415},{1... | collective-permute-start | bytes 442376 | tf_op jit(solution)/shard_map/ppermute | solution.py:291
  7.3 6.5 %collective-permute-start.1 = (bf16[3,96,256]{2,1,0:T(8,128)(2,1)}, bf16[3,96,256]{2,1,0:T(8,128)(2,1)S(1)}, u32[]{:S(2)}, u32[]{:S(2)}) collective-permute-start(bf16[3,96,256]{2,1,0:T(8,128)(2,1)} %get-tuple-element.23), channel_id=1, source_target_pairs={{1,0},{2,1},{3,2},{4,3},{5,4},{6,5},{7,6},{8,7},{9,8},{10,9},{11,1... | collective-permute-start | bytes 442376 | tf_op jit(solution)/shard_map/ppermute | solution.py:293
  10.9 3.0 %copy-start.2 = (bf16[3,96,256]{2,1,0:T(8,128)(2,1)}, bf16[3,96,256]{2,1,0:T(8,128)(2,1)S(1)}, u32[]{:S(2)}) copy-start(bf16[3,96,256]{2,1,0:T(8,128)(2,1)S(1)} %collective-permute-done.south_ref) | copy-start | bytes 442372
  10.9 3.0 %copy-start.8 = (bf16[3,96,256]{2,1,0:T(8,128)(2,1)}, bf16[3,96,256]{2,1,0:T(8,128)(2,1)S(1)}, u32[]{:S(2)}) copy-start(bf16[3,96,256]{2,1,0:T(8,128)(2,1)S(1)} %collective-permute-done.2.mirror_ref) | copy-start | bytes 442372
  13.8 0.7 copy-start.9
  14.5 11.6 %copy-start.10 = (f32[96,7,7]{0,2,1:T(8,128)S(1)}, f32[96,7,7]{0,2,1:T(8,128)}, u32[]{:S(2)}) copy-start(f32[96,7,7]{0,2,1:T(8,128)} %param.10) | copy-start | bytes 56452
  16.6 14.5 %collective-permute-start.3 = (bf16[96,128]{1,0:T(8,128)(2,1)}, bf16[96,128]{1,0:T(8,128)(2,1)S(1)}, u32[]{:S(2)}, u32[]{:S(2)}) collective-permute-start(bf16[96,128]{1,0:T(8,128)(2,1)} %get-tuple-element.25), channel_id=1, source_target_pairs={{0,16},{16,32},{32,48},{48,64},{64,80},{80,96},{96,112},{112,128},... | collective-permute-start | bytes 73736 | tf_op jit(solution)/shard_map/ppermute | solution.py:299
  24.1 8.4 %collective-permute-start.4 = (bf16[96,128]{1,0:T(8,128)(2,1)}, bf16[96,128]{1,0:T(8,128)(2,1)S(1)}, u32[]{:S(2)}, u32[]{:S(2)}) collective-permute-start(bf16[96,128]{1,0:T(8,128)(2,1)} %get-tuple-element.26), channel_id=1, source_target_pairs={{0,496},{16,0},{32,16},{48,32},{64,48},{80,64},{96,80},{112,96},{1... | collective-permute-start | bytes 73736 | tf_op jit(solution)/shard_map/ppermute | solution.py:300
  26.8 0.7 copy-start.15
  27.4 0.8 copy-start.4
  28.2 0.8 copy-start.5
  29.7 0.7 copy-start.16
  31.1 1.3 copy-start.11
  32.5 0.6 copy-start.12
  75.1 9.2 %copy-start.18 = (bf16[3,96,256]{2,1,0:T(8,128)(2,1)S(1)}, bf16[3,96,256]{2,1,0:T(8,128)(2,1)}, u32[]{:S(2)}) copy-start(bf16[3,96,256]{2,1,0:T(8,128)(2,1)} %get-tuple-element.29) | copy-start | bytes 442372
  75.1 11.9 %copy-start.17 = (bf16[3,96,256]{2,1,0:T(8,128)(2,1)S(1)}, bf16[3,96,256]{2,1,0:T(8,128)(2,1)}, u32[]{:S(2)}) copy-start(bf16[3,96,256]{2,1,0:T(8,128)(2,1)} %get-tuple-element.30) | copy-start | bytes 442372
  75.1 26.9 %all-to-all-start.1 = ((f32[32,24,128]{2,1,0:T(8,128)}), f32[32,24,128]{2,1,0:T(8,128)S(1)}, u32[]{:S(2)}, u32[]{:S(2)}) async-start(f32[32,24,128]{2,1,0:T(8,128)} %broadcast_in_dim.20), calls=%async_computation.1 | async-start | bytes 786432 | tf_op jit(solution)/shard_map/all_to_all | solution.py:326
  84.3 23.6 %collective-permute-start.5 = (bf16[3,96,256]{2,1,0:T(8,128)(2,1)S(1)}, bf16[3,96,256]{2,1,0:T(8,128)(2,1)S(1)}, u32[]{:S(2)}, u32[]{:S(2)}) collective-permute-start(bf16[3,96,256]{2,1,0:T(8,128)(2,1)S(1)} %copy-done.18), channel_id=1, source_target_pairs={{0,1},{1,2},{2,3},{3,4},{4,5},{5,6},{6,7},{7,8},{8,9},{9,10},{10,1... | collective-permute-start | bytes 442376 | tf_op jit(solution)/shard_map/ppermute | solution.py:292
  86.3 21.5 %collective-permute-start.7 = (bf16[3,96,256]{2,1,0:T(8,128)(2,1)S(1)}, bf16[3,96,256]{2,1,0:T(8,128)(2,1)S(1)}, u32[]{:S(2)}, u32[]{:S(2)}) collective-permute-start(bf16[3,96,256]{2,1,0:T(8,128)(2,1)S(1)} %copy-done.18), channel_id=1, source_target_pairs={{15,511},{31,495},{47,479},{63,463},{79,447},{95,431},{111,415},{1... | collective-permute-start | bytes 442376 | tf_op jit(solution)/shard_map/ppermute | solution.py:291
  87.0 20.9 %collective-permute-start.6 = (bf16[3,96,256]{2,1,0:T(8,128)(2,1)S(1)}, bf16[3,96,256]{2,1,0:T(8,128)(2,1)S(1)}, u32[]{:S(2)}, u32[]{:S(2)}) collective-permute-start(bf16[3,96,256]{2,1,0:T(8,128)(2,1)S(1)} %copy-done.17), channel_id=1, source_target_pairs={{1,0},{2,1},{3,2},{4,3},{5,4},{6,5},{7,6},{8,7},{9,8},{10,9},{11,1... | collective-permute-start | bytes 442376 | tf_op jit(solution)/shard_map/ppermute | solution.py:293
  102.7 5.0 %copy-start = (f32[96,49]{1,0:T(8,128)S(1)}, f32[96,49]{1,0:T(8,128)}, u32[]{:S(2)}) copy-start(f32[96,49]{1,0:T(8,128)} %copy.30.dw_ref) | copy-start | bytes 56452
  102.7 28.3 %all-to-all-start.2 = ((f32[16,24,128]{2,1,0:T(8,128)}), f32[16,24,128]{2,1,0:T(8,128)S(1)}, u32[]{:S(2)}, u32[]{:S(2)}) async-start(f32[16,24,128]{2,1,0:T(8,128)} %broadcast_in_dim.21), calls=%async_computation.2 | async-start | bytes 393216 | tf_op jit(solution)/shard_map/all_to_all | solution.py:328
  107.8 8.0 %copy-start.3 = (f32[96,49]{1,0:T(8,128)}, f32[96,49]{1,0:T(8,128)S(1)}, u32[]{:S(2)}) copy-start(f32[96,49]{1,0:T(8,128)S(1)} %rev.7.dw_ref) | copy-start | bytes 56452
  107.8 0.7 copy-start.1
  107.9 0.7 copy-start.6
  107.9 0.8 copy-start.7
  110.8 5.7 %collective-permute-start.8 = (bf16[96,128]{1,0:T(8,128)(2,1)}, bf16[96,128]{1,0:T(8,128)(2,1)S(1)}, u32[]{:S(2)}, u32[]{:S(2)}) collective-permute-start(bf16[96,128]{1,0:T(8,128)(2,1)} %get-tuple-element.32), channel_id=1, source_target_pairs={{0,16},{16,32},{32,48},{48,64},{64,80},{80,96},{96,112},{112,128},... | collective-permute-start | bytes 73736 | tf_op jit(solution)/shard_map/ppermute | solution.py:299
  113.9 8.4 %collective-permute-start.9 = (bf16[96,128]{1,0:T(8,128)(2,1)}, bf16[96,128]{1,0:T(8,128)(2,1)S(1)}, u32[]{:S(2)}, u32[]{:S(2)}) collective-permute-start(bf16[96,128]{1,0:T(8,128)(2,1)} %get-tuple-element.33), channel_id=1, source_target_pairs={{0,496},{16,0},{32,16},{48,32},{64,48},{80,64},{96,80},{112,96},{1... | collective-permute-start | bytes 73736 | tf_op jit(solution)/shard_map/ppermute | solution.py:300
  116.5 5.8 %copy-start.13 = (bf16[96,128]{1,0:T(8,128)(2,1)}, bf16[96,128]{1,0:T(8,128)(2,1)S(1)}, u32[]{:S(2)}) copy-start(bf16[96,128]{1,0:T(8,128)(2,1)S(1)} %collective-permute-done.8.before_ref) | copy-start | bytes 73732
  122.3 0.6 copy-start.14

commit v2 on v1

--- a/solution.py
+++ b/solution.py
@@ -13,15 +13,23 @@
 RING = 3
 
 
-def call(body, outs, *args, scratch=()):
+def call(body, outs, *args, scratch=(), smem=0, waits=()):
+    specs = [pl.BlockSpec(memory_space=pltpu.VMEM)] * (len(args) - smem)
+    specs += [pl.BlockSpec(memory_space=pltpu.SMEM)] * smem
+    specs += [pl.BlockSpec(memory_space=pl.ANY)] * len(waits)
+    count = len(args)
+
+    def run(*refs):
+        body(*refs[:count], *refs[count + len(waits) :])
+
     return pl.pallas_call(
-        body,
+        run,
         out_shape=outs,
-        in_specs=[pl.BlockSpec(memory_space=pltpu.VMEM)] * len(args),
+        in_specs=specs,
         out_specs=[pl.BlockSpec(memory_space=pltpu.VMEM)] * len(outs),
         scratch_shapes=list(scratch),
         compiler_params=pltpu.CompilerParams(vmem_limit_bytes=VMEM_LIMIT),
-    )(*args)
+    )(*args, *waits)
 
 
 def lanes():
@@ -58,10 +66,13 @@
             last_ref[i - (rows - RING)] = row
 
 
-def strips_body(m_ref, south_ref, north_ref, mirror_ref, flip_ref, halo_ref, left_ref, right_ref):
+def strips_body(m_ref, south_ref, north_ref, mirror_ref, halo_ref, left_ref, right_ref):
     rows, channels, cols = m_ref.shape
+    here = lax.broadcasted_iota(jnp.int32, (cols, cols), 0)
+    there = lax.broadcasted_iota(jnp.int32, (cols, cols), 1)
+    flip = (here + there == cols - 1).astype(F32).astype(BF16)
     for k in range(RING):
-        turned = jnp.dot(mirror_ref[RING - 1 - k], flip_ref[...], preferred_element_type=F32)
+        turned = jnp.dot(mirror_ref[RING - 1 - k], flip, preferred_element_type=F32)
         halo_ref[k] = (north_ref[k].astype(F32) + turned).astype(BF16)
     lane = lax.broadcasted_iota(jnp.int32, (channels, 128), 1)
     left = jnp.zeros((channels, 128), F32)
@@ -122,11 +133,15 @@
     return jnp.broadcast_to(weights[:, index : index + 1], (8, 128))
 
 
-def correlate(ext, c0, rows, pairs, lane, weights, north):
+def correlate(ext, c0, rows, pairs, lane, weights, top):
     summed = [[None] * pairs for _ in range(rows)]
     for b in range(7):
-        taps = [tap(weights, a * 7 + b) for a in range(7)]
-        far = taps if north is None else [tap(north, a * 7 + b) for a in range(7)]
+        if top is None:
+            taps = [tap(weights, a * 7 + b) for a in range(7)]
+            far = taps
+        else:
+            taps = [tap(weights, 48 - a * 7 - b) for a in range(7)]
+            far = [jnp.where(top, tap(weights, a * 7 + b), taps[a]) for a in range(7)]
         for r in range(rows + 2 * RING):
             tiles = [ext[r, pl.ds(c0, 8), t * 128 : t * 128 + 128] for t in range(pairs + 1)]
             wins = windows(tiles, b - RING, lane)
@@ -143,9 +158,9 @@
 
 def block_body(
     m_ref, south_ref, halo_ref, before_ref, after_ref, ct_ref, mask_ref,
-    dw_ref, gain_ref, w_in_ref, w_in_t_ref, b_ref, w_out_ref, w_out_t_ref,
+    dw_ref, gain_ref, w_in_ref, b_ref, w_out_ref,
     out_ref, g_ref, first_ref, last_ref, sums_ref,
-    ext, conv, flat, act, back, sca, pre, b_acc, gain_acc,
+    ext, conv, flat, act, back, sca, pre, b_acc, gain_acc, tail,
 ):
     rows, channels, cols = m_ref.shape
     hidden = w_out_ref.shape[0]
@@ -169,8 +184,12 @@
 
     b_acc[...] = jnp.zeros_like(b_acc)
     gain_acc[...] = jnp.zeros_like(gain_acc)
-    gain = jnp.broadcast_to(gain_ref[...], (channels, cols))
-    bias = jnp.broadcast_to(b_ref[...], (hidden, cols))
+    gain = jnp.broadcast_to(gain_ref[...], (128, channels)).T
+    gain = jnp.concatenate([gain] * pairs, axis=1)
+    bias = jnp.broadcast_to(b_ref[...], (128, hidden)).T
+    bias = jnp.concatenate([bias] * pairs, axis=1)
+    w_in_t = w_in_ref[...].T
+    w_out_t = w_out_ref[...].T
     root = 0.7978845608028654
     for i in range(rows):
         span = slice(i * cols, i * cols + cols)
@@ -180,14 +199,14 @@
         normed = centred * inv_std
         scaled = (normed * gain).astype(BF16)
         sca[:, span] = scaled
-        v = jnp.dot(w_in_t_ref[...], scaled, preferred_element_type=F32) + bias
+        v = jnp.dot(w_in_t, scaled, preferred_element_type=F32) + bias
         v2 = v * v
         t = jnp.tanh(root * v * (1.0 + 0.044715 * v2))
         half = 0.5 * (1.0 + t)
         activated = (v * half).astype(BF16)
         act[:, span] = activated
         slope = half + 0.5 * v * (1.0 - t * t) * (root * (1.0 + 3 * 0.044715 * v2))
-        mixed = jnp.dot(w_out_t_ref[...], activated, preferred_element_type=F32)
+        mixed = jnp.dot(w_out_t, activated, preferred_element_type=F32)
         mixed = m_ref[i].astype(F32) + mixed
         for t in range(pairs):
             flat[t, pl.ds(i, channels, stride=rows), :] = mixed[:, t * 128 : t * 128 + 128]
@@ -217,19 +236,18 @@
     over_cells = (((1,), (1,)), ((), ()))
     w_in_sum = lax.dot_general(sca[...], pre[...], over_cells, preferred_element_type=F32)
     w_out_sum = lax.dot_general(act[...], back[...], over_cells, preferred_element_type=F32)
-    sums_ref[0:channels, :] = w_in_sum[:, 0:128]
-    sums_ref[channels : channels + hidden, :] = jnp.zeros((hidden, 128), F32)
-    sums_ref[channels : channels + hidden, 0:channels] = w_out_sum
     low = channels + hidden
-    sums_ref[low : low + channels, :] = jnp.zeros((channels, 128), F32)
-    sums_ref[low : low + channels, 0 : hidden - 128] = w_in_sum[:, 128:hidden]
     shift = hidden - 128
+    sums_ref[0:channels, :] = w_in_sum[:, 0:128].astype(BF16)
+    blank = jnp.zeros((hidden, 128 - channels), F32)
+    sums_ref[channels:low, :] = jnp.concatenate([w_out_sum, blank], axis=1).astype(BF16)
+    blank = jnp.zeros((channels, 128 - shift), F32)
+    tail[...] = jnp.concatenate([w_in_sum[:, 128:hidden], blank], axis=1)
 
     def kernel_step(ct, carry):
         c0 = pl.multiple_of(ct * 8, 8)
         lane = lanes()
-        at = pl.multiple_of(low + c0, 8)
-        tile = sums_ref[pl.ds(at, 8), :]
+        tile = tail[pl.ds(c0, 8), :]
         grads = [
             [conv[i, pl.ds(c0, 8), t * 128 : t * 128 + 128] for t in range(pairs)]
             for i in range(rows)
@@ -254,14 +272,15 @@
             start = pl.multiple_of(part * channels + c0, 8)
             total = jnp.sum(b_acc[pl.ds(start, 8), :], axis=1, keepdims=True)
             tile = jnp.where(lane == shift + 50 + part, total, tile)
-        sums_ref[pl.ds(at, 8), :] = tile
+        tail[pl.ds(c0, 8), :] = tile
         return carry
 
     lax.fori_loop(0, channels // 8, kernel_step, 0)
+    sums_ref[low : low + channels, :] = tail[...].astype(BF16)
 
 
 def back_body(
-    g_ref, south_ref, halo_ref, before_ref, after_ref, ct_ref, mask_ref, dw_ref, north_ref,
+    g_ref, south_ref, halo_ref, before_ref, after_ref, ct_ref, mask_ref, dw_ref, top_ref,
     out_ref, ext, flat,
 ):
     rows, channels, cols = g_ref.shape
@@ -271,9 +290,8 @@
     def step(ct, carry):
         c0 = pl.multiple_of(ct * 8, 8)
         lane = lanes()
-        summed = correlate(
-            ext, c0, rows, pairs, lane, dw_ref[pl.ds(c0, 8), :], north_ref[pl.ds(c0, 8), :]
-        )
+        top = jnp.broadcast_to(top_ref[0], (8, 128)) > 0
+        summed = correlate(ext, c0, rows, pairs, lane, dw_ref[pl.ds(c0, 8), :], top)
         for i in range(rows):
             for t in range(pairs):
                 flat[t, pl.ds(c0 * rows + i, 8, stride=rows), :] = summed[i][t]
@@ -305,51 +323,58 @@
     return jax.ShapeDtypeStruct(shape, dtype)
 
 
-def halo(rows_of, first, last, flip):
+def halo(rows_of, first, last):
     rows, channels, cols = rows_of.shape
     south, north, mirror = lat_halo(first, last)
     strip = like((channels, 128), BF16)
     fold, left, right = call(
         strips_body, [like((RING, channels, cols), BF16), strip, strip],
-        rows_of, south, north, mirror, flip,
+        rows_of, south, north, mirror,
     )
     before, after = lon_halo(left, right)
-    return south, fold, before, after
-
-
-def total(sums):
-    n_lat, n_lon = lax.axis_size("lat"), lax.axis_size("lon")
-    size = sums.shape[0] // n_lat
-    pieces = sums.reshape(n_lat, size, 128)
-    pieces = lax.all_to_all(pieces, "lat", 0, 0, tiled=True)
-    own = jnp.sum(pieces, axis=0, keepdims=True)
-    own = lax.all_to_all(jnp.broadcast_to(own, (n_lon, size, 128)), "lon", 0, 0, tiled=True)
-    own = jnp.sum(own, axis=0, keepdims=True)
-    own = lax.all_to_all(jnp.broadcast_to(own, (n_lat, size, 128)), "lat", 0, 0, tiled=True)
-    return own.reshape(n_lat * size, 128)
+    return (south, fold, before, after), left
+
+
+def spread_body(pieces_ref, out_ref):
+    summed = jnp.sum(pieces_ref[...].astype(F32), axis=0).astype(out_ref.dtype)
+    for i in range(out_ref.shape[0]):
+        out_ref[i] = summed
+
+
+def unpack_body(scale, sums_ref, w_in_ref, w_out_ref, dw_ref, gain_ref, b_ref):
+    channels, hidden = w_in_ref.shape
+    low = channels + hidden
+    shift = hidden - 128
+    tail = sums_ref[low : low + channels, :] * scale
+    w_in_ref[...] = jnp.concatenate([sums_ref[0:channels, :] * scale, tail[:, 0:shift]], axis=1)
+    w_out_ref[...] = sums_ref[channels:low, 0:channels] * scale
+    dw_ref[...] = tail[:, shift : shift + 49]
+    turned = tail.T
+    gain_ref[...] = turned[shift + 49 : shift + 50, :]
+    parts = [turned[shift + 50 + k : shift + 51 + k, :] for k in range(hidden // channels)]
+    b_ref[...] = jnp.concatenate(parts, axis=1)
 
 
 def shards(fields, land_mask, dw_kernel, gain, w_in, b_in, w_out, cotangent):
     channels, rows, cols = fields.shape
     hidden = w_out.shape[0]
-    flip = jnp.eye(cols, dtype=BF16)[::-1]
+    n_lat, n_lon = lax.axis_size("lat"), lax.axis_size("lon")
     taps = dw_kernel.reshape(channels, 49)
-    turned = taps[:, ::-1]
-    is_top = lax.axis_index("lat") == lax.axis_size("lat") - 1
-    north = jnp.where(is_top, taps, turned)
+    is_top = (lax.axis_index("lat") == n_lat - 1).astype(jnp.int32).reshape(1)
     ring = like((RING, channels, cols), BF16)
     grid = like((rows, channels, cols), BF16)
     whole = like((channels, rows, cols), BF16)
     flat = pltpu.VMEM((cols // 128, channels * rows, 128), F32)
     ext = pltpu.VMEM((rows + 2 * RING, channels, cols + 128), F32)
     masked, first, last = call(rows_body, [grid, ring, ring], fields, land_mask, scratch=[flat])
-    south, fold, before, after = halo(masked, first, last, flip)
+    around, _ = halo(masked, first, last)
     cells = rows * cols
+    height = 2 * channels + hidden
     output, grads, first, last, sums = call(
         block_body,
-        [whole, grid, ring, ring, like((2 * channels + hidden, 128), F32)],
-        masked, south, fold, before, after, cotangent, land_mask,
-        taps, gain[:, None], w_in, w_in.T, b_in[:, None], w_out, w_out.T,
+        [whole, grid, ring, ring, like((height, 128), BF16)],
+        masked, *around, cotangent, land_mask,
+        taps, gain.reshape(1, channels), w_in, b_in.reshape(1, hidden), w_out,
         scratch=[
             ext,
             pltpu.VMEM((rows, channels, cols), F32),
@@ -360,26 +385,40 @@
             pltpu.VMEM((hidden, cells), BF16),
             pltpu.VMEM((hidden, 128), F32),
             pltpu.VMEM((channels, 128), F32),
+            pltpu.VMEM((channels, 128), F32),
         ],
     )
-    south, fold, before, after = halo(grads, first, last, flip)
+    size = height // n_lat
+    around, strip = halo(grads, first, last)
+    pieces = lax.all_to_all(sums.reshape(n_lat, size, 128), "lat", 0, 0, tiled=True)
+    (pieces,) = call(spread_body, [like((n_lon, size, 128), BF16)], pieces, waits=[strip])
+    pieces = lax.all_to_all(pieces, "lon", 0, 0, tiled=True)
+    (pieces,) = call(spread_body, [like((n_lat, size, 128), F32)], pieces, waits=around[2:])
+    pieces = lax.all_to_all(pieces, "lat", 0, 0, tiled=True)
     (input_grad,) = call(
-        back_body, [whole], grads, south, fold, before, after, cotangent, land_mask, turned, north,
-        scratch=[ext, flat],
-    )
-    scale = float(cells * lax.axis_size("lat") * lax.axis_size("lon")) ** -0.5
-    sums = total(sums) * scale
-    low = channels + hidden
-    shift = hidden - 128
-    tail = sums[low:, shift:]
+        back_body, [whole], grads, *around, cotangent, land_mask, taps, is_top,
+        scratch=[ext, flat], smem=1,
+    )
+    scale = float(cells * n_lat * n_lon) ** -0.5
+    w_in_grad, w_out_grad, dw_grad, gain_grad, b_grad = call(
+        functools.partial(unpack_body, scale),
+        [
+            like((channels, hidden), F32),
+            like((hidden, channels), F32),
+            like((channels, 49), F32),
+            like((1, channels), F32),
+            like((1, hidden), F32),
+        ],
+        pieces.reshape(height, 128),
+    )
     return (
         output,
         input_grad,
-        tail[:, :49].reshape(channels, 7, 7),
-        tail[:, 49],
-        jnp.concatenate([sums[:channels], sums[low:, :shift]], axis=1),
-        tail[:, 50 : 50 + hidden // channels].T.reshape(hidden),
-        sums[channels:low, :channels],
+        dw_grad.reshape(channels, 7, 7),
+        gain_grad.reshape(channels),
+        w_in_grad,
+        b_grad.reshape(hidden),
+        w_out_grad,
     )
 
 

time: 136 us -> 128 us (0.941)
  the two profiles are of different devices: /device:TPU:15 before, /device:TPU:1 now
where the time goes in v2:
time: 128 us; the launch traced here: 126 us
  starting transfers between devices  59.1 us (46%)
  Pallas kernels  39.5 us (31%)
  waiting for transfers between devices  20 us (16%)
  local copies, waits for them, and re-layouts  6.16 us (5%)
    pallas_call x8, Pallas kernels, call(): pl.pallas_call(run, out_shape=outs, in_specs=specs, out_specs=[pl.BlockSp...  39.5 us
    all_to_all x1, starting transfers between devices, shards(): lax.all_to_all(sums.reshape(n_lat, size, 128), 'lat', 0, 0, tiled=True)  14.7 us
    all_to_all x1, starting transfers between devices, shards(): pieces = lax.all_to_all(pieces, 'lon', 0, 0, tiled=True)  11.1 us
    ppermute x2, waiting for transfers between devices, lat_halo(): north = lax.ppermute(first, 'lat', [(i + 1, i) for i in range(n_lat - 1)])  8.8 us
    ppermute x2, starting transfers between devices, lon_halo(): lax.ppermute(right, 'lon', [(i, (i + 1) % n_lon) for i in range(n_lon)])  8.8 us
    ppermute x2, starting transfers between devices, lat_halo(): south = lax.ppermute(last, 'lat', [(i, i + 1) for i in range(n_lat - 1)])  8.09 us
    all_to_all x1, starting transfers between devices, shards(): pieces = lax.all_to_all(pieces, 'lat', 0, 0, tiled=True)  7.47 us
    ppermute x2, waiting for transfers between devices, lon_halo(): lax.ppermute(left, 'lon', [(i, (i - 1) % n_lon) for i in range(n_lon)])  5.05 us
  transfers between devices with their start and end apart: 13, of which 8 were waited for; matrix products, arithmetic and copies ran while one was open for 1% of the time, Pallas kernels for 8%

profile of v2, /device:TPU:1, one launch (start us, length us, event | category | flops | bytes accessed | tf_op | source)
XLA Modules:
  0.0 125.6 jit_solution(9317805978854798904)
XLA Ops:
  0.6 2.0 %shard_map.135 = (bf16[8,96,256]{2,1,0:T(8,128)(2,1)}, bf16[3,96,256]{2,1,0:T(8,128)(2,1)}, bf16[3,96,256]{2,1,0:T(8,128)(2,1)}) custom-call(bf16[96,8,256]{2,1,0:T(8,128)(2,1)} %refs_0_.1, s32[8,256]{1,0:T(8,128)} %refs_6_.3), custom_call_target="tpu_custom_call" | custom-call | tf_op jit(solution)/shard_map/pallas_call | solution.py:25
  2.6 4.8 %collective-permute-start = (bf16[3,96,256]{2,1,0:T(8,128)(2,1)}, bf16[3,96,256]{2,1,0:T(8,128)(2,1)S(1)}, u32[]{:S(2)}, u32[]{:S(2)}) collective-permute-start(bf16[3,96,256]{2,1,0:T(8,128)(2,1)} %get-tuple-element.27), channel_id=1, source_target_pairs={{0,1},{1,2},{2,3},{3,4},{4,5},{5,6},{6,7},{7,8},{8,9},{9,10},{10,1... | collective-permute-start | bytes 442376 | tf_op jit(solution)/shard_map/ppermute | solution.py:310
  7.4 0.7 collective-permute-start.2
  8.1 1.3 %collective-permute-start.1 = (bf16[3,96,256]{2,1,0:T(8,128)(2,1)}, bf16[3,96,256]{2,1,0:T(8,128)(2,1)S(1)}, u32[]{:S(2)}, u32[]{:S(2)}) collective-permute-start(bf16[3,96,256]{2,1,0:T(8,128)(2,1)} %get-tuple-element.28), channel_id=1, source_target_pairs={{1,0},{2,1},{3,2},{4,3},{5,4},{6,5},{7,6},{8,7},{9,8},{10,9},{11,1... | collective-permute-start | bytes 442376 | tf_op jit(solution)/shard_map/ppermute | solution.py:311
  9.4 0.4 collective-permute-done.refs_1_
  9.8 0.0 copy-start.3
  9.8 0.0 collective-permute-done.2.refs_3_
  9.8 0.0 copy-start.5
  9.8 4.4 %collective-permute-done.1.refs_2_ = bf16[3,96,256]{2,1,0:T(8,128)(2,1)S(1)} collective-permute-done((bf16[3,96,256]{2,1,0:T(8,128)(2,1)}, bf16[3,96,256]{2,1,0:T(8,128)(2,1)S(1)}, u32[]{:S(2)}, u32[]{:S(2)}) %collective-permute-start.1) | collective-permute-done | bytes 147488 | tf_op jit(solution)/shard_map/ppermute | solution.py:311
  14.2 0.0 copy-start.7
  14.2 0.0 copy-done.3
  14.2 0.0 copy-done.5
  14.2 0.7 copy-done.7
  14.9 0.0 copy-start.11
  14.9 2.1 %shard_map.136 = (bf16[3,96,256]{2,1,0:T(8,128)(2,1)}, bf16[96,128]{1,0:T(8,128)(2,1)}, bf16[96,128]{1,0:T(8,128)(2,1)}) custom-call(bf16[8,96,256]{2,1,0:T(8,128)(2,1)} %get-tuple-element.26.refs_0_, bf16[3,96,256]{2,1,0:T(8,128)(2,1)} %copy-done.3, bf16[3,96,256]{2,1,0:T(8,128)(2,1)} %copy-done.7, bf16[3,96,256]{2,1,0:T(8,128)(2,1)} %copy-done.5), custom_call_target="tpu_custom_call" | custom-call | tf_op jit(solution)/shard_map/pallas_call | solution.py:25
  17.0 5.3 %collective-permute-start.3 = (bf16[96,128]{1,0:T(8,128)(2,1)}, bf16[96,128]{1,0:T(8,128)(2,1)S(1)}, u32[]{:S(2)}, u32[]{:S(2)}) collective-permute-start(bf16[96,128]{1,0:T(8,128)(2,1)} %get-tuple-element.30), channel_id=1, source_target_pairs={{0,16},{16,32},{32,48},{48,64},{64,80},{80,96},{96,112},{112,128},... | collective-permute-start | bytes 73736 | tf_op jit(solution)/shard_map/ppermute | solution.py:317
  22.2 3.0 %collective-permute-start.4 = (bf16[96,128]{1,0:T(8,128)(2,1)}, bf16[96,128]{1,0:T(8,128)(2,1)S(1)}, u32[]{:S(2)}, u32[]{:S(2)}) collective-permute-start(bf16[96,128]{1,0:T(8,128)(2,1)} %get-tuple-element.31), channel_id=1, source_target_pairs={{0,496},{16,0},{32,16},{48,32},{64,48},{80,64},{96,80},{112,96},{1... | collective-permute-start | bytes 73736 | tf_op jit(solution)/shard_map/ppermute | solution.py:318
  25.3 0.0 copy-done.11
  25.3 0.7 copy.17.refs_7_
  26.0 0.0 collective-permute-done.3.refs_3_
  26.0 0.0 copy-start.13
  26.0 1.6 %collective-permute-done.4.refs_4_ = bf16[96,128]{1,0:T(8,128)(2,1)S(1)} collective-permute-done((bf16[96,128]{1,0:T(8,128)(2,1)}, bf16[96,128]{1,0:T(8,128)(2,1)S(1)}, u32[]{:S(2)}, u32[]{:S(2)}) %collective-permute-start.4) | collective-permute-done | bytes 24608 | tf_op jit(solution)/shard_map/ppermute | solution.py:318
  27.6 0.0 copy-start.14
  27.6 0.0 copy-done.13
  27.6 0.6 copy-done.14
  28.2 20.6 %shard_map.137 = (bf16[96,8,256]{2,1,0:T(8,128)(2,1)}, bf16[8,96,256]{2,1,0:T(8,128)(2,1)}, bf16[3,96,256]{2,1,0:T(8,128)(2,1)}, bf16[3,96,256]{2,1,0:T(8,128)(2,1)}, bf16[384,128]{1,0:T(8,128)(2,1)}) custom-call(bf16[8,96,256]{2,1,0:T(8,128)(2,1)} %get-tuple-element.26.refs_0_, bf16[3,96,256]{2,1,0:T(8,128)(2,1)} %copy-done.3, ...), custom_call_target="tpu_custom_call" | custom-call | tf_op jit(solution)/shard_map/pallas_call | solution.py:25
  48.8 0.0 copy-start.15
  48.8 14.7 %all-to-all-start = ((bf16[16,24,128]{2,1,0:T(8,128)(2,1)}), bf16[16,24,128]{2,1,0:T(8,128)(2,1)S(1)}, u32[]{:S(2)}, u32[]{:S(2)}) async-start(bf16[16,24,128]{2,1,0:T(8,128)(2,1)} %bitcast.12), calls=%async_computation | async-start | bytes 196608 | tf_op jit(solution)/shard_map/all_to_all | solution.py:393
  63.6 3.3 %collective-permute-start.5 = (bf16[3,96,256]{2,1,0:T(8,128)(2,1)}, bf16[3,96,256]{2,1,0:T(8,128)(2,1)S(1)}, u32[]{:S(2)}, u32[]{:S(2)}) collective-permute-start(bf16[3,96,256]{2,1,0:T(8,128)(2,1)} %get-tuple-element.34), channel_id=1, source_target_pairs={{0,1},{1,2},{2,3},{3,4},{4,5},{5,6},{6,7},{7,8},{8,9},{9,10},{10,1... | collective-permute-start | bytes 442376 | tf_op jit(solution)/shard_map/ppermute | solution.py:310
  66.9 0.7 collective-permute-start.7
  67.5 0.0 copy-done.15
  67.5 1.3 %collective-permute-start.6 = (bf16[3,96,256]{2,1,0:T(8,128)(2,1)S(1)}, bf16[3,96,256]{2,1,0:T(8,128)(2,1)S(1)}, u32[]{:S(2)}, u32[]{:S(2)}) collective-permute-start(bf16[3,96,256]{2,1,0:T(8,128)(2,1)S(1)} %copy-done.15), channel_id=1, source_target_pairs={{1,0},{2,1},{3,2},{4,3},{5,4},{6,5},{7,6},{8,7},{9,8},{10,9},{11,1... | collective-permute-start | bytes 442376 | tf_op jit(solution)/shard_map/ppermute | solution.py:311
  68.8 0.6 collective-permute-done.5.refs_1_
  69.5 0.0 copy-start.2
  69.5 0.0 collective-permute-done.7.refs_3_
  69.5 0.0 copy-start.6
  69.5 4.4 %collective-permute-done.6.refs_2_ = bf16[3,96,256]{2,1,0:T(8,128)(2,1)S(1)} collective-permute-done((bf16[3,96,256]{2,1,0:T(8,128)(2,1)S(1)}, bf16[3,96,256]{2,1,0:T(8,128)(2,1)S(1)}, u32[]{:S(2)}, u32[]{:S(2)}) %collective-permute-start.6) | collective-permute-done | bytes 147488 | tf_op jit(solution)/shard_map/ppermute | solution.py:311
  73.9 0.0 copy-done.2
  73.9 0.0 copy-done.6
  73.9 0.7 copy-done.8
  74.6 2.1 %shard_map.138 = (bf16[3,96,256]{2,1,0:T(8,128)(2,1)}, bf16[96,128]{1,0:T(8,128)(2,1)}, bf16[96,128]{1,0:T(8,128)(2,1)}) custom-call(bf16[8,96,256]{2,1,0:T(8,128)(2,1)} %get-tuple-element.33.refs_0_, bf16[3,96,256]{2,1,0:T(8,128)(2,1)} %copy-done.2, bf16[3,96,256]{2,1,0:T(8,128)(2,1)} %copy-done.8, bf16[3,96,256]{2,1,0:T(8,128)(2,1)} %copy-done.6), custom_call_target="tpu_custom_call" | custom-call | tf_op jit(solution)/shard_map/pallas_call | solution.py:25
  76.7 0.0 all-to-all-done.refs_0_
  76.7 0.6 copy-done.4
  77.3 1.6 %shard_map.140 = bf16[32,24,128]{2,1,0:T(8,128)(2,1)} custom-call(bf16[16,24,128]{2,1,0:T(8,128)(2,1)} %copy-done.4, bf16[96,128]{1,0:T(8,128)(2,1)} %get-tuple-element.38.refs_1_), custom_call_target="tpu_custom_call" | custom-call | tf_op jit(solution)/shard_map/pallas_call | solution.py:25
  78.9 11.1 %all-to-all-start.1 = ((bf16[32,24,128]{2,1,0:T(8,128)(2,1)}), bf16[32,24,128]{2,1,0:T(8,128)(2,1)S(1)}, u32[]{:S(2)}, u32[]{:S(2)}) async-start(bf16[32,24,128]{2,1,0:T(8,128)(2,1)} %shard_map.140), calls=%async_computation.1 | async-start | bytes 393216 | tf_op jit(solution)/shard_map/all_to_all | solution.py:395
  90.0 0.0 copy-done.16
  90.1 3.5 %collective-permute-start.8 = (bf16[96,128]{1,0:T(8,128)(2,1)S(1)}, bf16[96,128]{1,0:T(8,128)(2,1)S(1)}, u32[]{:S(2)}, u32[]{:S(2)}) collective-permute-start(bf16[96,128]{1,0:T(8,128)(2,1)S(1)} %copy-done.16), channel_id=1, source_target_pairs={{0,16},{16,32},{32,48},{48,64},{64,80},{80,96},{96,112},{112,128},... | collective-permute-start | bytes 73736 | tf_op jit(solution)/shard_map/ppermute | solution.py:317
  93.6 0.0 copy-done.12
  93.6 1.9 %collective-permute-start.9 = (bf16[96,128]{1,0:T(8,128)(2,1)S(1)}, bf16[96,128]{1,0:T(8,128)(2,1)S(1)}, u32[]{:S(2)}, u32[]{:S(2)}) collective-permute-start(bf16[96,128]{1,0:T(8,128)(2,1)S(1)} %copy-done.12), channel_id=1, source_target_pairs={{0,496},{16,0},{32,16},{48,32},{64,48},{80,64},{96,80},{112,96},{1... | collective-permute-start | bytes 73736 | tf_op jit(solution)/shard_map/ppermute | solution.py:318
  95.5 0.0 collective-permute-done.8.refs_3_.refs_1_
  95.6 0.0 copy-start.9
  95.6 3.5 %collective-permute-done.9.refs_4_.refs_2_ = bf16[96,128]{1,0:T(8,128)(2,1)S(1)} collective-permute-done((bf16[96,128]{1,0:T(8,128)(2,1)S(1)}, bf16[96,128]{1,0:T(8,128)(2,1)S(1)}, u32[]{:S(2)}, u32[]{:S(2)}) %collective-permute-start.9) | collective-permute-done | bytes 24608 | tf_op jit(solution)/shard_map/ppermute | solution.py:318
  99.1 3.6 %all-to-all-done.1.refs_0_ = bf16[32,24,128]{2,1,0:T(8,128)(2,1)S(1)} async-done(((bf16[32,24,128]{2,1,0:T(8,128)(2,1)}), bf16[32,24,128]{2,1,0:T(8,128)(2,1)S(1)}, u32[]{:S(2)}, u32[]{:S(2)}) %all-to-all-start.1) | async-done | bytes 196640 | tf_op jit(solution)/shard_map/all_to_all | solution.py:395
  102.6 0.0 copy-done.9
  102.6 0.0 copy-done.10
  102.6 0.7 copy-done
  103.3 1.7 %shard_map.141 = f32[16,24,128]{2,1,0:T(8,128)} custom-call(bf16[32,24,128]{2,1,0:T(8,128)(2,1)} %copy-done, bf16[96,128]{1,0:T(8,128)(2,1)} %copy-done.9, bf16[96,128]{1,0:T(8,128)(2,1)} %copy-done.10), custom_call_target="tpu_custom_call" | custom-call | tf_op jit(solution)/shard_map/pallas_call | solution.py:25
  105.0 7.5 %all-to-all-start.2 = ((f32[16,24,128]{2,1,0:T(8,128)}), f32[16,24,128]{2,1,0:T(8,128)S(1)}, u32[]{:S(2)}, u32[]{:S(2)}) async-start(f32[16,24,128]{2,1,0:T(8,128)} %shard_map.141), calls=%async_computation.2 | async-start | bytes 393216 | tf_op jit(solution)/shard_map/all_to_all | solution.py:397
  112.5 7.8 %shard_map.139 = bf16[96,8,256]{2,1,0:T(8,128)(2,1)} custom-call(bf16[8,96,256]{2,1,0:T(8,128)(2,1)} %get-tuple-element.33.refs_0_, bf16[3,96,256]{2,1,0:T(8,128)(2,1)} %copy-done.2, bf16[3,96,256]{2,1,0:T(8,128)(2,1)} %get-tuple-element.36.refs_2_, bf16[96,128]{1,0:T(8,128)(2,1)} %copy-done.9, bf16[96,128]{1,0:T(8,128)(2,1)} %copy-done.10, ...), custom_call_target="tpu_custom_call" | custom-call | tf_op jit(solution)/shard_map/pallas_call | solution.py:25
  120.2 1.5 %all-to-all-done.2 = f32[16,24,128]{2,1,0:T(8,128)S(1)} async-done(((f32[16,24,128]{2,1,0:T(8,128)}), f32[16,24,128]{2,1,0:T(8,128)S(1)}, u32[]{:S(2)}, u32[]{:S(2)}) %all-to-all-start.2) | async-done | bytes 196640 | tf_op jit(solution)/shard_map/all_to_all | solution.py:397
  121.7 0.7 copy-done.1
  122.4 1.7 %shard_map.142 = (f32[96,192]{1,0:T(8,128)}, f32[192,96]{1,0:T(8,128)}, f32[96,49]{1,0:T(8,128)}, f32[1,96]{1,0:T(1,128)}, f32[1,192]{1,0:T(1,128)}) custom-call(f32[384,128]{1,0:T(8,128)} %bitcast.11), custom_call_target="tpu_custom_call" | custom-call | tf_op jit(solution)/shard_map/pallas_call | solution.py:25
  124.1 0.9 copy.19
  125.0 0.6 reshape.50
  (8 shorter events, 0.0 us)
Async XLA Ops:
  2.6 7.2 %collective-permute-start = (bf16[3,96,256]{2,1,0:T(8,128)(2,1)}, bf16[3,96,256]{2,1,0:T(8,128)(2,1)S(1)}, u32[]{:S(2)}, u32[]{:S(2)}) collective-permute-start(bf16[3,96,256]{2,1,0:T(8,128)(2,1)} %get-tuple-element.27), channel_id=1, source_target_pairs={{0,1},{1,2},{2,3},{3,4},{4,5},{5,6},{6,7},{7,8},{8,9},{9,10},{10,1... | collective-permute-start | bytes 442376 | tf_op jit(solution)/shard_map/ppermute | solution.py:310
  7.4 2.4 %collective-permute-start.2 = (bf16[3,96,256]{2,1,0:T(8,128)(2,1)}, bf16[3,96,256]{2,1,0:T(8,128)(2,1)S(1)}, u32[]{:S(2)}, u32[]{:S(2)}) collective-permute-start(bf16[3,96,256]{2,1,0:T(8,128)(2,1)} %get-tuple-element.27), channel_id=1, source_target_pairs={{15,511},{31,495},{47,479},{63,463},{79,447},{95,431},{111,415},{1... | collective-permute-start | bytes 442376 | tf_op jit(solution)/shard_map/ppermute | solution.py:309
  8.1 6.1 %collective-permute-start.1 = (bf16[3,96,256]{2,1,0:T(8,128)(2,1)}, bf16[3,96,256]{2,1,0:T(8,128)(2,1)S(1)}, u32[]{:S(2)}, u32[]{:S(2)}) collective-permute-start(bf16[3,96,256]{2,1,0:T(8,128)(2,1)} %get-tuple-element.28), channel_id=1, source_target_pairs={{1,0},{2,1},{3,2},{4,3},{5,4},{6,5},{7,6},{8,7},{9,8},{10,9},{11,1... | collective-permute-start | bytes 442376 | tf_op jit(solution)/shard_map/ppermute | solution.py:311
  9.8 4.4 %copy-start.3 = (bf16[3,96,256]{2,1,0:T(8,128)(2,1)}, bf16[3,96,256]{2,1,0:T(8,128)(2,1)S(1)}, u32[]{:S(2)}) copy-start(bf16[3,96,256]{2,1,0:T(8,128)(2,1)S(1)} %collective-permute-done.refs_1_) | copy-start | bytes 442372
  9.8 4.4 %copy-start.5 = (bf16[3,96,256]{2,1,0:T(8,128)(2,1)}, bf16[3,96,256]{2,1,0:T(8,128)(2,1)S(1)}, u32[]{:S(2)}) copy-start(bf16[3,96,256]{2,1,0:T(8,128)(2,1)S(1)} %collective-permute-done.2.refs_3_) | copy-start | bytes 442372
  14.2 0.7 copy-start.7
  14.9 10.4 %copy-start.11 = (f32[96,7,7]{0,2,1:T(8,128)S(1)}, f32[96,7,7]{0,2,1:T(8,128)}, u32[]{:S(2)}) copy-start(f32[96,7,7]{0,2,1:T(8,128)} %param.10) | copy-start | bytes 56452
  17.0 9.1 %collective-permute-start.3 = (bf16[96,128]{1,0:T(8,128)(2,1)}, bf16[96,128]{1,0:T(8,128)(2,1)S(1)}, u32[]{:S(2)}, u32[]{:S(2)}) collective-permute-start(bf16[96,128]{1,0:T(8,128)(2,1)} %get-tuple-element.30), channel_id=1, source_target_pairs={{0,16},{16,32},{32,48},{48,64},{64,80},{80,96},{96,112},{112,128},... | collective-permute-start | bytes 73736 | tf_op jit(solution)/shard_map/ppermute | solution.py:317
  22.2 5.4 %collective-permute-start.4 = (bf16[96,128]{1,0:T(8,128)(2,1)}, bf16[96,128]{1,0:T(8,128)(2,1)S(1)}, u32[]{:S(2)}, u32[]{:S(2)}) collective-permute-start(bf16[96,128]{1,0:T(8,128)(2,1)} %get-tuple-element.31), channel_id=1, source_target_pairs={{0,496},{16,0},{32,16},{48,32},{64,48},{80,64},{96,80},{112,96},{1... | collective-permute-start | bytes 73736 | tf_op jit(solution)/shard_map/ppermute | solution.py:318
  26.0 1.6 %copy-start.13 = (bf16[96,128]{1,0:T(8,128)(2,1)}, bf16[96,128]{1,0:T(8,128)(2,1)S(1)}, u32[]{:S(2)}) copy-start(bf16[96,128]{1,0:T(8,128)(2,1)S(1)} %collective-permute-done.3.refs_3_) | copy-start | bytes 73732
  27.6 0.6 copy-start.14
  48.8 18.7 %copy-start.15 = (bf16[3,96,256]{2,1,0:T(8,128)(2,1)S(1)}, bf16[3,96,256]{2,1,0:T(8,128)(2,1)}, u32[]{:S(2)}) copy-start(bf16[3,96,256]{2,1,0:T(8,128)(2,1)} %get-tuple-element.35) | copy-start | bytes 442372
  48.8 27.8 %all-to-all-start = ((bf16[16,24,128]{2,1,0:T(8,128)(2,1)}), bf16[16,24,128]{2,1,0:T(8,128)(2,1)S(1)}, u32[]{:S(2)}, u32[]{:S(2)}) async-start(bf16[16,24,128]{2,1,0:T(8,128)(2,1)} %bitcast.12), calls=%async_computation | async-start | bytes 196608 | tf_op jit(solution)/shard_map/all_to_all | solution.py:393
  63.6 5.9 %collective-permute-start.5 = (bf16[3,96,256]{2,1,0:T(8,128)(2,1)}, bf16[3,96,256]{2,1,0:T(8,128)(2,1)S(1)}, u32[]{:S(2)}, u32[]{:S(2)}) collective-permute-start(bf16[3,96,256]{2,1,0:T(8,128)(2,1)} %get-tuple-element.34), channel_id=1, source_target_pairs={{0,1},{1,2},{2,3},{3,4},{4,5},{5,6},{6,7},{7,8},{8,9},{9,10},{10,1... | collective-permute-start | bytes 442376 | tf_op jit(solution)/shard_map/ppermute | solution.py:310
  66.9 2.6 %collective-permute-start.7 = (bf16[3,96,256]{2,1,0:T(8,128)(2,1)}, bf16[3,96,256]{2,1,0:T(8,128)(2,1)S(1)}, u32[]{:S(2)}, u32[]{:S(2)}) collective-permute-start(bf16[3,96,256]{2,1,0:T(8,128)(2,1)} %get-tuple-element.34), channel_id=1, source_target_pairs={{15,511},{31,495},{47,479},{63,463},{79,447},{95,431},{111,415},{1... | collective-permute-start | bytes 442376 | tf_op jit(solution)/shard_map/ppermute | solution.py:309
  67.5 6.4 %collective-permute-start.6 = (bf16[3,96,256]{2,1,0:T(8,128)(2,1)S(1)}, bf16[3,96,256]{2,1,0:T(8,128)(2,1)S(1)}, u32[]{:S(2)}, u32[]{:S(2)}) collective-permute-start(bf16[3,96,256]{2,1,0:T(8,128)(2,1)S(1)} %copy-done.15), channel_id=1, source_target_pairs={{1,0},{2,1},{3,2},{4,3},{5,4},{6,5},{7,6},{8,7},{9,8},{10,9},{11,1... | collective-permute-start | bytes 442376 | tf_op jit(solution)/shard_map/ppermute | solution.py:311
  69.5 4.4 %copy-start.2 = (bf16[3,96,256]{2,1,0:T(8,128)(2,1)}, bf16[3,96,256]{2,1,0:T(8,128)(2,1)S(1)}, u32[]{:S(2)}) copy-start(bf16[3,96,256]{2,1,0:T(8,128)(2,1)S(1)} %collective-permute-done.5.refs_1_) | copy-start | bytes 442372
  69.5 4.4 %copy-start.6 = (bf16[3,96,256]{2,1,0:T(8,128)(2,1)}, bf16[3,96,256]{2,1,0:T(8,128)(2,1)S(1)}, u32[]{:S(2)}) copy-start(bf16[3,96,256]{2,1,0:T(8,128)(2,1)S(1)} %collective-permute-done.7.refs_3_) | copy-start | bytes 442372
  73.9 0.7 copy-start.8
  76.7 0.6 copy-start.4
  78.9 11.1 %copy-start.16 = (bf16[96,128]{1,0:T(8,128)(2,1)S(1)}, bf16[96,128]{1,0:T(8,128)(2,1)}, u32[]{:S(2)}) copy-start(bf16[96,128]{1,0:T(8,128)(2,1)} %get-tuple-element.37) | copy-start | bytes 73732
  78.9 14.7 %copy-start.12 = (bf16[96,128]{1,0:T(8,128)(2,1)S(1)}, bf16[96,128]{1,0:T(8,128)(2,1)}, u32[]{:S(2)}) copy-start(bf16[96,128]{1,0:T(8,128)(2,1)} %get-tuple-element.38.refs_1_) | copy-start | bytes 73732
  78.9 23.7 %all-to-all-start.1 = ((bf16[32,24,128]{2,1,0:T(8,128)(2,1)}), bf16[32,24,128]{2,1,0:T(8,128)(2,1)S(1)}, u32[]{:S(2)}, u32[]{:S(2)}) async-start(bf16[32,24,128]{2,1,0:T(8,128)(2,1)} %shard_map.140), calls=%async_computation.1 | async-start | bytes 393216 | tf_op jit(solution)/shard_map/all_to_all | solution.py:395
  90.1 5.5 %collective-permute-start.8 = (bf16[96,128]{1,0:T(8,128)(2,1)S(1)}, bf16[96,128]{1,0:T(8,128)(2,1)S(1)}, u32[]{:S(2)}, u32[]{:S(2)}) collective-permute-start(bf16[96,128]{1,0:T(8,128)(2,1)S(1)} %copy-done.16), channel_id=1, source_target_pairs={{0,16},{16,32},{32,48},{48,64},{64,80},{80,96},{96,112},{112,128},... | collective-permute-start | bytes 73736 | tf_op jit(solution)/shard_map/ppermute | solution.py:317
  93.6 5.4 %collective-permute-start.9 = (bf16[96,128]{1,0:T(8,128)(2,1)S(1)}, bf16[96,128]{1,0:T(8,128)(2,1)S(1)}, u32[]{:S(2)}, u32[]{:S(2)}) collective-permute-start(bf16[96,128]{1,0:T(8,128)(2,1)S(1)} %copy-done.12), channel_id=1, source_target_pairs={{0,496},{16,0},{32,16},{48,32},{64,48},{80,64},{96,80},{112,96},{1... | collective-permute-start | bytes 73736 | tf_op jit(solution)/shard_map/ppermute | solution.py:318
  95.6 7.1 %copy-start.9 = (bf16[96,128]{1,0:T(8,128)(2,1)}, bf16[96,128]{1,0:T(8,128)(2,1)S(1)}, u32[]{:S(2)}) copy-start(bf16[96,128]{1,0:T(8,128)(2,1)S(1)} %collective-permute-done.8.refs_3_.refs_1_) | copy-start | bytes 73732
  99.1 3.6 %copy-start.10 = (bf16[96,128]{1,0:T(8,128)(2,1)}, bf16[96,128]{1,0:T(8,128)(2,1)S(1)}, u32[]{:S(2)}) copy-start(bf16[96,128]{1,0:T(8,128)(2,1)S(1)} %collective-permute-done.9.refs_4_.refs_2_) | copy-start | bytes 73732
  102.6 0.7 copy-start
  105.0 16.7 %all-to-all-start.2 = ((f32[16,24,128]{2,1,0:T(8,128)}), f32[16,24,128]{2,1,0:T(8,128)S(1)}, u32[]{:S(2)}, u32[]{:S(2)}) async-start(f32[16,24,128]{2,1,0:T(8,128)} %shard_map.141), calls=%async_computation.2 | async-start | bytes 393216 | tf_op jit(solution)/shard_map/all_to_all | solution.py:397
  121.7 0.7 copy-start.1

commit v3 on v2

--- a/solution.py
+++ b/solution.py
@@ -9,27 +9,50 @@
 
 F32 = jnp.float32
 BF16 = jnp.bfloat16
-VMEM_LIMIT = 56 * 1024 * 1024
+VMEM_LIMIT = 48 * 1024 * 1024
 RING = 3
 
 
-def call(body, outs, *args, scratch=(), smem=0, waits=()):
-    specs = [pl.BlockSpec(memory_space=pltpu.VMEM)] * (len(args) - smem)
-    specs += [pl.BlockSpec(memory_space=pltpu.SMEM)] * smem
+def call(body, outs, args, raw=(), scalars=(), scratch=(), waits=()):
+    count = len(args)
+    end = count + len(raw) + len(scalars) + len(waits)
+    specs = [pl.BlockSpec(memory_space=pltpu.VMEM)] * count
+    specs += [pl.BlockSpec(memory_space=pltpu.HBM)] * len(raw)
+    specs += [pl.BlockSpec(memory_space=pltpu.SMEM)] * len(scalars)
     specs += [pl.BlockSpec(memory_space=pl.ANY)] * len(waits)
-    count = len(args)
+    near = [pltpu.with_memory_space_constraint(x, pltpu.VMEM) for x in args]
+    far = [pltpu.with_memory_space_constraint(x, pltpu.HBM) for x in raw]
+    slots = [pltpu.VMEM(x.shape, x.dtype) for x in raw]
 
     def run(*refs):
-        body(*refs[:count], *refs[count + len(waits) :])
-
+        first = end + len(outs)
+        made = refs[len(refs) - 1 - len(raw) : len(refs) - 1] if raw else ()
+        inner = refs[first : len(refs) - 1 - len(raw)] if raw else refs[first:]
+        rest = (*refs[count + len(raw) : end - len(waits)], *refs[end:first], *inner)
+        if not raw:
+            return body(*refs[:count], *rest)
+        copies = [
+            pltpu.make_async_copy(refs[count + i], made[i], refs[-1].at[i])
+            for i in range(len(raw))
+        ]
+        for copy in copies:
+            copy.start()
+
+        def settle():
+            for copy in copies:
+                copy.wait()
+
+        return body(settle, *refs[:count], *made, *rest)
+
+    extra = [*slots, pltpu.SemaphoreType.DMA((len(raw),))] if raw else []
     return pl.pallas_call(
         run,
         out_shape=outs,
         in_specs=specs,
         out_specs=[pl.BlockSpec(memory_space=pltpu.VMEM)] * len(outs),
-        scratch_shapes=list(scratch),
+        scratch_shapes=[*scratch, *extra],
         compiler_params=pltpu.CompilerParams(vmem_limit_bytes=VMEM_LIMIT),
-    )(*args, *waits)
+    )(*near, *far, *scalars, *waits)
 
 
 def lanes():
@@ -53,10 +76,10 @@
     return jnp.concatenate(parts, axis=1)
 
 
-def rows_body(f_ref, mask_ref, m_ref, first_ref, last_ref, flat):
+def rows_body(settle, f_ref, mask_ref, m_ref, first_ref, last_ref, flat):
     channels, rows, cols = f_ref.shape
-    sea = mask_ref[...].astype(F32)
-    spread(flat, f_ref[...].astype(F32) * sea[None])
+    settle()
+    spread(flat, f_ref[...].astype(F32) * mask_ref[...].astype(F32)[None])
     for i in range(rows):
         row = row_of(flat, i, channels, rows).astype(BF16)
         m_ref[i] = row
@@ -66,14 +89,20 @@
             last_ref[i - (rows - RING)] = row
 
 
-def strips_body(m_ref, south_ref, north_ref, mirror_ref, halo_ref, left_ref, right_ref):
-    rows, channels, cols = m_ref.shape
+def turn_body(mirror_ref, turned_ref):
+    cols = mirror_ref.shape[2]
     here = lax.broadcasted_iota(jnp.int32, (cols, cols), 0)
     there = lax.broadcasted_iota(jnp.int32, (cols, cols), 1)
     flip = (here + there == cols - 1).astype(F32).astype(BF16)
     for k in range(RING):
-        turned = jnp.dot(mirror_ref[RING - 1 - k], flip, preferred_element_type=F32)
-        halo_ref[k] = (north_ref[k].astype(F32) + turned).astype(BF16)
+        row = jnp.dot(mirror_ref[RING - 1 - k], flip, preferred_element_type=F32)
+        turned_ref[k] = row.astype(BF16)
+
+
+def strips_body(m_ref, south_ref, north_ref, turned_ref, halo_ref, left_ref, right_ref):
+    rows, channels, cols = m_ref.shape
+    for k in range(RING):
+        halo_ref[k] = (north_ref[k].astype(F32) + turned_ref[k].astype(F32)).astype(BF16)
     lane = lax.broadcasted_iota(jnp.int32, (channels, 128), 1)
     left = jnp.zeros((channels, 128), F32)
     right = jnp.zeros((channels, 128), F32)
@@ -96,6 +125,13 @@
     right_ref[...] = right.astype(BF16)
 
 
+def strips_and_sums_body(
+    m_ref, south_ref, north_ref, turned_ref, sums_ref, halo_ref, left_ref, right_ref, out_ref
+):
+    strips_body(m_ref, south_ref, north_ref, turned_ref, halo_ref, left_ref, right_ref)
+    out_ref[...] = sums_ref[...]
+
+
 def fill(ext, m_ref, south_ref, halo_ref, before_ref, after_ref):
     rows, channels, cols = m_ref.shape
     lane = lax.broadcasted_iota(jnp.int32, (channels, 128), 1)
@@ -127,6 +163,12 @@
     turned = [pltpu.roll(t, -step, 1) for t in tiles]
     keep = lane >= -step
     return [jnp.where(keep, turned[t], turned[t - 1]) for t in range(count - 1)]
+
+
+def tap_columns(dw_ref):
+    rows = jnp.concatenate([dw_ref[a] for a in range(7)], axis=0)
+    blank = jnp.zeros((128 - rows.shape[0], rows.shape[1]), F32)
+    return jnp.concatenate([rows, blank], axis=0).T
 
 
 def tap(weights, index):
@@ -157,15 +199,18 @@
 
 
 def block_body(
-    m_ref, south_ref, halo_ref, before_ref, after_ref, ct_ref, mask_ref,
+    settle, m_ref, south_ref, halo_ref, before_ref, after_ref, ct_ref, mask_ref,
     dw_ref, gain_ref, w_in_ref, b_ref, w_out_ref,
-    out_ref, g_ref, first_ref, last_ref, sums_ref,
-    ext, conv, flat, act, back, sca, pre, b_acc, gain_acc, tail,
+    out_ref, g_ref, first_ref, last_ref, wide_ref, tail_ref, ext_ref,
+    conv, flat, act, back, sca, pre, b_acc, gain_acc, taps,
 ):
+    ext = ext_ref
     rows, channels, cols = m_ref.shape
     hidden = w_out_ref.shape[0]
     pairs = cols // 128
     fill(ext, m_ref, south_ref, halo_ref, before_ref, after_ref)
+    settle()
+    taps[...] = tap_columns(dw_ref)
     sea = mask_ref[...].astype(F32)
     spread(flat, ct_ref[...].astype(F32) * sea[None])
     for i in range(rows):
@@ -174,7 +219,7 @@
     def conv_step(ct, carry):
         c0 = pl.multiple_of(ct * 8, 8)
         lane = lanes()
-        summed = correlate(ext, c0, rows, pairs, lane, dw_ref[pl.ds(c0, 8), :], None)
+        summed = correlate(ext, c0, rows, pairs, lane, taps[pl.ds(c0, 8), :], None)
         for i in range(rows):
             for t in range(pairs):
                 conv[i, pl.ds(c0, 8), t * 128 : t * 128 + 128] = summed[i][t]
@@ -224,7 +269,6 @@
             - jnp.mean(norm_grad, axis=0, keepdims=True)
             - normed * jnp.mean(norm_grad * normed, axis=0, keepdims=True)
         )
-        conv[i] = grad
         short = grad.astype(BF16)
         g_ref[i] = short
         if i < RING:
@@ -238,18 +282,30 @@
     w_out_sum = lax.dot_general(act[...], back[...], over_cells, preferred_element_type=F32)
     low = channels + hidden
     shift = hidden - 128
-    sums_ref[0:channels, :] = w_in_sum[:, 0:128].astype(BF16)
+    wide_ref[0:channels, :] = w_in_sum[:, 0:128].astype(BF16)
     blank = jnp.zeros((hidden, 128 - channels), F32)
-    sums_ref[channels:low, :] = jnp.concatenate([w_out_sum, blank], axis=1).astype(BF16)
+    wide_ref[channels:low, :] = jnp.concatenate([w_out_sum, blank], axis=1).astype(BF16)
     blank = jnp.zeros((channels, 128 - shift), F32)
-    tail[...] = jnp.concatenate([w_in_sum[:, 128:hidden], blank], axis=1)
+    tail = jnp.concatenate([w_in_sum[:, 128:hidden], blank], axis=1)
+    lane = lax.broadcasted_iota(jnp.int32, (channels, 128), 1)
+    tail = jnp.where(lane == shift + 49, jnp.sum(gain_acc[...], axis=1, keepdims=True), tail)
+    for part in range(hidden // channels):
+        column = jnp.sum(b_acc[part * channels : part * channels + channels, :], axis=1, keepdims=True)
+        tail = jnp.where(lane == shift + 50 + part, column, tail)
+    tail_ref[...] = tail
+
+
+def kernel_body(shift, ext, g_ref, wide_ref, tail_ref, sums_ref, tail, grid):
+    rows, channels, cols = g_ref.shape
+    pairs = cols // 128
+    grid[...] = g_ref[...].astype(F32)
 
     def kernel_step(ct, carry):
         c0 = pl.multiple_of(ct * 8, 8)
         lane = lanes()
-        tile = tail[pl.ds(c0, 8), :]
+        tile = tail_ref[pl.ds(c0, 8), :]
         grads = [
-            [conv[i, pl.ds(c0, 8), t * 128 : t * 128 + 128] for t in range(pairs)]
+            [grid[i, pl.ds(c0, 8), t * 128 : t * 128 + 128] for t in range(pairs)]
             for i in range(rows)
         ]
         for b in range(7):
@@ -266,32 +322,30 @@
             for a in range(7):
                 total = jnp.sum(summed[a], axis=1, keepdims=True)
                 tile = jnp.where(lane == shift + a * 7 + b, total, tile)
-        total = jnp.sum(gain_acc[pl.ds(c0, 8), :], axis=1, keepdims=True)
-        tile = jnp.where(lane == shift + 49, total, tile)
-        for part in range(hidden // channels):
-            start = pl.multiple_of(part * channels + c0, 8)
-            total = jnp.sum(b_acc[pl.ds(start, 8), :], axis=1, keepdims=True)
-            tile = jnp.where(lane == shift + 50 + part, total, tile)
         tail[pl.ds(c0, 8), :] = tile
         return carry
 
     lax.fori_loop(0, channels // 8, kernel_step, 0)
+    low = wide_ref.shape[0]
+    sums_ref[0:low, :] = wide_ref[...]
     sums_ref[low : low + channels, :] = tail[...].astype(BF16)
 
 
 def back_body(
-    g_ref, south_ref, halo_ref, before_ref, after_ref, ct_ref, mask_ref, dw_ref, top_ref,
-    out_ref, ext, flat,
+    settle, g_ref, south_ref, halo_ref, before_ref, after_ref, ct_ref, mask_ref, dw_ref, top_ref,
+    out_ref, ext, flat, taps,
 ):
     rows, channels, cols = g_ref.shape
     pairs = cols // 128
     fill(ext, g_ref, south_ref, halo_ref, before_ref, after_ref)
+    settle()
+    taps[...] = tap_columns(dw_ref)
 
     def step(ct, carry):
         c0 = pl.multiple_of(ct * 8, 8)
         lane = lanes()
         top = jnp.broadcast_to(top_ref[0], (8, 128)) > 0
-        summed = correlate(ext, c0, rows, pairs, lane, dw_ref[pl.ds(c0, 8), :], top)
+        summed = correlate(ext, c0, rows, pairs, lane, taps[pl.ds(c0, 8), :], top)
         for i in range(rows):
             for t in range(pairs):
                 flat[t, pl.ds(c0 * rows + i, 8, stride=rows), :] = summed[i][t]
@@ -309,7 +363,8 @@
     mirror = lax.ppermute(last, ("lon", "lat"), list(zip(tops, tops[::-1])))
     south = lax.ppermute(last, "lat", [(i, i + 1) for i in range(n_lat - 1)])
     north = lax.ppermute(first, "lat", [(i + 1, i) for i in range(n_lat - 1)])
-    return south, north, mirror
+    (turned,) = call(turn_body, [pltpu.VMEM(last.shape, last.dtype)], [mirror])
+    return south, north, turned
 
 
 def lon_halo(left, right):
@@ -319,20 +374,12 @@
     return before, after
 
 
+def held(struct):
+    return pltpu.VMEM(struct.shape, struct.dtype)
+
+
 def like(shape, dtype):
     return jax.ShapeDtypeStruct(shape, dtype)
-
-
-def halo(rows_of, first, last):
-    rows, channels, cols = rows_of.shape
-    south, north, mirror = lat_halo(first, last)
-    strip = like((channels, 128), BF16)
-    fold, left, right = call(
-        strips_body, [like((RING, channels, cols), BF16), strip, strip],
-        rows_of, south, north, mirror,
-    )
-    before, after = lon_halo(left, right)
-    return (south, fold, before, after), left
 
 
 def spread_body(pieces_ref, out_ref):
@@ -348,8 +395,9 @@
     tail = sums_ref[low : low + channels, :] * scale
     w_in_ref[...] = jnp.concatenate([sums_ref[0:channels, :] * scale, tail[:, 0:shift]], axis=1)
     w_out_ref[...] = sums_ref[channels:low, 0:channels] * scale
-    dw_ref[...] = tail[:, shift : shift + 49]
     turned = tail.T
+    for a in range(7):
+        dw_ref[a] = turned[shift + 7 * a : shift + 7 * a + 7, :]
     gain_ref[...] = turned[shift + 49 : shift + 50, :]
     parts = [turned[shift + 50 + k : shift + 51 + k, :] for k in range(hidden // channels)]
     b_ref[...] = jnp.concatenate(parts, axis=1)
@@ -359,24 +407,39 @@
     channels, rows, cols = fields.shape
     hidden = w_out.shape[0]
     n_lat, n_lon = lax.axis_size("lat"), lax.axis_size("lon")
-    taps = dw_kernel.reshape(channels, 49)
+    taps = dw_kernel.transpose(1, 2, 0)
     is_top = (lax.axis_index("lat") == n_lat - 1).astype(jnp.int32).reshape(1)
     ring = like((RING, channels, cols), BF16)
     grid = like((rows, channels, cols), BF16)
     whole = like((channels, rows, cols), BF16)
     flat = pltpu.VMEM((cols // 128, channels * rows, 128), F32)
     ext = pltpu.VMEM((rows + 2 * RING, channels, cols + 128), F32)
-    masked, first, last = call(rows_body, [grid, ring, ring], fields, land_mask, scratch=[flat])
-    around, _ = halo(masked, first, last)
+    near_ring = held(ring)
+    strip = pltpu.VMEM((channels, 128), BF16)
+    height = 2 * channels + hidden
+    near_sums = pltpu.VMEM((height, 128), BF16)
     cells = rows * cols
-    height = 2 * channels + hidden
-    output, grads, first, last, sums = call(
+    masked, first, last = call(
+        rows_body, [held(grid), near_ring, near_ring], [], [fields, land_mask], scratch=[flat]
+    )
+    south, north, turned = lat_halo(first, last)
+    fold, left, right = call(
+        strips_body, [near_ring, strip, strip], [masked, south, north, turned]
+    )
+    before, after = lon_halo(left, right)
+    columns = pltpu.VMEM((channels, 128), F32)
+    output, grads, first, last, wide, tail, ext_rows = call(
         block_body,
-        [whole, grid, ring, ring, like((height, 128), BF16)],
-        masked, *around, cotangent, land_mask,
-        taps, gain.reshape(1, channels), w_in, b_in.reshape(1, hidden), w_out,
+        [
+            whole, held(grid), near_ring, near_ring,
+            pltpu.VMEM((height - channels, 128), BF16), columns, ext,
+        ],
+        [masked, south, fold, before, after],
+        [
+            cotangent, land_mask, taps, gain.reshape(1, channels), w_in,
+            b_in.reshape(1, hidden), w_out,
+        ],
         scratch=[
-            ext,
             pltpu.VMEM((rows, channels, cols), F32),
             flat,
             pltpu.VMEM((hidden, cells), BF16),
@@ -384,20 +447,31 @@
             pltpu.VMEM((channels, cells), BF16),
             pltpu.VMEM((hidden, cells), BF16),
             pltpu.VMEM((hidden, 128), F32),
-            pltpu.VMEM((channels, 128), F32),
-            pltpu.VMEM((channels, 128), F32),
+            columns,
+            columns,
         ],
     )
+    south, north, turned = lat_halo(first, last)
+    (sums,) = call(
+        functools.partial(kernel_body, hidden - 128), [near_sums], [ext_rows, grads, wide, tail],
+        scratch=[columns, pltpu.VMEM((rows, channels, cols), F32)],
+    )
+    fold, left, right, sums = call(
+        strips_and_sums_body, [near_ring, strip, strip, near_sums],
+        [grads, south, north, turned, sums],
+    )
+    before, after = lon_halo(left, right)
     size = height // n_lat
-    around, strip = halo(grads, first, last)
     pieces = lax.all_to_all(sums.reshape(n_lat, size, 128), "lat", 0, 0, tiled=True)
-    (pieces,) = call(spread_body, [like((n_lon, size, 128), BF16)], pieces, waits=[strip])
+    (pieces,) = call(
+        spread_body, [pltpu.VMEM((n_lon, size, 128), BF16)], [pieces], waits=[before, after]
+    )
     pieces = lax.all_to_all(pieces, "lon", 0, 0, tiled=True)
-    (pieces,) = call(spread_body, [like((n_lat, size, 128), F32)], pieces, waits=around[2:])
+    (pieces,) = call(spread_body, [pltpu.VMEM((n_lat, size, 128), F32)], [pieces])
     pieces = lax.all_to_all(pieces, "lat", 0, 0, tiled=True)
     (input_grad,) = call(
-        back_body, [whole], grads, *around, cotangent, land_mask, taps, is_top,
-        scratch=[ext, flat], smem=1,
+        back_body, [whole], [grads, south, fold, before, after], [cotangent, land_mask, taps],
+        [is_top], scratch=[ext, flat, columns],
     )
     scale = float(cells * n_lat * n_lon) ** -0.5
     w_in_grad, w_out_grad, dw_grad, gain_grad, b_grad = call(
@@ -405,16 +479,16 @@
         [
             like((channels, hidden), F32),
             like((hidden, channels), F32),
-            like((channels, 49), F32),
+            like((7, 7, channels), F32),
             like((1, channels), F32),
             like((1, hidden), F32),
         ],
-        pieces.reshape(height, 128),
+        [pieces.reshape(height, 128)],
     )
     return (
         output,
         input_grad,
-        dw_grad.reshape(channels, 7, 7),
+        dw_grad.transpose(2, 0, 1),
         gain_grad.reshape(channels),
         w_in_grad,
         b_grad.reshape(hidden),

time: 128 us -> 128 us (level); the launches traced: 126 us -> 128 us
  blocking collectives: 0 us -> 26.4 us
  waiting for transfers between devices: 20 us -> 9.85 us
  Pallas kernels: 39.5 us -> 31.7 us
  local copies, waits for them, and re-layouts: 6.16 us -> 0 us
    all_to_all x0 -> x1, blocking collectives: none -> 26.4 us  [shards(): pieces = lax.all_to_all(pieces, 'lon', 0, 0, tiled=True)]
    all_to_all x1 -> x0, starting transfers between devices: 11.1 us -> none  [shards(): pieces = lax.all_to_all(pieces, 'lon', 0, 0, tiled=True)]
    pallas_call x8 -> x11, Pallas kernels: 39.5 us -> 31.7 us  [call(): pl.pallas_call(run, out_shape=outs, in_specs=specs, out_specs=[pl.BlockSp...]
    ppermute x2, starting transfers between devices: 4.96 us -> 12.6 us  [lon_halo(): lax.ppermute(left, 'lon', [(i, (i - 1) % n_lon) for i in range(n_lon)])]
    all_to_all x1, starting transfers between devices: 14.7 us -> 19.8 us  [shards(): lax.all_to_all(sums.reshape(n_lat, size, 128), 'lat', 0, 0, tiled=True)]
    ppermute x2, waiting for transfers between devices: 8.8 us -> 3.81 us  [lat_halo(): north = lax.ppermute(first, 'lat', [(i + 1, i) for i in range(n_lat - 1)])]
    unnamed x34 -> x0, local copies, waits for them, and re-layouts: 3.94 us -> none
    all_to_all x1 -> x0, waiting for transfers between devices: 3.58 us -> none  [shards(): pieces = lax.all_to_all(pieces, 'lon', 0, 0, tiled=True)]
  transfers between devices with their start and end apart: 13 -> 12, of which waited for: 8 -> 5; matrix products, arithmetic and copies ran while one was open for 1% -> 0% of each run, Pallas kernels for 8% -> 13%
where the time goes in v3:
time: 128 us
  starting transfers between devices  58.7 us (46%)
  Pallas kernels  31.7 us (25%)
  blocking collectives  26.4 us (21%)
  waiting for transfers between devices  9.85 us (8%)
    pallas_call x11, Pallas kernels, call(): pl.pallas_call(run, out_shape=outs, in_specs=specs, out_specs=[pl.BlockSp...  31.7 us
    all_to_all x1, blocking collectives, shards(): pieces = lax.all_to_all(pieces, 'lon', 0, 0, tiled=True)  26.4 us
    all_to_all x1, starting transfers between devices, shards(): lax.all_to_all(sums.reshape(n_lat, size, 128), 'lat', 0, 0, tiled=True)  19.8 us
    ppermute x2, starting transfers between devices, lon_halo(): lax.ppermute(left, 'lon', [(i, (i - 1) % n_lon) for i in range(n_lon)])  12.6 us
    ppermute x2, starting transfers between devices, lat_halo(): south = lax.ppermute(last, 'lat', [(i, i + 1) for i in range(n_lat - 1)])  8.03 us
    ppermute x2, starting transfers between devices, lon_halo(): lax.ppermute(right, 'lon', [(i, (i + 1) % n_lon) for i in range(n_lon)])  7.19 us
    all_to_all x1, starting transfers between devices, shards(): pieces = lax.all_to_all(pieces, 'lat', 0, 0, tiled=True)  7.19 us
    ppermute x2, waiting for transfers between devices, lat_halo(): north = lax.ppermute(first, 'lat', [(i + 1, i) for i in range(n_lat - 1)])  3.81 us
  transfers between devices with their start and end apart: 12, of which 5 were waited for; matrix products, arithmetic and copies ran while one was open for 0% of the time, Pallas kernels for 13%

profile of v3, /device:TPU:1, one launch (start us, length us, event | category | flops | bytes accessed | tf_op | source)
XLA Modules:
  0.0 127.6 jit_solution(8757790266452306588)
XLA Ops:
  0.6 1.2 shard_map.135
  1.9 0.7 collective-permute-start.2
  2.6 4.8 %collective-permute-start = (bf16[3,96,256]{2,1,0:T(8,128)(2,1)S(1)}, bf16[3,96,256]{2,1,0:T(8,128)(2,1)S(1)}, u32[]{:S(2)}, u32[]{:S(2)}) collective-permute-start(bf16[3,96,256]{2,1,0:T(8,128)(2,1)S(1)} %get-tuple-element.30), channel_id=1, source_target_pairs={{0,1},{1,2},{2,3},{3,4},{4,5},{5,6},{6,7},{7,8},{8,9},{9,10},{10,1... | collective-permute-start | bytes 442376 | tf_op jit(solution)/shard_map/ppermute | solution.py:364
  7.4 1.3 %collective-permute-start.1 = (bf16[3,96,256]{2,1,0:T(8,128)(2,1)S(1)}, bf16[3,96,256]{2,1,0:T(8,128)(2,1)S(1)}, u32[]{:S(2)}, u32[]{:S(2)}) collective-permute-start(bf16[3,96,256]{2,1,0:T(8,128)(2,1)S(1)} %get-tuple-element.31), channel_id=1, source_target_pairs={{1,0},{2,1},{3,2},{4,3},{5,4},{6,5},{7,6},{8,7},{9,8},{10,9},{11,1... | collective-permute-start | bytes 442376 | tf_op jit(solution)/shard_map/ppermute | solution.py:365
  8.7 0.0 collective-permute-done.2.refs_0_
  8.7 0.2 shard_map.136.refs_3_
  8.9 0.6 collective-permute-done.refs_1_
  9.5 3.8 %collective-permute-done.1.refs_2_ = bf16[3,96,256]{2,1,0:T(8,128)(2,1)S(1)} collective-permute-done((bf16[3,96,256]{2,1,0:T(8,128)(2,1)S(1)}, bf16[3,96,256]{2,1,0:T(8,128)(2,1)S(1)}, u32[]{:S(2)}, u32[]{:S(2)}) %collective-permute-start.1) | collective-permute-done | bytes 147488 | tf_op jit(solution)/shard_map/ppermute | solution.py:365
  13.3 0.2 shard_map.137
  13.5 5.3 %collective-permute-start.3 = (bf16[96,128]{1,0:T(8,128)(2,1)S(1)}, bf16[96,128]{1,0:T(8,128)(2,1)S(1)}, u32[]{:S(2)}, u32[]{:S(2)}) collective-permute-start(bf16[96,128]{1,0:T(8,128)(2,1)S(1)} %get-tuple-element.33), channel_id=1, source_target_pairs={{0,16},{16,32},{32,48},{48,64},{64,80},{80,96},{96,112},{112,128},... | collective-permute-start | bytes 73736 | tf_op jit(solution)/shard_map/ppermute | solution.py:372
  18.8 3.0 %collective-permute-start.4 = (bf16[96,128]{1,0:T(8,128)(2,1)S(1)}, bf16[96,128]{1,0:T(8,128)(2,1)S(1)}, u32[]{:S(2)}, u32[]{:S(2)}) collective-permute-start(bf16[96,128]{1,0:T(8,128)(2,1)S(1)} %get-tuple-element.34), channel_id=1, source_target_pairs={{0,496},{16,0},{32,16},{48,32},{64,48},{80,64},{96,80},{112,96},{1... | collective-permute-start | bytes 73736 | tf_op jit(solution)/shard_map/ppermute | solution.py:373
  21.9 0.0 collective-permute-done.3.refs_3_
  21.9 2.1 %collective-permute-done.4.refs_4_ = bf16[96,128]{1,0:T(8,128)(2,1)S(1)} collective-permute-done((bf16[96,128]{1,0:T(8,128)(2,1)S(1)}, bf16[96,128]{1,0:T(8,128)(2,1)S(1)}, u32[]{:S(2)}, u32[]{:S(2)}) %collective-permute-start.4) | collective-permute-done | bytes 24608 | tf_op jit(solution)/shard_map/ppermute | solution.py:373
  24.0 11.4 %shard_map.138 = (bf16[96,8,256]{2,1,0:T(8,128)(2,1)}, bf16[8,96,256]{2,1,0:T(8,128)(2,1)S(1)}, bf16[3,96,256]{2,1,0:T(8,128)(2,1)S(1)}, bf16[3,96,256]{2,1,0:T(...) custom-call(bf16[8,96,256]{2,1,0:T(8,128)(2,1)S(1)} %get-tuple-element.29.refs_0_, ...), custom_call_target="tpu_custom_call" | custom-call | tf_op jit(solution)/shard_map/pallas_call | solution.py:48
  35.4 0.7 collective-permute-start.7
  36.1 3.2 %collective-permute-start.5 = (bf16[3,96,256]{2,1,0:T(8,128)(2,1)S(1)}, bf16[3,96,256]{2,1,0:T(8,128)(2,1)S(1)}, u32[]{:S(2)}, u32[]{:S(2)}) collective-permute-start(bf16[3,96,256]{2,1,0:T(8,128)(2,1)S(1)} %get-tuple-element.37), channel_id=1, source_target_pairs={{0,1},{1,2},{2,3},{3,4},{4,5},{5,6},{6,7},{7,8},{8,9},{9,10},{10,1... | collective-permute-start | bytes 442376 | tf_op jit(solution)/shard_map/ppermute | solution.py:364
  39.3 1.3 %collective-permute-start.6 = (bf16[3,96,256]{2,1,0:T(8,128)(2,1)S(1)}, bf16[3,96,256]{2,1,0:T(8,128)(2,1)S(1)}, u32[]{:S(2)}, u32[]{:S(2)}) collective-permute-start(bf16[3,96,256]{2,1,0:T(8,128)(2,1)S(1)} %get-tuple-element.38), channel_id=1, source_target_pairs={{1,0},{2,1},{3,2},{4,3},{5,4},{6,5},{7,6},{8,7},{9,8},{10,9},{11,1... | collective-permute-start | bytes 442376 | tf_op jit(solution)/shard_map/ppermute | solution.py:365
  40.6 8.7 %shard_map.140.refs_4_ = bf16[384,128]{1,0:T(8,128)(2,1)S(1)} custom-call(f32[14,96,384]{2,1,0:T(8,128)S(1)} %get-tuple-element.39.refs_0_, bf16[8,96,256]{2,1,0:T(8,128)(2,1)S(1)} %get-tuple-element.36.refs_1_.refs_0_, bf16[288,128]{1,0:T(8,128)(2,1)S(1)} %get-tuple-element.40.refs_2_, f32[96,128]{1,0:T(8,128)S(1)} %get-tuple-element.41.refs_3_), custom_call_target="tpu_custom_call" | custom-call | tf_op jit(solution)/shard_map/pallas_call | solution.py:48
  49.3 0.0 collective-permute-done.7.refs_0_
  49.3 0.2 shard_map.139.refs_3_
  49.5 0.0 collective-permute-done.5.refs_1_
  49.5 0.0 collective-permute-done.6.refs_2_
  49.5 0.8 shard_map.141
  50.4 19.8 %all-to-all-start = ((bf16[16,24,128]{2,1,0:T(8,128)(2,1)}), bf16[16,24,128]{2,1,0:T(8,128)(2,1)S(1)}, u32[]{:S(2)}, u32[]{:S(2)}) async-start(bf16[16,24,128]{2,1,0:T(8,128)(2,1)} %bitcast.4), calls=%async_computation | async-start | bytes 196608 | tf_op jit(solution)/shard_map/all_to_all | solution.py:465
  70.1 1.9 %collective-permute-start.8 = (bf16[96,128]{1,0:T(8,128)(2,1)S(1)}, bf16[96,128]{1,0:T(8,128)(2,1)S(1)}, u32[]{:S(2)}, u32[]{:S(2)}) collective-permute-start(bf16[96,128]{1,0:T(8,128)(2,1)S(1)} %get-tuple-element.43), channel_id=1, source_target_pairs={{0,16},{16,32},{32,48},{48,64},{64,80},{80,96},{96,112},{112,128},... | collective-permute-start | bytes 73736 | tf_op jit(solution)/shard_map/ppermute | solution.py:372
  72.1 9.6 %collective-permute-start.9 = (bf16[96,128]{1,0:T(8,128)(2,1)S(1)}, bf16[96,128]{1,0:T(8,128)(2,1)S(1)}, u32[]{:S(2)}, u32[]{:S(2)}) collective-permute-start(bf16[96,128]{1,0:T(8,128)(2,1)S(1)} %get-tuple-element.44), channel_id=1, source_target_pairs={{0,496},{16,0},{32,16},{48,32},{64,48},{80,64},{96,80},{112,96},{1... | collective-permute-start | bytes 73736 | tf_op jit(solution)/shard_map/ppermute | solution.py:373
  81.6 0.0 collective-permute-done.8.refs_3_.refs_1_
  81.7 0.8 collective-permute-done.9.refs_4_.refs_2_
  82.5 0.0 all-to-all-done.refs_0_
  82.5 26.4 %all_to_all.15.refs_0_ = bf16[32,24,128]{2,1,0:T(8,128)(2,1)S(1)} all-to-all(bf16[32,24,128]{2,1,0:T(8,128)(2,1)S(1)} %shard_map.143), channel_id=1, replica_groups=mesh['lon'=32,'lat'=16] {'lon'}, dimensions={0} | all-to-all | bytes 393216 | tf_op jit(solution)/shard_map/all_to_all | solution.py:469
  108.9 0.7 shard_map.144
  109.6 7.2 %all-to-all-start.2 = ((f32[16,24,128]{2,1,0:T(8,128)}), f32[16,24,128]{2,1,0:T(8,128)S(1)}, u32[]{:S(2)}, u32[]{:S(2)}) async-start(f32[16,24,128]{2,1,0:T(8,128)} %shard_map.144), calls=%async_computation.2 | async-start | bytes 393216 | tf_op jit(solution)/shard_map/all_to_all | solution.py:471
  116.8 7.4 %shard_map.142 = bf16[96,8,256]{2,1,0:T(8,128)(2,1)} custom-call(bf16[8,96,256]{2,1,0:T(8,128)(2,1)S(1)} %get-tuple-element.36.refs_1_.refs_0_, bf16[3,96,256]{2,1,0:T(8,128)(2,1)S(1)} %collective-permute-done.5.refs_1_, bf16[3,96,256]{2,1,0:T(8,128)(2,1)S(1)} %get-tuple-element.42.refs_2_, bf16[96,128]{1,0:T(8,128)(2,1)S(1)} %collective-permute-done.8.refs_3_.refs_1_, ...), custom_call_target="tpu_custom_call" | custom-call | tf_op jit(solution)/shard_map/pallas_call | solution.py:48
  124.2 2.6 %all-to-all-done.2 = f32[16,24,128]{2,1,0:T(8,128)S(1)} async-done(((f32[16,24,128]{2,1,0:T(8,128)}), f32[16,24,128]{2,1,0:T(8,128)S(1)}, u32[]{:S(2)}, u32[]{:S(2)}) %all-to-all-start.2) | async-done | bytes 196640 | tf_op jit(solution)/shard_map/all_to_all | solution.py:471
  126.8 0.8 shard_map.145
  (1 shorter events, 0.0 us)
Async XLA Ops:
  1.9 6.8 %collective-permute-start.2 = (bf16[3,96,256]{2,1,0:T(8,128)(2,1)S(1)}, bf16[3,96,256]{2,1,0:T(8,128)(2,1)S(1)}, u32[]{:S(2)}, u32[]{:S(2)}) collective-permute-start(bf16[3,96,256]{2,1,0:T(8,128)(2,1)S(1)} %get-tuple-element.30), channel_id=1, source_target_pairs={{15,511},{31,495},{47,479},{63,463},{79,447},{95,431},{111,415},{1... | collective-permute-start | bytes 442376 | tf_op jit(solution)/shard_map/ppermute | solution.py:363
  2.6 6.9 %collective-permute-start = (bf16[3,96,256]{2,1,0:T(8,128)(2,1)S(1)}, bf16[3,96,256]{2,1,0:T(8,128)(2,1)S(1)}, u32[]{:S(2)}, u32[]{:S(2)}) collective-permute-start(bf16[3,96,256]{2,1,0:T(8,128)(2,1)S(1)} %get-tuple-element.30), channel_id=1, source_target_pairs={{0,1},{1,2},{2,3},{3,4},{4,5},{5,6},{6,7},{7,8},{8,9},{9,10},{10,1... | collective-permute-start | bytes 442376 | tf_op jit(solution)/shard_map/ppermute | solution.py:364
  7.4 5.9 %collective-permute-start.1 = (bf16[3,96,256]{2,1,0:T(8,128)(2,1)S(1)}, bf16[3,96,256]{2,1,0:T(8,128)(2,1)S(1)}, u32[]{:S(2)}, u32[]{:S(2)}) collective-permute-start(bf16[3,96,256]{2,1,0:T(8,128)(2,1)S(1)} %get-tuple-element.31), channel_id=1, source_target_pairs={{1,0},{2,1},{3,2},{4,3},{5,4},{6,5},{7,6},{8,7},{9,8},{10,9},{11,1... | collective-permute-start | bytes 442376 | tf_op jit(solution)/shard_map/ppermute | solution.py:365
  13.5 8.3 %collective-permute-start.3 = (bf16[96,128]{1,0:T(8,128)(2,1)S(1)}, bf16[96,128]{1,0:T(8,128)(2,1)S(1)}, u32[]{:S(2)}, u32[]{:S(2)}) collective-permute-start(bf16[96,128]{1,0:T(8,128)(2,1)S(1)} %get-tuple-element.33), channel_id=1, source_target_pairs={{0,16},{16,32},{32,48},{48,64},{64,80},{80,96},{96,112},{112,128},... | collective-permute-start | bytes 73736 | tf_op jit(solution)/shard_map/ppermute | solution.py:372
  18.8 5.1 %collective-permute-start.4 = (bf16[96,128]{1,0:T(8,128)(2,1)S(1)}, bf16[96,128]{1,0:T(8,128)(2,1)S(1)}, u32[]{:S(2)}, u32[]{:S(2)}) collective-permute-start(bf16[96,128]{1,0:T(8,128)(2,1)S(1)} %get-tuple-element.34), channel_id=1, source_target_pairs={{0,496},{16,0},{32,16},{48,32},{64,48},{80,64},{96,80},{112,96},{1... | collective-permute-start | bytes 73736 | tf_op jit(solution)/shard_map/ppermute | solution.py:373
  35.4 13.9 %collective-permute-start.7 = (bf16[3,96,256]{2,1,0:T(8,128)(2,1)S(1)}, bf16[3,96,256]{2,1,0:T(8,128)(2,1)S(1)}, u32[]{:S(2)}, u32[]{:S(2)}) collective-permute-start(bf16[3,96,256]{2,1,0:T(8,128)(2,1)S(1)} %get-tuple-element.37), channel_id=1, source_target_pairs={{15,511},{31,495},{47,479},{63,463},{79,447},{95,431},{111,415},{1... | collective-permute-start | bytes 442376 | tf_op jit(solution)/shard_map/ppermute | solution.py:363
  36.1 13.5 %collective-permute-start.5 = (bf16[3,96,256]{2,1,0:T(8,128)(2,1)S(1)}, bf16[3,96,256]{2,1,0:T(8,128)(2,1)S(1)}, u32[]{:S(2)}, u32[]{:S(2)}) collective-permute-start(bf16[3,96,256]{2,1,0:T(8,128)(2,1)S(1)} %get-tuple-element.37), channel_id=1, source_target_pairs={{0,1},{1,2},{2,3},{3,4},{4,5},{5,6},{6,7},{7,8},{8,9},{9,10},{10,1... | collective-permute-start | bytes 442376 | tf_op jit(solution)/shard_map/ppermute | solution.py:364
  39.3 10.3 %collective-permute-start.6 = (bf16[3,96,256]{2,1,0:T(8,128)(2,1)S(1)}, bf16[3,96,256]{2,1,0:T(8,128)(2,1)S(1)}, u32[]{:S(2)}, u32[]{:S(2)}) collective-permute-start(bf16[3,96,256]{2,1,0:T(8,128)(2,1)S(1)} %get-tuple-element.38), channel_id=1, source_target_pairs={{1,0},{2,1},{3,2},{4,3},{5,4},{6,5},{7,6},{8,7},{9,8},{10,9},{11,1... | collective-permute-start | bytes 442376 | tf_op jit(solution)/shard_map/ppermute | solution.py:365
  50.4 32.1 %all-to-all-start = ((bf16[16,24,128]{2,1,0:T(8,128)(2,1)}), bf16[16,24,128]{2,1,0:T(8,128)(2,1)S(1)}, u32[]{:S(2)}, u32[]{:S(2)}) async-start(bf16[16,24,128]{2,1,0:T(8,128)(2,1)} %bitcast.4), calls=%async_computation | async-start | bytes 196608 | tf_op jit(solution)/shard_map/all_to_all | solution.py:465
  70.1 11.5 %collective-permute-start.8 = (bf16[96,128]{1,0:T(8,128)(2,1)S(1)}, bf16[96,128]{1,0:T(8,128)(2,1)S(1)}, u32[]{:S(2)}, u32[]{:S(2)}) collective-permute-start(bf16[96,128]{1,0:T(8,128)(2,1)S(1)} %get-tuple-element.43), channel_id=1, source_target_pairs={{0,16},{16,32},{32,48},{48,64},{64,80},{80,96},{96,112},{112,128},... | collective-permute-start | bytes 73736 | tf_op jit(solution)/shard_map/ppermute | solution.py:372
  72.1 10.4 %collective-permute-start.9 = (bf16[96,128]{1,0:T(8,128)(2,1)S(1)}, bf16[96,128]{1,0:T(8,128)(2,1)S(1)}, u32[]{:S(2)}, u32[]{:S(2)}) collective-permute-start(bf16[96,128]{1,0:T(8,128)(2,1)S(1)} %get-tuple-element.44), channel_id=1, source_target_pairs={{0,496},{16,0},{32,16},{48,32},{64,48},{80,64},{96,80},{112,96},{1... | collective-permute-start | bytes 73736 | tf_op jit(solution)/shard_map/ppermute | solution.py:373
  109.6 17.1 %all-to-all-start.2 = ((f32[16,24,128]{2,1,0:T(8,128)}), f32[16,24,128]{2,1,0:T(8,128)S(1)}, u32[]{:S(2)}, u32[]{:S(2)}) async-start(f32[16,24,128]{2,1,0:T(8,128)} %shard_map.144), calls=%async_computation.2 | async-start | bytes 393216 | tf_op jit(solution)/shard_map/all_to_all | solution.py:471

commit v4 on v3

--- a/solution.py
+++ b/solution.py
@@ -76,33 +76,38 @@
     return jnp.concatenate(parts, axis=1)
 
 
-def rows_body(settle, f_ref, mask_ref, m_ref, first_ref, last_ref, flat):
+def choose(flag, yes, no):
+    return jnp.where(jnp.broadcast_to(flag, yes.shape) > 0, yes, no)
+
+
+def rows_body(settle, f_ref, mask_ref, place_ref, m_ref, inner_ref, outer_ref, flat):
     channels, rows, cols = f_ref.shape
     settle()
     spread(flat, f_ref[...].astype(F32) * mask_ref[...].astype(F32)[None])
+    kept = [row_of(flat, i, channels, rows) for i in range(rows)]
     for i in range(rows):
-        row = row_of(flat, i, channels, rows).astype(BF16)
-        m_ref[i] = row
-        if i < RING:
-            first_ref[i] = row
-        if i >= rows - RING:
-            last_ref[i - (rows - RING)] = row
-
-
-def turn_body(mirror_ref, turned_ref):
-    cols = mirror_ref.shape[2]
+        m_ref[i] = kept[i].astype(BF16)
+    even = place_ref[0]
+    for k in range(RING):
+        first, last = kept[k], kept[rows - RING + k]
+        inner_ref[k] = choose(even, last, first).astype(BF16)
+        outer_ref[k] = choose(even, first, last).astype(BF16)
+
+
+def strips_body(
+    m_ref, inner_ref, outer_ref, place_ref, south_ref, halo_ref, near_ref, far_ref
+):
+    rows, channels, cols = m_ref.shape
     here = lax.broadcasted_iota(jnp.int32, (cols, cols), 0)
     there = lax.broadcasted_iota(jnp.int32, (cols, cols), 1)
     flip = (here + there == cols - 1).astype(F32).astype(BF16)
+    even, top, lon_even = place_ref[0], place_ref[1], place_ref[2]
     for k in range(RING):
-        row = jnp.dot(mirror_ref[RING - 1 - k], flip, preferred_element_type=F32)
-        turned_ref[k] = row.astype(BF16)
-
-
-def strips_body(m_ref, south_ref, north_ref, turned_ref, halo_ref, left_ref, right_ref):
-    rows, channels, cols = m_ref.shape
-    for k in range(RING):
-        halo_ref[k] = (north_ref[k].astype(F32) + turned_ref[k].astype(F32)).astype(BF16)
+        inner = inner_ref[k].astype(F32)
+        outer = outer_ref[k].astype(F32)
+        turned = jnp.dot(outer_ref[RING - 1 - k], flip, preferred_element_type=F32)
+        south_ref[k] = choose(even, outer, inner).astype(BF16)
+        halo_ref[k] = choose(even, inner, choose(top, turned, outer)).astype(BF16)
     lane = lax.broadcasted_iota(jnp.int32, (channels, 128), 1)
     left = jnp.zeros((channels, 128), F32)
     right = jnp.zeros((channels, 128), F32)
@@ -121,22 +126,27 @@
         tail = pltpu.roll(tail, RING * r + RING, 1)
         left = jnp.where(here, head, left)
         right = jnp.where(here, tail, right)
-    left_ref[...] = left.astype(BF16)
-    right_ref[...] = right.astype(BF16)
+    near_ref[...] = choose(lon_even, right, left).astype(BF16)
+    far_ref[...] = choose(lon_even, left, right).astype(BF16)
 
 
 def strips_and_sums_body(
-    m_ref, south_ref, north_ref, turned_ref, sums_ref, halo_ref, left_ref, right_ref, out_ref
+    m_ref, inner_ref, outer_ref, sums_ref, place_ref,
+    south_ref, halo_ref, near_ref, far_ref, out_ref,
 ):
-    strips_body(m_ref, south_ref, north_ref, turned_ref, halo_ref, left_ref, right_ref)
+    strips_body(
+        m_ref, inner_ref, outer_ref, place_ref, south_ref, halo_ref, near_ref, far_ref
+    )
     out_ref[...] = sums_ref[...]
 
 
-def fill(ext, m_ref, south_ref, halo_ref, before_ref, after_ref):
+def fill(ext, m_ref, south_ref, halo_ref, near_ref, far_ref, lon_even):
     rows, channels, cols = m_ref.shape
     lane = lax.broadcasted_iota(jnp.int32, (channels, 128), 1)
-    before = before_ref[...].astype(F32)
-    after = after_ref[...].astype(F32)
+    near = near_ref[...].astype(F32)
+    far = far_ref[...].astype(F32)
+    before = choose(lon_even, far, near)
+    after = choose(lon_even, near, far)
     for r in range(rows + 2 * RING):
         if r < RING:
             row = south_ref[r]
@@ -199,16 +209,16 @@
 
 
 def block_body(
-    settle, m_ref, south_ref, halo_ref, before_ref, after_ref, ct_ref, mask_ref,
-    dw_ref, gain_ref, w_in_ref, b_ref, w_out_ref,
-    out_ref, g_ref, first_ref, last_ref, wide_ref, tail_ref, ext_ref,
+    settle, m_ref, south_ref, halo_ref, near_ref, far_ref, ct_ref, mask_ref,
+    dw_ref, gain_ref, w_in_ref, b_ref, w_out_ref, place_ref,
+    out_ref, g_ref, inner_ref, outer_ref, wide_ref, tail_ref, ext_ref,
     conv, flat, act, back, sca, pre, b_acc, gain_acc, taps,
 ):
     ext = ext_ref
     rows, channels, cols = m_ref.shape
     hidden = w_out_ref.shape[0]
     pairs = cols // 128
-    fill(ext, m_ref, south_ref, halo_ref, before_ref, after_ref)
+    fill(ext, m_ref, south_ref, halo_ref, near_ref, far_ref, place_ref[2])
     settle()
     taps[...] = tap_columns(dw_ref)
     sea = mask_ref[...].astype(F32)
@@ -269,13 +279,13 @@
             - jnp.mean(norm_grad, axis=0, keepdims=True)
             - normed * jnp.mean(norm_grad * normed, axis=0, keepdims=True)
         )
-        short = grad.astype(BF16)
-        g_ref[i] = short
-        if i < RING:
-            first_ref[i] = short
-        if i >= rows - RING:
-            last_ref[i - (rows - RING)] = short
-
+        g_ref[i] = grad.astype(BF16)
+
+    even = place_ref[0]
+    for k in range(RING):
+        first, last = g_ref[k].astype(F32), g_ref[rows - RING + k].astype(F32)
+        inner_ref[k] = choose(even, last, first).astype(BF16)
+        outer_ref[k] = choose(even, first, last).astype(BF16)
     out_ref[...] = (gather(flat, channels, rows) * sea[None]).astype(BF16)
     over_cells = (((1,), (1,)), ((), ()))
     w_in_sum = lax.dot_general(sca[...], pre[...], over_cells, preferred_element_type=F32)
@@ -332,19 +342,19 @@
 
 
 def back_body(
-    settle, g_ref, south_ref, halo_ref, before_ref, after_ref, ct_ref, mask_ref, dw_ref, top_ref,
+    settle, g_ref, south_ref, halo_ref, near_ref, far_ref, ct_ref, mask_ref, dw_ref, place_ref,
     out_ref, ext, flat, taps,
 ):
     rows, channels, cols = g_ref.shape
     pairs = cols // 128
-    fill(ext, g_ref, south_ref, halo_ref, before_ref, after_ref)
+    fill(ext, g_ref, south_ref, halo_ref, near_ref, far_ref, place_ref[2])
     settle()
     taps[...] = tap_columns(dw_ref)
 
     def step(ct, carry):
         c0 = pl.multiple_of(ct * 8, 8)
         lane = lanes()
-        top = jnp.broadcast_to(top_ref[0], (8, 128)) > 0
+        top = jnp.broadcast_to(place_ref[1], (8, 128)) > 0
         summed = correlate(ext, c0, rows, pairs, lane, taps[pl.ds(c0, 8), :], top)
         for i in range(rows):
             for t in range(pairs):
@@ -357,21 +367,23 @@
     out_ref[...] = (grad * sea).astype(BF16)
 
 
-def lat_halo(first, last):
+def lat_halo(inner, outer):
     n_lat, n_lon = lax.axis_size("lat"), lax.axis_size("lon")
-    tops = [i * n_lat + n_lat - 1 for i in range(n_lon)]
-    mirror = lax.ppermute(last, ("lon", "lat"), list(zip(tops, tops[::-1])))
-    south = lax.ppermute(last, "lat", [(i, i + 1) for i in range(n_lat - 1)])
-    north = lax.ppermute(first, "lat", [(i + 1, i) for i in range(n_lat - 1)])
-    (turned,) = call(turn_body, [pltpu.VMEM(last.shape, last.dtype)], [mirror])
-    return south, north, turned
-
-
-def lon_halo(left, right):
+    pairs = []
+    for i in range(n_lon):
+        for j in range(1, n_lat - 1, 2):
+            pairs += [(i * n_lat + j, i * n_lat + j + 1), (i * n_lat + j + 1, i * n_lat + j)]
+        pairs.append((i * n_lat + n_lat - 1, (n_lon - 1 - i) * n_lat + n_lat - 1))
+    outer = lax.ppermute(outer, ("lon", "lat"), pairs)
+    inner = lax.ppermute(inner, "lat", [(i, i ^ 1) for i in range(n_lat)])
+    return inner, outer
+
+
+def lon_halo(near, far):
     n_lon = lax.axis_size("lon")
-    before = lax.ppermute(right, "lon", [(i, (i + 1) % n_lon) for i in range(n_lon)])
-    after = lax.ppermute(left, "lon", [(i, (i - 1) % n_lon) for i in range(n_lon)])
-    return before, after
+    far = lax.ppermute(far, "lon", [(i, (i - 1 + 2 * (i % 2)) % n_lon) for i in range(n_lon)])
+    near = lax.ppermute(near, "lon", [(i, i ^ 1) for i in range(n_lon)])
+    return near, far
 
 
 def held(struct):
@@ -408,7 +420,8 @@
     hidden = w_out.shape[0]
     n_lat, n_lon = lax.axis_size("lat"), lax.axis_size("lon")
     taps = dw_kernel.transpose(1, 2, 0)
-    is_top = (lax.axis_index("lat") == n_lat - 1).astype(jnp.int32).reshape(1)
+    lat, lon = lax.axis_index("lat"), lax.axis_index("lon")
+    place = jnp.stack([1 - lat % 2, (lat == n_lat - 1).astype(jnp.int32), 1 - lon % 2])
     ring = like((RING, channels, cols), BF16)
     grid = like((rows, channels, cols), BF16)
     whole = like((channels, rows, cols), BF16)
@@ -419,26 +432,28 @@
     height = 2 * channels + hidden
     near_sums = pltpu.VMEM((height, 128), BF16)
     cells = rows * cols
-    masked, first, last = call(
-        rows_body, [held(grid), near_ring, near_ring], [], [fields, land_mask], scratch=[flat]
-    )
-    south, north, turned = lat_halo(first, last)
-    fold, left, right = call(
-        strips_body, [near_ring, strip, strip], [masked, south, north, turned]
-    )
-    before, after = lon_halo(left, right)
+    masked, inner, outer = call(
+        rows_body, [held(grid), near_ring, near_ring], [], [fields, land_mask], [place],
+        scratch=[flat],
+    )
+    inner, outer = lat_halo(inner, outer)
+    south, north, near, far = call(
+        strips_body, [near_ring, near_ring, strip, strip], [masked, inner, outer], (), [place]
+    )
+    near, far = lon_halo(near, far)
     columns = pltpu.VMEM((channels, 128), F32)
-    output, grads, first, last, wide, tail, ext_rows = call(
+    output, grads, inner, outer, wide, tail, ext_rows = call(
         block_body,
         [
             whole, held(grid), near_ring, near_ring,
             pltpu.VMEM((height - channels, 128), BF16), columns, ext,
         ],
-        [masked, south, fold, before, after],
+        [masked, south, north, near, far],
         [
             cotangent, land_mask, taps, gain.reshape(1, channels), w_in,
             b_in.reshape(1, hidden), w_out,
         ],
+        [place],
         scratch=[
             pltpu.VMEM((rows, channels, cols), F32),
             flat,
@@ -451,27 +466,27 @@
             columns,
         ],
     )
-    south, north, turned = lat_halo(first, last)
+    inner, outer = lat_halo(inner, outer)
     (sums,) = call(
         functools.partial(kernel_body, hidden - 128), [near_sums], [ext_rows, grads, wide, tail],
         scratch=[columns, pltpu.VMEM((rows, channels, cols), F32)],
     )
-    fold, left, right, sums = call(
-        strips_and_sums_body, [near_ring, strip, strip, near_sums],
-        [grads, south, north, turned, sums],
-    )
-    before, after = lon_halo(left, right)
+    south, north, near, far, sums = call(
+        strips_and_sums_body, [near_ring, near_ring, strip, strip, near_sums],
+        [grads, inner, outer, sums], (), [place],
+    )
+    near, far = lon_halo(near, far)
     size = height // n_lat
     pieces = lax.all_to_all(sums.reshape(n_lat, size, 128), "lat", 0, 0, tiled=True)
+    (pieces,) = call(spread_body, [pltpu.VMEM((n_lon, size, 128), BF16)], [pieces])
+    pieces = lax.all_to_all(pieces, "lon", 0, 0, tiled=True)
     (pieces,) = call(
-        spread_body, [pltpu.VMEM((n_lon, size, 128), BF16)], [pieces], waits=[before, after]
-    )
-    pieces = lax.all_to_all(pieces, "lon", 0, 0, tiled=True)
-    (pieces,) = call(spread_body, [pltpu.VMEM((n_lat, size, 128), F32)], [pieces])
+        spread_body, [pltpu.VMEM((n_lat, size, 128), F32)], [pieces], waits=[near, far]
+    )
     pieces = lax.all_to_all(pieces, "lat", 0, 0, tiled=True)
     (input_grad,) = call(
-        back_body, [whole], [grads, south, fold, before, after], [cotangent, land_mask, taps],
-        [is_top], scratch=[ext, flat, columns],
+        back_body, [whole], [grads, south, north, near, far], [cotangent, land_mask, taps],
+        [place], scratch=[ext, flat, columns],
     )
     scale = float(cells * n_lat * n_lon) ** -0.5
     w_in_grad, w_out_grad, dw_grad, gain_grad, b_grad = call(

time: 128 us -> 115 us (0.90)
  starting transfers between devices: 58.7 us -> 42.2 us
  waiting for transfers between devices: 9.85 us -> 13.6 us
  blocking collectives: 26.4 us -> 23 us
  Pallas kernels: 31.7 us -> 34.5 us
    all_to_all x1, starting transfers between devices: 19.8 us -> 10.1 us  [shards(): pieces = lax.all_to_all(pieces, 'lon', 0, 0, tiled=True)]
    all_to_all x1, waiting for transfers between devices: 0.01 us -> 3.85 us  [shards(): pieces = lax.all_to_all(pieces, 'lon', 0, 0, tiled=True)]
    all_to_all x1, starting transfers between devices: 7.19 us -> 3.52 us  [shards(): pieces = lax.all_to_all(pieces, 'lat', 0, 0, tiled=True)]
    all_to_all x1, blocking collectives: 26.4 us -> 23 us  [shards(): lax.all_to_all(sums.reshape(n_lat, size, 128), 'lat', 0, 0, tiled=True)]
    ppermute x10 -> x8, starting transfers between devices: 31.8 us -> 28.6 us  [the longest x2 11.3 us: lat_halo(): inner = lax.ppermute(inner, 'lat', [(i, i ^ 1) for i in range(n_lat)])]
    pallas_call x11 -> x9, Pallas kernels: 31.7 us -> 34.5 us  [call(): pl.pallas_call(run, out_shape=outs, in_specs=specs, out_specs=[pl.BlockSp...]
    ppermute x10 -> x8, waiting for transfers between devices: 7.29 us -> 7.41 us  [the longest x2 5.56 us: lon_halo(): lax.ppermute(far, 'lon', [(i, (i - 1 + 2 * (i % 2)) % n_lon) for i in ran...]
  transfers between devices with their start and end apart: 12 -> 10, of which waited for: 5 -> 5; matrix products, arithmetic and copies ran while one was open for 0% -> 0% of each run, Pallas kernels for 13% -> 15%
where the time goes in v4:
time: 115 us; the launch traced here: 114 us
  starting transfers between devices  42.2 us (37%)
  Pallas kernels  34.5 us (30%)
  blocking collectives  23 us (20%)
  waiting for transfers between devices  13.6 us (12%)
    pallas_call x9, Pallas kernels, call(): pl.pallas_call(run, out_shape=outs, in_specs=specs, out_specs=[pl.BlockSp...  34.5 us
    all_to_all x1, blocking collectives, shards(): lax.all_to_all(sums.reshape(n_lat, size, 128), 'lat', 0, 0, tiled=True)  23 us
    ppermute x2, starting transfers between devices, lat_halo(): inner = lax.ppermute(inner, 'lat', [(i, i ^ 1) for i in range(n_lat)])  11.3 us
    ppermute x2, starting transfers between devices, lon_halo(): near = lax.ppermute(near, 'lon', [(i, i ^ 1) for i in range(n_lon)])  10.6 us
    all_to_all x1, starting transfers between devices, shards(): pieces = lax.all_to_all(pieces, 'lon', 0, 0, tiled=True)  10.1 us
    ppermute x2, waiting for transfers between devices, lon_halo(): lax.ppermute(far, 'lon', [(i, (i - 1 + 2 * (i % 2)) % n_lon) for i in ran...  5.56 us
    ppermute x2, starting transfers between devices, lon_halo(): lax.ppermute(far, 'lon', [(i, (i - 1 + 2 * (i % 2)) % n_lon) for i in ran...  5.37 us
    all_to_all x1, waiting for transfers between devices, shards(): pieces = lax.all_to_all(pieces, 'lon', 0, 0, tiled=True)  3.85 us
  transfers between devices with their start and end apart: 10, of which 5 were waited for; matrix products, arithmetic and copies ran while one was open for 0% of the time, Pallas kernels for 15%

profile of v4, /device:TPU:1, one launch (start us, length us, event | category | flops | bytes accessed | tf_op | source)
XLA Modules:
  0.0 114.2 jit_solution(9174093677208387268)
XLA Ops:
  0.7 0.1 pad_add_fusion.refs_2_.refs_3_.refs_12_.refs_4_.refs_8_
  0.7 1.8 %shard_map.135 = (bf16[8,96,256]{2,1,0:T(8,128)(2,1)S(1)}, bf16[3,96,256]{2,1,0:T(8,128)(2,1)S(1)}, bf16[3,96,256]{2,1,0:T(8,128)(2,1)S(1)}) custom-call(bf16[96,8,256]{2,1,0:T(8,128)(2,1)} %refs_0_.1, s32[8,256]{1,0:T(8,128)} %refs_6_.3, s32[3]{0:T(128)S(1)} %pad_add_fusion.refs_2_.refs_3_.refs_12_.refs_4_.refs_8_), custom_call_target="tpu_custom_call" | custom-call | tf_op jit(solution)/shard_map/pallas_call | solution.py:48
  2.6 4.8 %collective-permute-start = (bf16[3,96,256]{2,1,0:T(8,128)(2,1)S(1)}, bf16[3,96,256]{2,1,0:T(8,128)(2,1)S(1)}, u32[]{:S(2)}, u32[]{:S(2)}) collective-permute-start(bf16[3,96,256]{2,1,0:T(8,128)(2,1)S(1)} %get-tuple-element.32), channel_id=1, source_target_pairs={{0,1},{1,0},{2,3},{3,2},{4,5},{5,4},{6,7},{7,6},{8,9},{9,8},{10,11... | collective-permute-start | bytes 442376 | tf_op jit(solution)/shard_map/ppermute | solution.py:378
  7.4 0.7 collective-permute-start.1
  8.1 1.8 %collective-permute-done.refs_1_ = bf16[3,96,256]{2,1,0:T(8,128)(2,1)S(1)} collective-permute-done((bf16[3,96,256]{2,1,0:T(8,128)(2,1)S(1)}, bf16[3,96,256]{2,1,0:T(8,128)(2,1)S(1)}, u32[]{:S(2)}, u32[]{:S(2)}) %collective-permute-start) | collective-permute-done | bytes 147488 | tf_op jit(solution)/shard_map/ppermute | solution.py:378
  9.9 0.0 collective-permute-done.1.refs_2_
  9.9 0.9 shard_map.136
  10.9 8.5 %collective-permute-start.2 = (bf16[96,128]{1,0:T(8,128)(2,1)S(1)}, bf16[96,128]{1,0:T(8,128)(2,1)S(1)}, u32[]{:S(2)}, u32[]{:S(2)}) collective-permute-start(bf16[96,128]{1,0:T(8,128)(2,1)S(1)} %get-tuple-element.36), channel_id=1, source_target_pairs={{0,16},{16,0},{32,48},{48,32},{64,80},{80,64},{96,112},{112,96},{1... | collective-permute-start | bytes 73736 | tf_op jit(solution)/shard_map/ppermute | solution.py:385
  19.3 1.9 %collective-permute-start.3 = (bf16[96,128]{1,0:T(8,128)(2,1)S(1)}, bf16[96,128]{1,0:T(8,128)(2,1)S(1)}, u32[]{:S(2)}, u32[]{:S(2)}) collective-permute-start(bf16[96,128]{1,0:T(8,128)(2,1)S(1)} %get-tuple-element.37), channel_id=1, source_target_pairs={{0,496},{16,32},{32,16},{48,64},{64,48},{80,96},{96,80},{112,128},... | collective-permute-start | bytes 73736 | tf_op jit(solution)/shard_map/ppermute | solution.py:384
  21.3 0.0 collective-permute-done.2.refs_3_
  21.3 3.2 %collective-permute-done.3.refs_4_ = bf16[96,128]{1,0:T(8,128)(2,1)S(1)} collective-permute-done((bf16[96,128]{1,0:T(8,128)(2,1)S(1)}, bf16[96,128]{1,0:T(8,128)(2,1)S(1)}, u32[]{:S(2)}, u32[]{:S(2)}) %collective-permute-start.3) | collective-permute-done | bytes 24608 | tf_op jit(solution)/shard_map/ppermute | solution.py:384
  24.5 12.0 %shard_map.137 = (bf16[96,8,256]{2,1,0:T(8,128)(2,1)}, bf16[8,96,256]{2,1,0:T(8,128)(2,1)S(1)}, bf16[3,96,256]{2,1,0:T(8,128)(2,1)S(1)}, bf16[3,96,256]{2,1,0:T(...) custom-call(bf16[8,96,256]{2,1,0:T(8,128)(2,1)S(1)} %get-tuple-element.31.refs_0_, ...), custom_call_target="tpu_custom_call" | custom-call | tf_op jit(solution)/shard_map/pallas_call | solution.py:48
  36.5 6.5 %collective-permute-start.4 = (bf16[3,96,256]{2,1,0:T(8,128)(2,1)S(1)}, bf16[3,96,256]{2,1,0:T(8,128)(2,1)S(1)}, u32[]{:S(2)}, u32[]{:S(2)}) collective-permute-start(bf16[3,96,256]{2,1,0:T(8,128)(2,1)S(1)} %get-tuple-element.40), channel_id=1, source_target_pairs={{0,1},{1,0},{2,3},{3,2},{4,5},{5,4},{6,7},{7,6},{8,9},{9,8},{10,11... | collective-permute-start | bytes 442376 | tf_op jit(solution)/shard_map/ppermute | solution.py:378
  42.9 0.7 collective-permute-start.5
  43.6 8.7 %shard_map.138.refs_3_ = bf16[384,128]{1,0:T(8,128)(2,1)S(1)} custom-call(f32[14,96,384]{2,1,0:T(8,128)S(1)} %get-tuple-element.42.refs_0_, bf16[8,96,256]{2,1,0:T(8,128)(2,1)S(1)} %get-tuple-element.39.refs_1_.refs_0_, bf16[288,128]{1,0:T(8,128)(2,1)S(1)} %get-tuple-element.43.refs_2_, f32[96,128]{1,0:T(8,128)S(1)} %get-tuple-element.44.refs_3_), custom_call_target="tpu_custom_call" | custom-call | tf_op jit(solution)/shard_map/pallas_call | solution.py:48
  52.4 0.0 collective-permute-done.4.refs_1_
  52.4 0.0 collective-permute-done.5.refs_2_
  52.4 0.9 shard_map.139
  53.3 23.0 %all_to_all.15.refs_0_ = bf16[16,24,128]{2,1,0:T(8,128)(2,1)S(1)} all-to-all(bf16[16,24,128]{2,1,0:T(8,128)(2,1)S(1)} %bitcast.12), channel_id=1, replica_groups=mesh['lon'=32,'lat'=16] {'lat'}, dimensions={0} | all-to-all | bytes 196608 | tf_op jit(solution)/shard_map/all_to_all | solution.py:480
  76.4 0.7 shard_map.141
  77.1 10.1 %all-to-all-start.1 = ((bf16[32,24,128]{2,1,0:T(8,128)(2,1)}), bf16[32,24,128]{2,1,0:T(8,128)(2,1)S(1)}, u32[]{:S(2)}, u32[]{:S(2)}) async-start(bf16[32,24,128]{2,1,0:T(8,128)(2,1)} %shard_map.141), calls=%async_computation.1 | async-start | bytes 393216 | tf_op jit(solution)/shard_map/all_to_all | solution.py:482
  87.1 2.1 %collective-permute-start.6 = (bf16[96,128]{1,0:T(8,128)(2,1)S(1)}, bf16[96,128]{1,0:T(8,128)(2,1)S(1)}, u32[]{:S(2)}, u32[]{:S(2)}) collective-permute-start(bf16[96,128]{1,0:T(8,128)(2,1)S(1)} %get-tuple-element.47), channel_id=1, source_target_pairs={{0,16},{16,0},{32,48},{48,32},{64,80},{80,64},{96,112},{112,96},{1... | collective-permute-start | bytes 73736 | tf_op jit(solution)/shard_map/ppermute | solution.py:385
  89.3 3.5 %collective-permute-start.7 = (bf16[96,128]{1,0:T(8,128)(2,1)S(1)}, bf16[96,128]{1,0:T(8,128)(2,1)S(1)}, u32[]{:S(2)}, u32[]{:S(2)}) collective-permute-start(bf16[96,128]{1,0:T(8,128)(2,1)S(1)} %get-tuple-element.48), channel_id=1, source_target_pairs={{0,496},{16,32},{32,16},{48,64},{64,48},{80,96},{96,80},{112,128},... | collective-permute-start | bytes 73736 | tf_op jit(solution)/shard_map/ppermute | solution.py:384
  92.8 0.0 collective-permute-done.6.refs_3_.refs_1_
  92.8 2.3 %collective-permute-done.7.refs_4_.refs_2_ = bf16[96,128]{1,0:T(8,128)(2,1)S(1)} collective-permute-done((bf16[96,128]{1,0:T(8,128)(2,1)S(1)}, bf16[96,128]{1,0:T(8,128)(2,1)S(1)}, u32[]{:S(2)}, u32[]{:S(2)}) %collective-permute-start.7) | collective-permute-done | bytes 24608 | tf_op jit(solution)/shard_map/ppermute | solution.py:384
  95.1 3.8 %all-to-all-done.1.refs_0_ = bf16[32,24,128]{2,1,0:T(8,128)(2,1)S(1)} async-done(((bf16[32,24,128]{2,1,0:T(8,128)(2,1)}), bf16[32,24,128]{2,1,0:T(8,128)(2,1)S(1)}, u32[]{:S(2)}, u32[]{:S(2)}) %all-to-all-start.1) | async-done | bytes 196640 | tf_op jit(solution)/shard_map/all_to_all | solution.py:482
  99.0 0.7 shard_map.142
  99.7 3.5 %all-to-all-start.2 = ((f32[16,24,128]{2,1,0:T(8,128)}), f32[16,24,128]{2,1,0:T(8,128)S(1)}, u32[]{:S(2)}, u32[]{:S(2)}) async-start(f32[16,24,128]{2,1,0:T(8,128)} %shard_map.142), calls=%async_computation.2 | async-start | bytes 393216 | tf_op jit(solution)/shard_map/all_to_all | solution.py:486
  103.2 7.9 %shard_map.140 = bf16[96,8,256]{2,1,0:T(8,128)(2,1)} custom-call(bf16[8,96,256]{2,1,0:T(8,128)(2,1)S(1)} %get-tuple-element.39.refs_1_.refs_0_, bf16[3,96,256]{2,1,0:T(8,128)(2,1)S(1)} %get-tuple-element.45.refs_1_, bf16[3,96,256]{2,1,0:T(8,128)(2,1)S(1)} %get-tuple-element.46.refs_2_, bf16[96,128]{1,0:T(8,128)(2,1)S(1)} %collective-permute-done.6.refs_3_.refs_1_, ...), custom_call_target="tpu_custom_call" | custom-call | tf_op jit(solution)/shard_map/pallas_call | solution.py:48
  111.1 2.3 %all-to-all-done.2 = f32[16,24,128]{2,1,0:T(8,128)S(1)} async-done(((f32[16,24,128]{2,1,0:T(8,128)}), f32[16,24,128]{2,1,0:T(8,128)S(1)}, u32[]{:S(2)}, u32[]{:S(2)}) %all-to-all-start.2) | async-done | bytes 196640 | tf_op jit(solution)/shard_map/all_to_all | solution.py:486
  113.4 0.8 shard_map.143
Async XLA Ops:
  2.6 7.4 %collective-permute-start = (bf16[3,96,256]{2,1,0:T(8,128)(2,1)S(1)}, bf16[3,96,256]{2,1,0:T(8,128)(2,1)S(1)}, u32[]{:S(2)}, u32[]{:S(2)}) collective-permute-start(bf16[3,96,256]{2,1,0:T(8,128)(2,1)S(1)} %get-tuple-element.32), channel_id=1, source_target_pairs={{0,1},{1,0},{2,3},{3,2},{4,5},{5,4},{6,7},{7,6},{8,9},{9,8},{10,11... | collective-permute-start | bytes 442376 | tf_op jit(solution)/shard_map/ppermute | solution.py:378
  7.4 2.5 %collective-permute-start.1 = (bf16[3,96,256]{2,1,0:T(8,128)(2,1)S(1)}, bf16[3,96,256]{2,1,0:T(8,128)(2,1)S(1)}, u32[]{:S(2)}, u32[]{:S(2)}) collective-permute-start(bf16[3,96,256]{2,1,0:T(8,128)(2,1)S(1)} %get-tuple-element.33), channel_id=1, source_target_pairs={{1,2},{2,1},{3,4},{4,3},{5,6},{6,5},{7,8},{8,7},{9,10},{10,9},{11,... | collective-permute-start | bytes 442376 | tf_op jit(solution)/shard_map/ppermute | solution.py:377
  10.9 10.4 %collective-permute-start.2 = (bf16[96,128]{1,0:T(8,128)(2,1)S(1)}, bf16[96,128]{1,0:T(8,128)(2,1)S(1)}, u32[]{:S(2)}, u32[]{:S(2)}) collective-permute-start(bf16[96,128]{1,0:T(8,128)(2,1)S(1)} %get-tuple-element.36), channel_id=1, source_target_pairs={{0,16},{16,0},{32,48},{48,32},{64,80},{80,64},{96,112},{112,96},{1... | collective-permute-start | bytes 73736 | tf_op jit(solution)/shard_map/ppermute | solution.py:385
  19.3 5.1 %collective-permute-start.3 = (bf16[96,128]{1,0:T(8,128)(2,1)S(1)}, bf16[96,128]{1,0:T(8,128)(2,1)S(1)}, u32[]{:S(2)}, u32[]{:S(2)}) collective-permute-start(bf16[96,128]{1,0:T(8,128)(2,1)S(1)} %get-tuple-element.37), channel_id=1, source_target_pairs={{0,496},{16,32},{32,16},{48,64},{64,48},{80,96},{96,80},{112,128},... | collective-permute-start | bytes 73736 | tf_op jit(solution)/shard_map/ppermute | solution.py:384
  36.5 15.9 %collective-permute-start.4 = (bf16[3,96,256]{2,1,0:T(8,128)(2,1)S(1)}, bf16[3,96,256]{2,1,0:T(8,128)(2,1)S(1)}, u32[]{:S(2)}, u32[]{:S(2)}) collective-permute-start(bf16[3,96,256]{2,1,0:T(8,128)(2,1)S(1)} %get-tuple-element.40), channel_id=1, source_target_pairs={{0,1},{1,0},{2,3},{3,2},{4,5},{5,4},{6,7},{7,6},{8,9},{9,8},{10,11... | collective-permute-start | bytes 442376 | tf_op jit(solution)/shard_map/ppermute | solution.py:378
  42.9 9.4 %collective-permute-start.5 = (bf16[3,96,256]{2,1,0:T(8,128)(2,1)S(1)}, bf16[3,96,256]{2,1,0:T(8,128)(2,1)S(1)}, u32[]{:S(2)}, u32[]{:S(2)}) collective-permute-start(bf16[3,96,256]{2,1,0:T(8,128)(2,1)S(1)} %get-tuple-element.41), channel_id=1, source_target_pairs={{1,2},{2,1},{3,4},{4,3},{5,6},{6,5},{7,8},{8,7},{9,10},{10,9},{11,... | collective-permute-start | bytes 442376 | tf_op jit(solution)/shard_map/ppermute | solution.py:377
  77.1 21.9 %all-to-all-start.1 = ((bf16[32,24,128]{2,1,0:T(8,128)(2,1)}), bf16[32,24,128]{2,1,0:T(8,128)(2,1)S(1)}, u32[]{:S(2)}, u32[]{:S(2)}) async-start(bf16[32,24,128]{2,1,0:T(8,128)(2,1)} %shard_map.141), calls=%async_computation.1 | async-start | bytes 393216 | tf_op jit(solution)/shard_map/all_to_all | solution.py:482
  87.1 5.6 %collective-permute-start.6 = (bf16[96,128]{1,0:T(8,128)(2,1)S(1)}, bf16[96,128]{1,0:T(8,128)(2,1)S(1)}, u32[]{:S(2)}, u32[]{:S(2)}) collective-permute-start(bf16[96,128]{1,0:T(8,128)(2,1)S(1)} %get-tuple-element.47), channel_id=1, source_target_pairs={{0,16},{16,0},{32,48},{48,32},{64,80},{80,64},{96,112},{112,96},{1... | collective-permute-start | bytes 73736 | tf_op jit(solution)/shard_map/ppermute | solution.py:385
  89.3 5.8 %collective-permute-start.7 = (bf16[96,128]{1,0:T(8,128)(2,1)S(1)}, bf16[96,128]{1,0:T(8,128)(2,1)S(1)}, u32[]{:S(2)}, u32[]{:S(2)}) collective-permute-start(bf16[96,128]{1,0:T(8,128)(2,1)S(1)} %get-tuple-element.48), channel_id=1, source_target_pairs={{0,496},{16,32},{32,16},{48,64},{64,48},{80,96},{96,80},{112,128},... | collective-permute-start | bytes 73736 | tf_op jit(solution)/shard_map/ppermute | solution.py:384
  99.7 13.8 %all-to-all-start.2 = ((f32[16,24,128]{2,1,0:T(8,128)}), f32[16,24,128]{2,1,0:T(8,128)S(1)}, u32[]{:S(2)}, u32[]{:S(2)}) async-start(f32[16,24,128]{2,1,0:T(8,128)} %shard_map.142), calls=%async_computation.2 | async-start | bytes 393216 | tf_op jit(solution)/shard_map/all_to_all | solution.py:486

commit v5 on v4

--- a/solution.py
+++ b/solution.py
@@ -80,18 +80,21 @@
     return jnp.where(jnp.broadcast_to(flag, yes.shape) > 0, yes, no)
 
 
+def split_ends(m_ref, even, inner_ref, outer_ref):
+    rows = m_ref.shape[0]
+    for k in range(RING):
+        first, last = m_ref[k].astype(F32), m_ref[rows - RING + k].astype(F32)
+        inner_ref[k] = choose(even, last, first).astype(BF16)
+        outer_ref[k] = choose(even, first, last).astype(BF16)
+
+
 def rows_body(settle, f_ref, mask_ref, place_ref, m_ref, inner_ref, outer_ref, flat):
     channels, rows, cols = f_ref.shape
     settle()
     spread(flat, f_ref[...].astype(F32) * mask_ref[...].astype(F32)[None])
-    kept = [row_of(flat, i, channels, rows) for i in range(rows)]
     for i in range(rows):
-        m_ref[i] = kept[i].astype(BF16)
-    even = place_ref[0]
-    for k in range(RING):
-        first, last = kept[k], kept[rows - RING + k]
-        inner_ref[k] = choose(even, last, first).astype(BF16)
-        outer_ref[k] = choose(even, first, last).astype(BF16)
+        m_ref[i] = row_of(flat, i, channels, rows).astype(BF16)
+    split_ends(m_ref, place_ref[0], inner_ref, outer_ref)
 
 
 def strips_body(
@@ -166,11 +169,11 @@
     if step == 0:
         return tiles[:-1]
     count = len(tiles)
+    shift = 128 - step if step > 0 else -step
+    turned = [jnp.zeros((8, 128), F32) if t is None else pltpu.roll(t, shift, 1) for t in tiles]
     if step > 0:
-        turned = [pltpu.roll(t, 128 - step, 1) for t in tiles]
         keep = lane < 128 - step
         return [jnp.where(keep, turned[t], turned[t + 1]) for t in range(count - 1)]
-    turned = [pltpu.roll(t, -step, 1) for t in tiles]
     keep = lane >= -step
     return [jnp.where(keep, turned[t], turned[t - 1]) for t in range(count - 1)]
 
@@ -185,40 +188,129 @@
     return jnp.broadcast_to(weights[:, index : index + 1], (8, 128))
 
 
-def correlate(ext, c0, rows, pairs, lane, weights, top):
-    summed = [[None] * pairs for _ in range(rows)]
+def correlate(read, span, rows, lane, weights, flipped, top, summed):
     for b in range(7):
-        if top is None:
-            taps = [tap(weights, a * 7 + b) for a in range(7)]
-            far = taps
-        else:
-            taps = [tap(weights, 48 - a * 7 - b) for a in range(7)]
+        taps = [tap(weights, 48 - a * 7 - b if flipped else a * 7 + b) for a in range(7)]
+        far = taps
+        if top is not None:
             far = [jnp.where(top, tap(weights, a * 7 + b), taps[a]) for a in range(7)]
-        for r in range(rows + 2 * RING):
-            tiles = [ext[r, pl.ds(c0, 8), t * 128 : t * 128 + 128] for t in range(pairs + 1)]
-            wins = windows(tiles, b - RING, lane)
+        for r in span:
+            wins = windows(read(r), b - RING, lane)
             for a in range(7):
                 i = r - a
                 if 0 <= i < rows:
                     weight = far[a] if r >= rows + RING else taps[a]
-                    for t in range(pairs):
-                        term = weight * wins[t]
+                    for t, win in enumerate(wins):
+                        term = weight * win
                         old = summed[i][t]
                         summed[i][t] = term if old is None else old + term
     return summed
 
 
+def edges(before, after, rows, lane, weights, flipped, top):
+    spot = lane % RING
+    left = jnp.zeros((8, 128), F32)
+    right = jnp.zeros((8, 128), F32)
+    for a in range(7):
+        for b in (0, 1, 2, 4, 5, 6):
+            weight = tap(weights, 48 - a * 7 - b if flipped else a * 7 + b)
+            if top is not None and a > RING:
+                beyond = top & (lane >= RING * (rows + RING - a))
+                weight = jnp.where(beyond, tap(weights, a * 7 + b), weight)
+            back = -(RING * a + b) % 128 if b < RING else -(RING * a + b - 6) % 128
+            strip = before if b < RING else after
+            moved = pltpu.roll(strip, back, 1) if back else strip
+            if b < RING:
+                left = left + jnp.where(spot <= 2 - b, weight * moved, 0.0)
+            else:
+                right = right + jnp.where(spot >= 6 - b, weight * moved, 0.0)
+    return left, right
+
+
+def place_edges(left, right, i, lane):
+    head = pltpu.roll(left, 128 - RING * i, 1) if i else left
+    tail = pltpu.roll(right, 128 - RING - RING * i, 1)
+    return jnp.where(lane < RING, head, 0.0), jnp.where(lane >= 128 - RING, tail, 0.0)
+
+
+def own_body(flipped, settle, m_ref, dw_ref, conv_ref, wide, taps):
+    rows, channels, cols = m_ref.shape
+    pairs = cols // 128
+    wide[...] = m_ref[...].astype(F32)
+    settle()
+    taps[...] = tap_columns(dw_ref)
+
+    def step(ct, carry):
+        c0 = pl.multiple_of(ct * 8, 8)
+
+        def read(r):
+            tiles = [wide[r - RING, pl.ds(c0, 8), t * 128 : t * 128 + 128] for t in range(pairs)]
+            return tiles + [None]
+
+        blank = [[None] * pairs for _ in range(rows)]
+        span = range(RING, rows + RING)
+        weights = taps[pl.ds(c0, 8), :]
+        summed = correlate(read, span, rows, lanes(), weights, flipped, None, blank)
+        for i in range(rows):
+            for t in range(pairs):
+                conv_ref[i, pl.ds(c0, 8), t * 128 : t * 128 + 128] = summed[i][t]
+        return carry
+
+    lax.fori_loop(0, channels // 8, step, 0)
+
+
+def with_ends(conv_ref, wide, c0, lane, weights, flipped, top):
+    rows, channels, cols = conv_ref.shape
+    pairs = cols // 128
+
+    def read(r):
+        at = r if r < RING else r - rows
+        tiles = [wide[at, pl.ds(c0, 8), t * 128 : t * 128 + 128] for t in range(pairs)]
+        return tiles + [None]
+
+    summed = [
+        [conv_ref[i, pl.ds(c0, 8), t * 128 : t * 128 + 128] for t in range(pairs)]
+        for i in range(rows)
+    ]
+    span = [*range(RING), *range(rows + RING, rows + 2 * RING)]
+    return correlate(read, span, rows, lane, weights, flipped, top, summed)
+
+
+def ends_body(settle, south_ref, halo_ref, conv_ref, dw_ref, out_ref, wide, taps):
+    rows, channels, cols = conv_ref.shape
+    wide[0:RING] = south_ref[...].astype(F32)
+    wide[RING : 2 * RING] = halo_ref[...].astype(F32)
+    settle()
+    taps[...] = tap_columns(dw_ref)
+
+    def step(ct, carry):
+        c0 = pl.multiple_of(ct * 8, 8)
+        summed = with_ends(conv_ref, wide, c0, lanes(), taps[pl.ds(c0, 8), :], False, None)
+        for i in range(rows):
+            for t in range(cols // 128):
+                out_ref[i, pl.ds(c0, 8), t * 128 : t * 128 + 128] = summed[i][t]
+        return carry
+
+    lax.fori_loop(0, channels // 8, step, 0)
+
+
+def split_sides(sides, near_ref, far_ref, lon_even):
+    near = near_ref[...].astype(F32)
+    far = far_ref[...].astype(F32)
+    sides[0] = choose(lon_even, far, near)
+    sides[1] = choose(lon_even, near, far)
+
+
 def block_body(
-    settle, m_ref, south_ref, halo_ref, near_ref, far_ref, ct_ref, mask_ref,
+    settle, m_ref, conv_ref, near_ref, far_ref, ct_ref, mask_ref,
     dw_ref, gain_ref, w_in_ref, b_ref, w_out_ref, place_ref,
-    out_ref, g_ref, inner_ref, outer_ref, wide_ref, tail_ref, ext_ref,
-    conv, flat, act, back, sca, pre, b_acc, gain_acc, taps,
+    out_ref, g_ref, inner_ref, outer_ref, wide_ref, tail_ref,
+    conv, flat, act, back, sca, pre, b_acc, gain_acc, taps, sides,
 ):
-    ext = ext_ref
     rows, channels, cols = m_ref.shape
     hidden = w_out_ref.shape[0]
     pairs = cols // 128
-    fill(ext, m_ref, south_ref, halo_ref, near_ref, far_ref, place_ref[2])
+    split_sides(sides, near_ref, far_ref, place_ref[2])
     settle()
     taps[...] = tap_columns(dw_ref)
     sea = mask_ref[...].astype(F32)
@@ -229,10 +321,18 @@
     def conv_step(ct, carry):
         c0 = pl.multiple_of(ct * 8, 8)
         lane = lanes()
-        summed = correlate(ext, c0, rows, pairs, lane, taps[pl.ds(c0, 8), :], None)
+        before, after = sides[0, pl.ds(c0, 8), :], sides[1, pl.ds(c0, 8), :]
+        weights = taps[pl.ds(c0, 8), :]
+        left, right = edges(before, after, rows, lane, weights, False, None)
         for i in range(rows):
+            head, tail = place_edges(left, right, i, lane)
             for t in range(pairs):
-                conv[i, pl.ds(c0, 8), t * 128 : t * 128 + 128] = summed[i][t]
+                tile = conv_ref[i, pl.ds(c0, 8), t * 128 : t * 128 + 128]
+                if t == 0:
+                    tile = tile + head
+                if t == pairs - 1:
+                    tile = tile + tail
+                conv[i, pl.ds(c0, 8), t * 128 : t * 128 + 128] = tile
         return carry
 
     lax.fori_loop(0, channels // 8, conv_step, 0)
@@ -281,11 +381,7 @@
         )
         g_ref[i] = grad.astype(BF16)
 
-    even = place_ref[0]
-    for k in range(RING):
-        first, last = g_ref[k].astype(F32), g_ref[rows - RING + k].astype(F32)
-        inner_ref[k] = choose(even, last, first).astype(BF16)
-        outer_ref[k] = choose(even, first, last).astype(BF16)
+    split_ends(g_ref, place_ref[0], inner_ref, outer_ref)
     out_ref[...] = (gather(flat, channels, rows) * sea[None]).astype(BF16)
     over_cells = (((1,), (1,)), ((), ()))
     w_in_sum = lax.dot_general(sca[...], pre[...], over_cells, preferred_element_type=F32)
@@ -305,9 +401,13 @@
     tail_ref[...] = tail
 
 
-def kernel_body(shift, ext, g_ref, wide_ref, tail_ref, sums_ref, tail, grid):
+def kernel_body(
+    shift, m_ref, south_ref, halo_ref, near_ref, far_ref, g_ref, wide_ref, tail_ref, place_ref,
+    sums_ref, tail, grid, ext,
+):
     rows, channels, cols = g_ref.shape
     pairs = cols // 128
+    fill(ext, m_ref, south_ref, halo_ref, near_ref, far_ref, place_ref[2])
     grid[...] = g_ref[...].astype(F32)
 
     def kernel_step(ct, carry):
@@ -342,12 +442,14 @@
 
 
 def back_body(
-    settle, g_ref, south_ref, halo_ref, near_ref, far_ref, ct_ref, mask_ref, dw_ref, place_ref,
-    out_ref, ext, flat, taps,
+    settle, conv_ref, south_ref, halo_ref, near_ref, far_ref, ct_ref, mask_ref, dw_ref, place_ref,
+    out_ref, wide, flat, taps, sides,
 ):
-    rows, channels, cols = g_ref.shape
+    rows, channels, cols = conv_ref.shape
     pairs = cols // 128
-    fill(ext, g_ref, south_ref, halo_ref, near_ref, far_ref, place_ref[2])
+    wide[0:RING] = south_ref[...].astype(F32)
+    wide[RING : 2 * RING] = halo_ref[...].astype(F32)
+    split_sides(sides, near_ref, far_ref, place_ref[2])
     settle()
     taps[...] = tap_columns(dw_ref)
 
@@ -355,10 +457,19 @@
         c0 = pl.multiple_of(ct * 8, 8)
         lane = lanes()
         top = jnp.broadcast_to(place_ref[1], (8, 128)) > 0
-        summed = correlate(ext, c0, rows, pairs, lane, taps[pl.ds(c0, 8), :], top)
+        weights = taps[pl.ds(c0, 8), :]
+        before, after = sides[0, pl.ds(c0, 8), :], sides[1, pl.ds(c0, 8), :]
+        left, right = edges(before, after, rows, lane, weights, True, top)
+        summed = with_ends(conv_ref, wide, c0, lane, weights, True, top)
         for i in range(rows):
+            head, tail = place_edges(left, right, i, lane)
             for t in range(pairs):
-                flat[t, pl.ds(c0 * rows + i, 8, stride=rows), :] = summed[i][t]
+                tile = summed[i][t]
+                if t == 0:
+                    tile = tile + head
+                if t == pairs - 1:
+                    tile = tile + tail
+                flat[t, pl.ds(c0 * rows + i, 8, stride=rows), :] = tile
         return carry
 
     lax.fori_loop(0, channels // 8, step, 0)
@@ -437,18 +548,29 @@
         scratch=[flat],
     )
     inner, outer = lat_halo(inner, outer)
+    columns = pltpu.VMEM((channels, 128), F32)
+    sides = pltpu.VMEM((2, channels, 128), F32)
+    sums_grid = pltpu.VMEM((rows, channels, cols), F32)
+    ends = pltpu.VMEM((2 * RING, channels, cols), F32)
+    (conv,) = call(
+        functools.partial(own_body, False), [sums_grid], [masked], [taps],
+        scratch=[sums_grid, columns],
+    )
     south, north, near, far = call(
-        strips_body, [near_ring, near_ring, strip, strip], [masked, inner, outer], (), [place]
+        strips_body, [near_ring, near_ring, strip, strip], [masked, inner, outer], (), [place],
+        waits=[conv],
     )
     near, far = lon_halo(near, far)
-    columns = pltpu.VMEM((channels, 128), F32)
-    output, grads, inner, outer, wide, tail, ext_rows = call(
+    (conv,) = call(
+        ends_body, [sums_grid], [south, north, conv], [taps], scratch=[ends, columns]
+    )
+    output, grads, inner, outer, wide, tail = call(
         block_body,
         [
             whole, held(grid), near_ring, near_ring,
-            pltpu.VMEM((height - channels, 128), BF16), columns, ext,
+            pltpu.VMEM((height - channels, 128), BF16), columns,
         ],
-        [masked, south, north, near, far],
+        [masked, conv, near, far],
         [
             cotangent, land_mask, taps, gain.reshape(1, channels), w_in,
             b_in.reshape(1, hidden), w_out,
@@ -464,29 +586,37 @@
             pltpu.VMEM((hidden, 128), F32),
             columns,
             columns,
+            sides,
         ],
     )
     inner, outer = lat_halo(inner, outer)
     (sums,) = call(
-        functools.partial(kernel_body, hidden - 128), [near_sums], [ext_rows, grads, wide, tail],
-        scratch=[columns, pltpu.VMEM((rows, channels, cols), F32)],
+        functools.partial(kernel_body, hidden - 128), [near_sums],
+        [masked, south, north, near, far, grads, wide, tail], (), [place],
+        scratch=[columns, sums_grid, ext],
     )
     south, north, near, far, sums = call(
         strips_and_sums_body, [near_ring, near_ring, strip, strip, near_sums],
         [grads, inner, outer, sums], (), [place],
     )
-    near, far = lon_halo(near, far)
     size = height // n_lat
     pieces = lax.all_to_all(sums.reshape(n_lat, size, 128), "lat", 0, 0, tiled=True)
-    (pieces,) = call(spread_body, [pltpu.VMEM((n_lon, size, 128), BF16)], [pieces])
+    (conv,) = call(
+        functools.partial(own_body, True), [sums_grid], [grads], [taps],
+        scratch=[sums_grid, columns], waits=[near],
+    )
+    (pieces,) = call(
+        spread_body, [pltpu.VMEM((n_lon, size, 128), BF16)], [pieces], waits=[conv]
+    )
+    near, far = lon_halo(near, far)
     pieces = lax.all_to_all(pieces, "lon", 0, 0, tiled=True)
     (pieces,) = call(
         spread_body, [pltpu.VMEM((n_lat, size, 128), F32)], [pieces], waits=[near, far]
     )
     pieces = lax.all_to_all(pieces, "lat", 0, 0, tiled=True)
     (input_grad,) = call(
-        back_body, [whole], [grads, south, north, near, far], [cotangent, land_mask, taps],
-        [place], scratch=[ext, flat, columns],
+        back_body, [whole], [conv, south, north, near, far], [cotangent, land_mask, taps],
+        [place], scratch=[ends, flat, columns, sides],
     )
     scale = float(cells * n_lat * n_lon) ** -0.5
     w_in_grad, w_out_grad, dw_grad, gain_grad, b_grad = call(

time: 115 us -> 115 us (level)
  blocking collectives: 23 us -> 0 us
  starting transfers between devices: 42.2 us -> 58.7 us
  Pallas kernels: 34.5 us -> 43.8 us
  waiting for transfers between devices: 13.6 us -> 10.3 us
    all_to_all x1 -> x0, blocking collectives: 23 us -> none  [shards(): lax.all_to_all(sums.reshape(n_lat, size, 128), 'lat', 0, 0, tiled=True)]
    all_to_all x0 -> x1, starting transfers between devices: none -> 15.1 us  [shards(): lax.all_to_all(sums.reshape(n_lat, size, 128), 'lat', 0, 0, tiled=True)]
    pallas_call x9 -> x12, Pallas kernels: 34.5 us -> 43.8 us  [call(): pl.pallas_call(run, out_shape=outs, in_specs=specs, out_specs=[pl.BlockSp...]
    ppermute x2, waiting for transfers between devices: 5.56 us -> 0.01 us  [lon_halo(): lax.ppermute(far, 'lon', [(i, (i - 1 + 2 * (i % 2)) % n_lon) for i in ran...]
    all_to_all x0 -> x1, waiting for transfers between devices: none -> 4.04 us  [shards(): lax.all_to_all(sums.reshape(n_lat, size, 128), 'lat', 0, 0, tiled=True)]
    all_to_all x1, waiting for transfers between devices: 3.85 us -> 1.08 us  [shards(): pieces = lax.all_to_all(pieces, 'lon', 0, 0, tiled=True)]
    all_to_all x1, waiting for transfers between devices: 2.33 us -> 4.33 us  [shards(): pieces = lax.all_to_all(pieces, 'lat', 0, 0, tiled=True)]
    ppermute x2, starting transfers between devices: 10.6 us -> 12.5 us  [lon_halo(): near = lax.ppermute(near, 'lon', [(i, i ^ 1) for i in range(n_lon)])]
  transfers between devices with their start and end apart: 10 -> 11, of which waited for: 5 -> 4; matrix products, arithmetic and copies ran while one was open for 0% -> 0% of each run, Pallas kernels for 15% -> 24%
where the time goes in v5:
time: 115 us; the launch traced here: 114 us
  starting transfers between devices  58.7 us (51%)
  Pallas kernels  43.8 us (38%)
  waiting for transfers between devices  10.3 us (9%)
    pallas_call x12, Pallas kernels, call(): pl.pallas_call(run, out_shape=outs, in_specs=specs, out_specs=[pl.BlockSp...  43.8 us
    all_to_all x1, starting transfers between devices, shards(): lax.all_to_all(sums.reshape(n_lat, size, 128), 'lat', 0, 0, tiled=True)  15.1 us
    ppermute x2, starting transfers between devices, lon_halo(): near = lax.ppermute(near, 'lon', [(i, i ^ 1) for i in range(n_lon)])  12.5 us
    ppermute x2, starting transfers between devices, lat_halo(): inner = lax.ppermute(inner, 'lat', [(i, i ^ 1) for i in range(n_lat)])  11.3 us
    all_to_all x1, starting transfers between devices, shards(): pieces = lax.all_to_all(pieces, 'lon', 0, 0, tiled=True)  9.53 us
    ppermute x2, starting transfers between devices, lon_halo(): lax.ppermute(far, 'lon', [(i, (i - 1 + 2 * (i % 2)) % n_lon) for i in ran...  5.46 us
    all_to_all x1, waiting for transfers between devices, shards(): pieces = lax.all_to_all(pieces, 'lat', 0, 0, tiled=True)  4.33 us
    all_to_all x1, waiting for transfers between devices, shards(): lax.all_to_all(sums.reshape(n_lat, size, 128), 'lat', 0, 0, tiled=True)  4.04 us
  transfers between devices with their start and end apart: 11, of which 4 were waited for; matrix products, arithmetic and copies ran while one was open for 0% of the time, Pallas kernels for 24%

profile of v5, /device:TPU:1, one launch (start us, length us, event | category | flops | bytes accessed | tf_op | source)
XLA Modules:
  0.0 113.7 jit_solution(7608097176144250059)
XLA Ops:
  0.7 0.1 pad_add_fusion.refs_2_.refs_3_.refs_11_.refs_8_.refs_4_
  0.7 1.8 %shard_map.135 = (bf16[8,96,256]{2,1,0:T(8,128)(2,1)S(1)}, bf16[3,96,256]{2,1,0:T(8,128)(2,1)S(1)}, bf16[3,96,256]{2,1,0:T(8,128)(2,1)S(1)}) custom-call(bf16[96,8,256]{2,1,0:T(8,128)(2,1)} %refs_0_.1, s32[8,256]{1,0:T(8,128)} %refs_6_.1, s32[3]{0:T(128)S(1)} %pad_add_fusion.refs_2_.refs_3_.refs_11_.refs_8_.refs_4_), custom_call_target="tpu_custom_call" | custom-call | tf_op jit(solution)/shard_map/pallas_call | solution.py:48
  2.6 4.8 %collective-permute-start = (bf16[3,96,256]{2,1,0:T(8,128)(2,1)S(1)}, bf16[3,96,256]{2,1,0:T(8,128)(2,1)S(1)}, u32[]{:S(2)}, u32[]{:S(2)}) collective-permute-start(bf16[3,96,256]{2,1,0:T(8,128)(2,1)S(1)} %get-tuple-element.31), channel_id=1, source_target_pairs={{0,1},{1,0},{2,3},{3,2},{4,5},{5,4},{6,7},{7,6},{8,9},{9,8},{10,11... | collective-permute-start | bytes 442376 | tf_op jit(solution)/shard_map/ppermute | solution.py:489
  7.4 0.7 collective-permute-start.1
  8.1 4.1 %shard_map.136.refs_4_.refs_2_ = f32[8,96,256]{2,1,0:T(8,128)S(1)} custom-call(bf16[8,96,256]{2,1,0:T(8,128)(2,1)S(1)} %get-tuple-element.30.refs_0_, f32[7,7,96]{2,1,0:T(8,128)} %bitcast.12), custom_call_target="tpu_custom_call" | custom-call | tf_op jit(solution)/shard_map/pallas_call | solution.py:48
  12.2 0.0 collective-permute-done.refs_1_
  12.2 0.0 collective-permute-done.1.refs_2_
  12.2 0.9 shard_map.137
  13.2 6.1 %collective-permute-start.2 = (bf16[96,128]{1,0:T(8,128)(2,1)S(1)}, bf16[96,128]{1,0:T(8,128)(2,1)S(1)}, u32[]{:S(2)}, u32[]{:S(2)}) collective-permute-start(bf16[96,128]{1,0:T(8,128)(2,1)S(1)} %get-tuple-element.35), channel_id=1, source_target_pairs={{0,16},{16,0},{32,48},{48,32},{64,80},{80,64},{96,112},{112,96},{1... | collective-permute-start | bytes 73736 | tf_op jit(solution)/shard_map/ppermute | solution.py:496
  19.3 1.9 %collective-permute-start.3 = (bf16[96,128]{1,0:T(8,128)(2,1)S(1)}, bf16[96,128]{1,0:T(8,128)(2,1)S(1)}, u32[]{:S(2)}, u32[]{:S(2)}) collective-permute-start(bf16[96,128]{1,0:T(8,128)(2,1)S(1)} %get-tuple-element.36), channel_id=1, source_target_pairs={{0,496},{16,32},{32,16},{48,64},{64,48},{80,96},{96,80},{112,128},... | collective-permute-start | bytes 73736 | tf_op jit(solution)/shard_map/ppermute | solution.py:495
  21.3 3.7 %shard_map.138.refs_1_ = f32[8,96,256]{2,1,0:T(8,128)S(1)} custom-call(bf16[3,96,256]{2,1,0:T(8,128)(2,1)S(1)} %get-tuple-element.33.refs_0_.refs_1_, bf16[3,96,256]{2,1,0:T(8,128)(2,1)S(1)} %get-tuple-element.34.refs_1_.refs_2_, f32[8,96,256]{2,1,0:T(8,128)S(1)} %shard_map.136.refs_4_.refs_2_, f32[7,7,96]{2,1,0:T(8,128)} %bitcast.13), custom_call_target="tpu_custom_call" | custom-call | tf_op jit(solution)/shard_map/pallas_call | solution.py:48
  25.0 0.0 collective-permute-done.2.refs_2_.refs_3_
  25.0 0.0 collective-permute-done.3.refs_3_.refs_4_
  25.0 9.8 %shard_map.139 = (bf16[96,8,256]{2,1,0:T(8,128)(2,1)}, bf16[8,96,256]{2,1,0:T(8,128)(2,1)S(1)}, bf16[3,96,256]{2,1,0:T(8,128)(2,1)S(1)}, bf16[3,96,256]{2,1,0:T(...) custom-call(bf16[8,96,256]{2,1,0:T(8,128)(2,1)S(1)} %get-tuple-element.30.refs_0_, ...), custom_call_target="tpu_custom_call" | custom-call | tf_op jit(solution)/shard_map/pallas_call | solution.py:48
  34.8 6.5 %collective-permute-start.4 = (bf16[3,96,256]{2,1,0:T(8,128)(2,1)S(1)}, bf16[3,96,256]{2,1,0:T(8,128)(2,1)S(1)}, u32[]{:S(2)}, u32[]{:S(2)}) collective-permute-start(bf16[3,96,256]{2,1,0:T(8,128)(2,1)S(1)} %get-tuple-element.39), channel_id=1, source_target_pairs={{0,1},{1,0},{2,3},{3,2},{4,5},{5,4},{6,7},{7,6},{8,9},{9,8},{10,11... | collective-permute-start | bytes 442376 | tf_op jit(solution)/shard_map/ppermute | solution.py:489
  41.3 0.7 collective-permute-start.5
  42.0 9.5 %shard_map.140.refs_3_ = bf16[384,128]{1,0:T(8,128)(2,1)S(1)} custom-call(bf16[8,96,256]{2,1,0:T(8,128)(2,1)S(1)} %get-tuple-element.30.refs_0_, bf16[3,96,256]{2,1,0:T(8,128)(2,1)S(1)} %get-tuple-element.33.refs_0_.refs_1_, bf16[3,96,256]{2,1,0:T(8,128)(2,1)S(1)} %get-tuple-element.34.refs_1_.refs_2_, ...), custom_call_target="tpu_custom_call" | custom-call | tf_op jit(solution)/shard_map/pallas_call | solution.py:48
  51.5 0.0 collective-permute-done.4.refs_1_
  51.6 0.0 collective-permute-done.5.refs_2_
  51.6 1.5 %shard_map.141 = (bf16[3,96,256]{2,1,0:T(8,128)(2,1)S(1)}, bf16[3,96,256]{2,1,0:T(8,128)(2,1)S(1)}, bf16[96,128]{1,0:T(8,128)(2,1)S(1)}, bf16[96,128]{1,0:T(8,128)(2,1)S(1)}, bf16[384,128]{1,0:T(8,128)(2,1)}) custom-call(bf16[8,96,256]{2,1,0:T(8,128)(2,1)S(1)} %get-tuple-element.38.refs_5_.refs_0_, bf16[3,96,256]{2,1,0:T(8,128)(2,1)S(1)} %collective-permute-done.4.refs_1_, ...), custom_call_target="tpu_custom_call" | custom-call | tf_op jit(solution)/shard_map/pallas_call | solution.py:48
  53.1 15.1 %all-to-all-start = ((bf16[16,24,128]{2,1,0:T(8,128)(2,1)}), bf16[16,24,128]{2,1,0:T(8,128)(2,1)S(1)}, u32[]{:S(2)}, u32[]{:S(2)}) async-start(bf16[16,24,128]{2,1,0:T(8,128)(2,1)} %bitcast.6), calls=%async_computation | async-start | bytes 196608 | tf_op jit(solution)/shard_map/all_to_all | solution.py:603
  68.1 4.1 %shard_map.142.refs_0_.refs_1_ = f32[8,96,256]{2,1,0:T(8,128)S(1)} custom-call(bf16[8,96,256]{2,1,0:T(8,128)(2,1)S(1)} %get-tuple-element.38.refs_5_.refs_0_, f32[7,7,96]{2,1,0:T(8,128)} %bitcast.15, bf16[96,128]{1,0:T(8,128)(2,1)S(1)} %get-tuple-element.43.refs_2_), custom_call_target="tpu_custom_call" | custom-call | tf_op jit(solution)/shard_map/pallas_call | solution.py:48
  72.3 4.0 %all-to-all-done.refs_0_ = bf16[16,24,128]{2,1,0:T(8,128)(2,1)S(1)} async-done(((bf16[16,24,128]{2,1,0:T(8,128)(2,1)}), bf16[16,24,128]{2,1,0:T(8,128)(2,1)S(1)}, u32[]{:S(2)}, u32[]{:S(2)}) %all-to-all-start) | async-done | bytes 98336 | tf_op jit(solution)/shard_map/all_to_all | solution.py:603
  76.3 0.7 shard_map.144
  77.0 9.5 %all-to-all-start.1 = ((bf16[32,24,128]{2,1,0:T(8,128)(2,1)}), bf16[32,24,128]{2,1,0:T(8,128)(2,1)S(1)}, u32[]{:S(2)}, u32[]{:S(2)}) async-start(bf16[32,24,128]{2,1,0:T(8,128)(2,1)} %shard_map.144), calls=%async_computation.1 | async-start | bytes 393216 | tf_op jit(solution)/shard_map/all_to_all | solution.py:612
  86.6 3.5 %collective-permute-start.7 = (bf16[96,128]{1,0:T(8,128)(2,1)S(1)}, bf16[96,128]{1,0:T(8,128)(2,1)S(1)}, u32[]{:S(2)}, u32[]{:S(2)}) collective-permute-start(bf16[96,128]{1,0:T(8,128)(2,1)S(1)} %get-tuple-element.46), channel_id=1, source_target_pairs={{0,496},{16,32},{32,16},{48,64},{64,48},{80,96},{96,80},{112,128},... | collective-permute-start | bytes 73736 | tf_op jit(solution)/shard_map/ppermute | solution.py:495
  90.1 6.4 %collective-permute-start.6 = (bf16[96,128]{1,0:T(8,128)(2,1)S(1)}, bf16[96,128]{1,0:T(8,128)(2,1)S(1)}, u32[]{:S(2)}, u32[]{:S(2)}) collective-permute-start(bf16[96,128]{1,0:T(8,128)(2,1)S(1)} %get-tuple-element.43.refs_2_), channel_id=1, source_target_pairs={{0,16},{16,0},{32,48},{48,32},{64,80},{80,64},{96,112},{112,96},{1... | collective-permute-start | bytes 73736 | tf_op jit(solution)/shard_map/ppermute | solution.py:496
  96.5 0.0 collective-permute-done.7.refs_4_.refs_2_
  96.5 0.8 collective-permute-done.6.refs_3_.refs_1_
  97.3 1.1 all-to-all-done.1.refs_0_
  98.4 0.7 shard_map.145
  99.1 3.5 %all-to-all-start.2 = ((f32[16,24,128]{2,1,0:T(8,128)}), f32[16,24,128]{2,1,0:T(8,128)S(1)}, u32[]{:S(2)}, u32[]{:S(2)}) async-start(f32[16,24,128]{2,1,0:T(8,128)} %shard_map.145), calls=%async_computation.2 | async-start | bytes 393216 | tf_op jit(solution)/shard_map/all_to_all | solution.py:616
  102.6 6.0 %shard_map.143 = bf16[96,8,256]{2,1,0:T(8,128)(2,1)} custom-call(f32[8,96,256]{2,1,0:T(8,128)S(1)} %shard_map.142.refs_0_.refs_1_, bf16[3,96,256]{2,1,0:T(8,128)(2,1)S(1)} %get-tuple-element.44.refs_1_, bf16[3,96,256]{2,1,0:T(8,128)(2,1)S(1)} %get-tuple-element.45.refs_2_, bf16[96,128]{1,0:T(8,128)(2,1)S(1)} %collective-permute-done.6.refs_3_.refs_1_, ...), custom_call_target="tpu_custom_call" | custom-call | tf_op jit(solution)/shard_map/pallas_call | solution.py:48
  108.6 4.3 %all-to-all-done.2 = f32[16,24,128]{2,1,0:T(8,128)S(1)} async-done(((f32[16,24,128]{2,1,0:T(8,128)}), f32[16,24,128]{2,1,0:T(8,128)S(1)}, u32[]{:S(2)}, u32[]{:S(2)}) %all-to-all-start.2) | async-done | bytes 196640 | tf_op jit(solution)/shard_map/all_to_all | solution.py:616
  113.0 0.8 shard_map.146
Async XLA Ops:
  2.6 9.7 %collective-permute-start = (bf16[3,96,256]{2,1,0:T(8,128)(2,1)S(1)}, bf16[3,96,256]{2,1,0:T(8,128)(2,1)S(1)}, u32[]{:S(2)}, u32[]{:S(2)}) collective-permute-start(bf16[3,96,256]{2,1,0:T(8,128)(2,1)S(1)} %get-tuple-element.31), channel_id=1, source_target_pairs={{0,1},{1,0},{2,3},{3,2},{4,5},{5,4},{6,7},{7,6},{8,9},{9,8},{10,11... | collective-permute-start | bytes 442376 | tf_op jit(solution)/shard_map/ppermute | solution.py:489
  7.4 4.8 %collective-permute-start.1 = (bf16[3,96,256]{2,1,0:T(8,128)(2,1)S(1)}, bf16[3,96,256]{2,1,0:T(8,128)(2,1)S(1)}, u32[]{:S(2)}, u32[]{:S(2)}) collective-permute-start(bf16[3,96,256]{2,1,0:T(8,128)(2,1)S(1)} %get-tuple-element.32), channel_id=1, source_target_pairs={{1,2},{2,1},{3,4},{4,3},{5,6},{6,5},{7,8},{8,7},{9,10},{10,9},{11,... | collective-permute-start | bytes 442376 | tf_op jit(solution)/shard_map/ppermute | solution.py:488
  13.2 11.8 %collective-permute-start.2 = (bf16[96,128]{1,0:T(8,128)(2,1)S(1)}, bf16[96,128]{1,0:T(8,128)(2,1)S(1)}, u32[]{:S(2)}, u32[]{:S(2)}) collective-permute-start(bf16[96,128]{1,0:T(8,128)(2,1)S(1)} %get-tuple-element.35), channel_id=1, source_target_pairs={{0,16},{16,0},{32,48},{48,32},{64,80},{80,64},{96,112},{112,96},{1... | collective-permute-start | bytes 73736 | tf_op jit(solution)/shard_map/ppermute | solution.py:496
  19.3 5.7 %collective-permute-start.3 = (bf16[96,128]{1,0:T(8,128)(2,1)S(1)}, bf16[96,128]{1,0:T(8,128)(2,1)S(1)}, u32[]{:S(2)}, u32[]{:S(2)}) collective-permute-start(bf16[96,128]{1,0:T(8,128)(2,1)S(1)} %get-tuple-element.36), channel_id=1, source_target_pairs={{0,496},{16,32},{32,16},{48,64},{64,48},{80,96},{96,80},{112,128},... | collective-permute-start | bytes 73736 | tf_op jit(solution)/shard_map/ppermute | solution.py:495
  34.8 16.7 %collective-permute-start.4 = (bf16[3,96,256]{2,1,0:T(8,128)(2,1)S(1)}, bf16[3,96,256]{2,1,0:T(8,128)(2,1)S(1)}, u32[]{:S(2)}, u32[]{:S(2)}) collective-permute-start(bf16[3,96,256]{2,1,0:T(8,128)(2,1)S(1)} %get-tuple-element.39), channel_id=1, source_target_pairs={{0,1},{1,0},{2,3},{3,2},{4,5},{5,4},{6,7},{7,6},{8,9},{9,8},{10,11... | collective-permute-start | bytes 442376 | tf_op jit(solution)/shard_map/ppermute | solution.py:489
  41.3 10.2 %collective-permute-start.5 = (bf16[3,96,256]{2,1,0:T(8,128)(2,1)S(1)}, bf16[3,96,256]{2,1,0:T(8,128)(2,1)S(1)}, u32[]{:S(2)}, u32[]{:S(2)}) collective-permute-start(bf16[3,96,256]{2,1,0:T(8,128)(2,1)S(1)} %get-tuple-element.40), channel_id=1, source_target_pairs={{1,2},{2,1},{3,4},{4,3},{5,6},{6,5},{7,8},{8,7},{9,10},{10,9},{11,... | collective-permute-start | bytes 442376 | tf_op jit(solution)/shard_map/ppermute | solution.py:488
  53.1 23.2 %all-to-all-start = ((bf16[16,24,128]{2,1,0:T(8,128)(2,1)}), bf16[16,24,128]{2,1,0:T(8,128)(2,1)S(1)}, u32[]{:S(2)}, u32[]{:S(2)}) async-start(bf16[16,24,128]{2,1,0:T(8,128)(2,1)} %bitcast.6), calls=%async_computation | async-start | bytes 196608 | tf_op jit(solution)/shard_map/all_to_all | solution.py:603
  77.0 21.4 %all-to-all-start.1 = ((bf16[32,24,128]{2,1,0:T(8,128)(2,1)}), bf16[32,24,128]{2,1,0:T(8,128)(2,1)S(1)}, u32[]{:S(2)}, u32[]{:S(2)}) async-start(bf16[32,24,128]{2,1,0:T(8,128)(2,1)} %shard_map.144), calls=%async_computation.1 | async-start | bytes 393216 | tf_op jit(solution)/shard_map/all_to_all | solution.py:612
  86.6 9.9 %collective-permute-start.7 = (bf16[96,128]{1,0:T(8,128)(2,1)S(1)}, bf16[96,128]{1,0:T(8,128)(2,1)S(1)}, u32[]{:S(2)}, u32[]{:S(2)}) collective-permute-start(bf16[96,128]{1,0:T(8,128)(2,1)S(1)} %get-tuple-element.46), channel_id=1, source_target_pairs={{0,496},{16,32},{32,16},{48,64},{64,48},{80,96},{96,80},{112,128},... | collective-permute-start | bytes 73736 | tf_op jit(solution)/shard_map/ppermute | solution.py:495
  90.1 7.2 %collective-permute-start.6 = (bf16[96,128]{1,0:T(8,128)(2,1)S(1)}, bf16[96,128]{1,0:T(8,128)(2,1)S(1)}, u32[]{:S(2)}, u32[]{:S(2)}) collective-permute-start(bf16[96,128]{1,0:T(8,128)(2,1)S(1)} %get-tuple-element.43.refs_2_), channel_id=1, source_target_pairs={{0,16},{16,0},{32,48},{48,32},{64,80},{80,64},{96,112},{112,96},{1... | collective-permute-start | bytes 73736 | tf_op jit(solution)/shard_map/ppermute | solution.py:496
  99.1 13.8 %all-to-all-start.2 = ((f32[16,24,128]{2,1,0:T(8,128)}), f32[16,24,128]{2,1,0:T(8,128)S(1)}, u32[]{:S(2)}, u32[]{:S(2)}) async-start(f32[16,24,128]{2,1,0:T(8,128)} %shard_map.145), calls=%async_computation.2 | async-start | bytes 393216 | tf_op jit(solution)/shard_map/all_to_all | solution.py:616

commit v6 on v5

--- a/solution.py
+++ b/solution.py
@@ -9,7 +9,7 @@
 
 F32 = jnp.float32
 BF16 = jnp.bfloat16
-VMEM_LIMIT = 48 * 1024 * 1024
+VMEM_LIMIT = 24 * 1024 * 1024
 RING = 3
 
 
@@ -98,7 +98,7 @@
 
 
 def strips_body(
-    m_ref, inner_ref, outer_ref, place_ref, south_ref, halo_ref, near_ref, far_ref
+    m_ref, outer_ref, inner_ref, place_ref, south_ref, halo_ref, near_ref, far_ref
 ):
     rows, channels, cols = m_ref.shape
     here = lax.broadcasted_iota(jnp.int32, (cols, cols), 0)
@@ -134,11 +134,11 @@
 
 
 def strips_and_sums_body(
-    m_ref, inner_ref, outer_ref, sums_ref, place_ref,
+    m_ref, outer_ref, inner_ref, sums_ref, place_ref,
     south_ref, halo_ref, near_ref, far_ref, out_ref,
 ):
     strips_body(
-        m_ref, inner_ref, outer_ref, place_ref, south_ref, halo_ref, near_ref, far_ref
+        m_ref, outer_ref, inner_ref, place_ref, south_ref, halo_ref, near_ref, far_ref
     )
     out_ref[...] = sums_ref[...]
 
@@ -184,16 +184,16 @@
     return jnp.concatenate([rows, blank], axis=0).T
 
 
-def tap(weights, index):
-    return jnp.broadcast_to(weights[:, index : index + 1], (8, 128))
+def tap_tiles(taps, c0):
+    return lambda index: taps[index, pl.ds(c0, 8), :]
 
 
 def correlate(read, span, rows, lane, weights, flipped, top, summed):
     for b in range(7):
-        taps = [tap(weights, 48 - a * 7 - b if flipped else a * 7 + b) for a in range(7)]
+        taps = [weights(48 - a * 7 - b if flipped else a * 7 + b) for a in range(7)]
         far = taps
         if top is not None:
-            far = [jnp.where(top, tap(weights, a * 7 + b), taps[a]) for a in range(7)]
+            far = [jnp.where(top, weights(a * 7 + b), taps[a]) for a in range(7)]
         for r in span:
             wins = windows(read(r), b - RING, lane)
             for a in range(7):
@@ -213,10 +213,10 @@
     right = jnp.zeros((8, 128), F32)
     for a in range(7):
         for b in (0, 1, 2, 4, 5, 6):
-            weight = tap(weights, 48 - a * 7 - b if flipped else a * 7 + b)
+            weight = weights(48 - a * 7 - b if flipped else a * 7 + b)
             if top is not None and a > RING:
                 beyond = top & (lane >= RING * (rows + RING - a))
-                weight = jnp.where(beyond, tap(weights, a * 7 + b), weight)
+                weight = jnp.where(beyond, weights(a * 7 + b), weight)
             back = -(RING * a + b) % 128 if b < RING else -(RING * a + b - 6) % 128
             strip = before if b < RING else after
             moved = pltpu.roll(strip, back, 1) if back else strip
@@ -233,12 +233,22 @@
     return jnp.where(lane < RING, head, 0.0), jnp.where(lane >= 128 - RING, tail, 0.0)
 
 
-def own_body(flipped, settle, m_ref, dw_ref, conv_ref, wide, taps):
+def spread_taps(dw_ref, taps_ref):
+    columns = tap_columns(dw_ref)
+    for k in range(49):
+        taps_ref[k] = jnp.broadcast_to(columns[:, k : k + 1], columns.shape)
+
+
+def first_body(flipped, settle, m_ref, dw_ref, conv_ref, taps_ref, wide):
+    settle()
+    spread_taps(dw_ref, taps_ref)
+    own_body(flipped, m_ref, taps_ref, conv_ref, wide)
+
+
+def own_body(flipped, m_ref, taps, conv_ref, wide):
     rows, channels, cols = m_ref.shape
     pairs = cols // 128
     wide[...] = m_ref[...].astype(F32)
-    settle()
-    taps[...] = tap_columns(dw_ref)
 
     def step(ct, carry):
         c0 = pl.multiple_of(ct * 8, 8)
@@ -249,7 +259,7 @@
 
         blank = [[None] * pairs for _ in range(rows)]
         span = range(RING, rows + RING)
-        weights = taps[pl.ds(c0, 8), :]
+        weights = tap_tiles(taps, c0)
         summed = correlate(read, span, rows, lanes(), weights, flipped, None, blank)
         for i in range(rows):
             for t in range(pairs):
@@ -276,16 +286,15 @@
     return correlate(read, span, rows, lane, weights, flipped, top, summed)
 
 
-def ends_body(settle, south_ref, halo_ref, conv_ref, dw_ref, out_ref, wide, taps):
+def ends_body(south_ref, halo_ref, conv_ref, taps, out_ref, wide):
     rows, channels, cols = conv_ref.shape
     wide[0:RING] = south_ref[...].astype(F32)
     wide[RING : 2 * RING] = halo_ref[...].astype(F32)
-    settle()
-    taps[...] = tap_columns(dw_ref)
 
     def step(ct, carry):
         c0 = pl.multiple_of(ct * 8, 8)
-        summed = with_ends(conv_ref, wide, c0, lanes(), taps[pl.ds(c0, 8), :], False, None)
+        weights = tap_tiles(taps, c0)
+        summed = with_ends(conv_ref, wide, c0, lanes(), weights, False, None)
         for i in range(rows):
             for t in range(cols // 128):
                 out_ref[i, pl.ds(c0, 8), t * 128 : t * 128 + 128] = summed[i][t]
@@ -302,17 +311,16 @@
 
 
 def block_body(
-    settle, m_ref, conv_ref, near_ref, far_ref, ct_ref, mask_ref,
-    dw_ref, gain_ref, w_in_ref, b_ref, w_out_ref, place_ref,
+    settle, m_ref, conv_ref, far_ref, near_ref, taps, ct_ref, mask_ref,
+    gain_ref, w_in_ref, b_ref, w_out_ref, place_ref,
     out_ref, g_ref, inner_ref, outer_ref, wide_ref, tail_ref,
-    conv, flat, act, back, sca, pre, b_acc, gain_acc, taps, sides,
+    conv, flat, act, back, sca, pre, b_acc, gain_acc, sides,
 ):
     rows, channels, cols = m_ref.shape
     hidden = w_out_ref.shape[0]
     pairs = cols // 128
     split_sides(sides, near_ref, far_ref, place_ref[2])
     settle()
-    taps[...] = tap_columns(dw_ref)
     sea = mask_ref[...].astype(F32)
     spread(flat, ct_ref[...].astype(F32) * sea[None])
     for i in range(rows):
@@ -322,7 +330,7 @@
         c0 = pl.multiple_of(ct * 8, 8)
         lane = lanes()
         before, after = sides[0, pl.ds(c0, 8), :], sides[1, pl.ds(c0, 8), :]
-        weights = taps[pl.ds(c0, 8), :]
+        weights = tap_tiles(taps, c0)
         left, right = edges(before, after, rows, lane, weights, False, None)
         for i in range(rows):
             head, tail = place_edges(left, right, i, lane)
@@ -403,7 +411,7 @@
 
 def kernel_body(
     shift, m_ref, south_ref, halo_ref, near_ref, far_ref, g_ref, wide_ref, tail_ref, place_ref,
-    sums_ref, tail, grid, ext,
+    sums_ref, tail, grid, ext, held_sums,
 ):
     rows, channels, cols = g_ref.shape
     pairs = cols // 128
@@ -413,7 +421,6 @@
     def kernel_step(ct, carry):
         c0 = pl.multiple_of(ct * 8, 8)
         lane = lanes()
-        tile = tail_ref[pl.ds(c0, 8), :]
         grads = [
             [grid[i, pl.ds(c0, 8), t * 128 : t * 128 + 128] for t in range(pairs)]
             for i in range(rows)
@@ -430,12 +437,19 @@
                             term = grads[i][t] * wins[t]
                             summed[a] = term if summed[a] is None else summed[a] + term
             for a in range(7):
-                total = jnp.sum(summed[a], axis=1, keepdims=True)
-                tile = jnp.where(lane == shift + a * 7 + b, total, tile)
-        tail[pl.ds(c0, 8), :] = tile
+                held_sums[a * 7 + b, pl.ds(c0, 8), :] = summed[a]
         return carry
 
     lax.fori_loop(0, channels // 8, kernel_step, 0)
+    tail[...] = tail_ref[...]
+    lane = lax.broadcasted_iota(jnp.int32, (channels, 128), 1)
+    ones = jnp.ones((256, 128), BF16)
+    for k in range(49):
+        high = held_sums[k].astype(BF16)
+        low_part = (held_sums[k] - high.astype(F32)).astype(BF16)
+        both = jnp.concatenate([high, low_part], axis=1)
+        over_lanes = jnp.dot(both, ones, preferred_element_type=F32)
+        tail[...] = jnp.where(lane == shift + k, over_lanes, tail[...])
     low = wide_ref.shape[0]
     sums_ref[0:low, :] = wide_ref[...]
     sums_ref[low : low + channels, :] = tail[...].astype(BF16)
@@ -443,7 +457,7 @@
 
 def back_body(
     settle, conv_ref, south_ref, halo_ref, near_ref, far_ref, ct_ref, mask_ref, dw_ref, place_ref,
-    out_ref, wide, flat, taps, sides,
+    out_ref, wide, flat, sides, taps,
 ):
     rows, channels, cols = conv_ref.shape
     pairs = cols // 128
@@ -451,13 +465,13 @@
     wide[RING : 2 * RING] = halo_ref[...].astype(F32)
     split_sides(sides, near_ref, far_ref, place_ref[2])
     settle()
-    taps[...] = tap_columns(dw_ref)
+    spread_taps(dw_ref, taps)
 
     def step(ct, carry):
         c0 = pl.multiple_of(ct * 8, 8)
         lane = lanes()
         top = jnp.broadcast_to(place_ref[1], (8, 128)) > 0
-        weights = taps[pl.ds(c0, 8), :]
+        weights = tap_tiles(taps, c0)
         before, after = sides[0, pl.ds(c0, 8), :], sides[1, pl.ds(c0, 8), :]
         left, right = edges(before, after, rows, lane, weights, True, top)
         summed = with_ends(conv_ref, wide, c0, lane, weights, True, top)
@@ -552,17 +566,18 @@
     sides = pltpu.VMEM((2, channels, 128), F32)
     sums_grid = pltpu.VMEM((rows, channels, cols), F32)
     ends = pltpu.VMEM((2 * RING, channels, cols), F32)
-    (conv,) = call(
-        functools.partial(own_body, False), [sums_grid], [masked], [taps],
-        scratch=[sums_grid, columns],
+    tap_grid = pltpu.VMEM((49, channels, 128), F32)
+    conv, tiles = call(
+        functools.partial(first_body, False), [sums_grid, tap_grid], [masked], [taps],
+        scratch=[sums_grid],
     )
     south, north, near, far = call(
-        strips_body, [near_ring, near_ring, strip, strip], [masked, inner, outer], (), [place],
+        strips_body, [near_ring, near_ring, strip, strip], [masked, outer, inner], (), [place],
         waits=[conv],
     )
     near, far = lon_halo(near, far)
     (conv,) = call(
-        ends_body, [sums_grid], [south, north, conv], [taps], scratch=[ends, columns]
+        ends_body, [sums_grid], [south, north, conv, tiles], scratch=[ends]
     )
     output, grads, inner, outer, wide, tail = call(
         block_body,
@@ -570,9 +585,9 @@
             whole, held(grid), near_ring, near_ring,
             pltpu.VMEM((height - channels, 128), BF16), columns,
         ],
-        [masked, conv, near, far],
+        [masked, conv, far, near, tiles],
         [
-            cotangent, land_mask, taps, gain.reshape(1, channels), w_in,
+            cotangent, land_mask, gain.reshape(1, channels), w_in,
             b_in.reshape(1, hidden), w_out,
         ],
         [place],
@@ -585,7 +600,6 @@
             pltpu.VMEM((hidden, cells), BF16),
             pltpu.VMEM((hidden, 128), F32),
             columns,
-            columns,
             sides,
         ],
     )
@@ -593,17 +607,17 @@
     (sums,) = call(
         functools.partial(kernel_body, hidden - 128), [near_sums],
         [masked, south, north, near, far, grads, wide, tail], (), [place],
-        scratch=[columns, sums_grid, ext],
+        scratch=[columns, sums_grid, ext, tap_grid],
     )
     south, north, near, far, sums = call(
         strips_and_sums_body, [near_ring, near_ring, strip, strip, near_sums],
-        [grads, inner, outer, sums], (), [place],
+        [grads, outer, inner, sums], (), [place],
     )
     size = height // n_lat
     pieces = lax.all_to_all(sums.reshape(n_lat, size, 128), "lat", 0, 0, tiled=True)
     (conv,) = call(
-        functools.partial(own_body, True), [sums_grid], [grads], [taps],
-        scratch=[sums_grid, columns], waits=[near],
+        functools.partial(first_body, True), [sums_grid], [grads], [taps],
+        scratch=[tap_grid, sums_grid], waits=[near],
     )
     (pieces,) = call(
         spread_body, [pltpu.VMEM((n_lon, size, 128), BF16)], [pieces], waits=[conv]
@@ -616,7 +630,7 @@
     pieces = lax.all_to_all(pieces, "lat", 0, 0, tiled=True)
     (input_grad,) = call(
         back_body, [whole], [conv, south, north, near, far], [cotangent, land_mask, taps],
-        [place], scratch=[ends, flat, columns, sides],
+        [place], scratch=[ends, flat, sides, tap_grid],
     )
     scale = float(cells * n_lat * n_lon) ** -0.5
     w_in_grad, w_out_grad, dw_grad, gain_grad, b_grad = call(

time: 115 us -> 107 us (0.930)
  Pallas kernels: 43.8 us -> 38.3 us
  starting transfers between devices: 58.7 us -> 57.5 us
    all_to_all x1, starting transfers between devices: 15.1 us -> 9.16 us  [shards(): lax.all_to_all(sums.reshape(n_lat, size, 128), 'lat', 0, 0, tiled=True)]
    pallas_call x12, Pallas kernels: 43.8 us -> 38.3 us  [call(): pl.pallas_call(run, out_shape=outs, in_specs=specs, out_specs=[pl.BlockSp...]
    ppermute x2, starting transfers between devices: 12.5 us -> 17.3 us  [lon_halo(): near = lax.ppermute(near, 'lon', [(i, i ^ 1) for i in range(n_lon)])]
    all_to_all x1, starting transfers between devices: 9.53 us -> 5.98 us  [shards(): pieces = lax.all_to_all(pieces, 'lon', 0, 0, tiled=True)]
    ppermute x2, starting transfers between devices: 5.46 us -> 7.78 us  [lon_halo(): lax.ppermute(far, 'lon', [(i, (i - 1 + 2 * (i % 2)) % n_lon) for i in ran...]
    ppermute x2, starting transfers between devices: 11.3 us -> 12.5 us  [lat_halo(): inner = lax.ppermute(inner, 'lat', [(i, i ^ 1) for i in range(n_lat)])]
  transfers between devices with their start and end apart: 11 -> 11, of which waited for: 4 -> 4; matrix products, arithmetic and copies ran while one was open for 0% -> 0% of each run, Pallas kernels for 24% -> 22%
where the time goes in v6:
time: 107 us; the launch traced here: 106 us
  starting transfers between devices  57.5 us (54%)
  Pallas kernels  38.3 us (36%)
  waiting for transfers between devices  9.64 us (9%)
    pallas_call x12, Pallas kernels, call(): pl.pallas_call(run, out_shape=outs, in_specs=specs, out_specs=[pl.BlockSp...  38.3 us
    ppermute x2, starting transfers between devices, lon_halo(): near = lax.ppermute(near, 'lon', [(i, i ^ 1) for i in range(n_lon)])  17.3 us
    ppermute x2, starting transfers between devices, lat_halo(): inner = lax.ppermute(inner, 'lat', [(i, i ^ 1) for i in range(n_lat)])  12.5 us
    all_to_all x1, starting transfers between devices, shards(): lax.all_to_all(sums.reshape(n_lat, size, 128), 'lat', 0, 0, tiled=True)  9.16 us
    ppermute x2, starting transfers between devices, lon_halo(): lax.ppermute(far, 'lon', [(i, (i - 1 + 2 * (i % 2)) % n_lon) for i in ran...  7.78 us
    all_to_all x1, starting transfers between devices, shards(): pieces = lax.all_to_all(pieces, 'lon', 0, 0, tiled=True)  5.98 us
    all_to_all x1, waiting for transfers between devices, shards(): pieces = lax.all_to_all(pieces, 'lat', 0, 0, tiled=True)  4.22 us
    all_to_all x1, starting transfers between devices, shards(): pieces = lax.all_to_all(pieces, 'lat', 0, 0, tiled=True)  3.52 us
  transfers between devices with their start and end apart: 11, of which 4 were waited for; matrix products, arithmetic and copies ran while one was open for 0% of the time, Pallas kernels for 22%

profile of v6, /device:TPU:1, one launch (start us, length us, event | category | flops | bytes accessed | tf_op | source)
XLA Modules:
  0.0 106.3 jit_solution(6163456397341103711)
XLA Ops:
  0.7 0.1 pad_add_fusion.refs_2_.refs_3_.refs_11_.refs_8_.refs_4_
  0.7 1.8 %shard_map.135 = (bf16[8,96,256]{2,1,0:T(8,128)(2,1)S(1)}, bf16[3,96,256]{2,1,0:T(8,128)(2,1)S(1)}, bf16[3,96,256]{2,1,0:T(8,128)(2,1)S(1)}) custom-call(bf16[96,8,256]{2,1,0:T(8,128)(2,1)} %refs_0_.1, s32[8,256]{1,0:T(8,128)} %refs_6_.3, s32[3]{0:T(128)S(1)} %pad_add_fusion.refs_2_.refs_3_.refs_11_.refs_8_.refs_4_), custom_call_target="tpu_custom_call" | custom-call | tf_op jit(solution)/shard_map/pallas_call | solution.py:48
  2.6 0.7 collective-permute-start
  3.2 6.5 %collective-permute-start.1 = (bf16[3,96,256]{2,1,0:T(8,128)(2,1)S(1)}, bf16[3,96,256]{2,1,0:T(8,128)(2,1)S(1)}, u32[]{:S(2)}, u32[]{:S(2)}) collective-permute-start(bf16[3,96,256]{2,1,0:T(8,128)(2,1)S(1)} %get-tuple-element.34), channel_id=1, source_target_pairs={{0,1},{1,0},{2,3},{3,2},{4,5},{5,4},{6,7},{7,6},{8,9},{9,8},{10,11... | collective-permute-start | bytes 442376 | tf_op jit(solution)/shard_map/ppermute | solution.py:503
  9.7 4.7 %shard_map.136 = (f32[8,96,256]{2,1,0:T(8,128)S(1)}, f32[49,96,128]{2,1,0:T(8,128)S(1)}) custom-call(bf16[8,96,256]{2,1,0:T(8,128)(2,1)S(1)} %get-tuple-element.32.refs_0_, f32[7,7,96]{2,1,0:T(8,128)} %bitcast.12), custom_call_target="tpu_custom_call" | custom-call | tf_op jit(solution)/shard_map/pallas_call | solution.py:48
  14.4 0.0 collective-permute-done.refs_1_
  14.4 0.0 collective-permute-done.1.refs_2_
  14.4 0.9 shard_map.137
  15.4 4.2 %collective-permute-start.2 = (bf16[96,128]{1,0:T(8,128)(2,1)S(1)}, bf16[96,128]{1,0:T(8,128)(2,1)S(1)}, u32[]{:S(2)}, u32[]{:S(2)}) collective-permute-start(bf16[96,128]{1,0:T(8,128)(2,1)S(1)} %get-tuple-element.39), channel_id=1, source_target_pairs={{0,496},{16,32},{32,16},{48,64},{64,48},{80,96},{96,80},{112,128},... | collective-permute-start | bytes 73736 | tf_op jit(solution)/shard_map/ppermute | solution.py:509
  19.6 10.9 %collective-permute-start.3 = (bf16[96,128]{1,0:T(8,128)(2,1)S(1)}, bf16[96,128]{1,0:T(8,128)(2,1)S(1)}, u32[]{:S(2)}, u32[]{:S(2)}) collective-permute-start(bf16[96,128]{1,0:T(8,128)(2,1)S(1)} %get-tuple-element.40), channel_id=1, source_target_pairs={{0,16},{16,0},{32,48},{48,32},{64,80},{80,64},{96,112},{112,96},{1... | collective-permute-start | bytes 73736 | tf_op jit(solution)/shard_map/ppermute | solution.py:510
  30.5 1.8 %shard_map.138.refs_1_ = f32[8,96,256]{2,1,0:T(8,128)S(1)} custom-call(bf16[3,96,256]{2,1,0:T(8,128)(2,1)S(1)} %get-tuple-element.36.refs_0_.refs_1_, bf16[3,96,256]{2,1,0:T(8,128)(2,1)S(1)} %get-tuple-element.37.refs_1_.refs_2_, f32[8,96,256]{2,1,0:T(8,128)S(1)} %get-tuple-element.35.refs_4_.refs_2_, f32[49,96,128]{2,1,0:T(8,128)S(1)} %get-tuple-element.38.refs_3_.refs_4_), custom_call_target="tpu_custom_call" | custom-call | tf_op jit(solution)/shard_map/pallas_call | solution.py:48
  32.4 0.0 collective-permute-done.2.refs_2_.refs_4_
  32.4 0.0 collective-permute-done.3.refs_3_
  32.4 8.9 %shard_map.139 = (bf16[96,8,256]{2,1,0:T(8,128)(2,1)}, bf16[8,96,256]{2,1,0:T(8,128)(2,1)S(1)}, bf16[3,96,256]{2,1,0:T(8,128)(2,1)S(1)}, bf16[3,96,256]{2,1,0:T(...) custom-call(bf16[8,96,256]{2,1,0:T(8,128)(2,1)S(1)} %get-tuple-element.32.refs_0_, ...), custom_call_target="tpu_custom_call" | custom-call | tf_op jit(solution)/shard_map/pallas_call | solution.py:48
  41.3 0.7 collective-permute-start.4
  42.0 6.0 %collective-permute-start.5 = (bf16[3,96,256]{2,1,0:T(8,128)(2,1)S(1)}, bf16[3,96,256]{2,1,0:T(8,128)(2,1)S(1)}, u32[]{:S(2)}, u32[]{:S(2)}) collective-permute-start(bf16[3,96,256]{2,1,0:T(8,128)(2,1)S(1)} %get-tuple-element.44), channel_id=1, source_target_pairs={{0,1},{1,0},{2,3},{3,2},{4,5},{5,4},{6,7},{7,6},{8,9},{9,8},{10,11... | collective-permute-start | bytes 442376 | tf_op jit(solution)/shard_map/ppermute | solution.py:503
  48.0 5.9 %shard_map.140.refs_3_ = bf16[384,128]{1,0:T(8,128)(2,1)S(1)} custom-call(bf16[8,96,256]{2,1,0:T(8,128)(2,1)S(1)} %get-tuple-element.32.refs_0_, bf16[3,96,256]{2,1,0:T(8,128)(2,1)S(1)} %get-tuple-element.36.refs_0_.refs_1_, bf16[3,96,256]{2,1,0:T(8,128)(2,1)S(1)} %get-tuple-element.37.refs_1_.refs_2_, bf16[96,128]{1,0:T(8,128)(2,1)S(1)} %collective-permute-done.3.refs_3_, ...), custom_call_target="tpu_custom_call" | custom-call | tf_op jit(solution)/shard_map/pallas_call | solution.py:48
  53.9 0.0 collective-permute-done.4.refs_1_
  53.9 0.0 collective-permute-done.5.refs_2_
  53.9 1.5 %shard_map.141 = (bf16[3,96,256]{2,1,0:T(8,128)(2,1)S(1)}, bf16[3,96,256]{2,1,0:T(8,128)(2,1)S(1)}, bf16[96,128]{1,0:T(8,128)(2,1)S(1)}, bf16[96,128]{1,0:T(8,128)(2,1)S(1)}, bf16[384,128]{1,0:T(8,128)(2,1)}) custom-call(bf16[8,96,256]{2,1,0:T(8,128)(2,1)S(1)} %get-tuple-element.42.refs_5_.refs_0_, bf16[3,96,256]{2,1,0:T(8,128)(2,1)S(1)} %collective-permute-done.4.refs_1_, ...), custom_call_target="tpu_custom_call" | custom-call | tf_op jit(solution)/shard_map/pallas_call | solution.py:48
  55.4 9.2 %all-to-all-start = ((bf16[16,24,128]{2,1,0:T(8,128)(2,1)}), bf16[16,24,128]{2,1,0:T(8,128)(2,1)S(1)}, u32[]{:S(2)}, u32[]{:S(2)}) async-start(bf16[16,24,128]{2,1,0:T(8,128)(2,1)} %bitcast.6), calls=%async_computation | async-start | bytes 196608 | tf_op jit(solution)/shard_map/all_to_all | solution.py:617
  64.6 4.7 %shard_map.142.refs_0_.refs_1_ = f32[8,96,256]{2,1,0:T(8,128)S(1)} custom-call(bf16[8,96,256]{2,1,0:T(8,128)(2,1)S(1)} %get-tuple-element.42.refs_5_.refs_0_, f32[7,7,96]{2,1,0:T(8,128)} %bitcast.13, bf16[96,128]{1,0:T(8,128)(2,1)S(1)} %get-tuple-element.47.refs_2_), custom_call_target="tpu_custom_call" | custom-call | tf_op jit(solution)/shard_map/pallas_call | solution.py:48
  69.3 3.5 %all-to-all-done.refs_0_ = bf16[16,24,128]{2,1,0:T(8,128)(2,1)S(1)} async-done(((bf16[16,24,128]{2,1,0:T(8,128)(2,1)}), bf16[16,24,128]{2,1,0:T(8,128)(2,1)S(1)}, u32[]{:S(2)}, u32[]{:S(2)}) %all-to-all-start) | async-done | bytes 98336 | tf_op jit(solution)/shard_map/all_to_all | solution.py:617
  72.8 0.7 shard_map.144
  73.5 6.0 %all-to-all-start.1 = ((bf16[32,24,128]{2,1,0:T(8,128)(2,1)}), bf16[32,24,128]{2,1,0:T(8,128)(2,1)S(1)}, u32[]{:S(2)}, u32[]{:S(2)}) async-start(bf16[32,24,128]{2,1,0:T(8,128)(2,1)} %shard_map.144), calls=%async_computation.1 | async-start | bytes 393216 | tf_op jit(solution)/shard_map/all_to_all | solution.py:626
  79.5 3.5 %collective-permute-start.7 = (bf16[96,128]{1,0:T(8,128)(2,1)S(1)}, bf16[96,128]{1,0:T(8,128)(2,1)S(1)}, u32[]{:S(2)}, u32[]{:S(2)}) collective-permute-start(bf16[96,128]{1,0:T(8,128)(2,1)S(1)} %get-tuple-element.50), channel_id=1, source_target_pairs={{0,496},{16,32},{32,16},{48,64},{64,48},{80,96},{96,80},{112,128},... | collective-permute-start | bytes 73736 | tf_op jit(solution)/shard_map/ppermute | solution.py:509
  83.0 6.4 %collective-permute-start.6 = (bf16[96,128]{1,0:T(8,128)(2,1)S(1)}, bf16[96,128]{1,0:T(8,128)(2,1)S(1)}, u32[]{:S(2)}, u32[]{:S(2)}) collective-permute-start(bf16[96,128]{1,0:T(8,128)(2,1)S(1)} %get-tuple-element.47.refs_2_), channel_id=1, source_target_pairs={{0,16},{16,0},{32,48},{48,32},{64,80},{80,64},{96,112},{112,96},{1... | collective-permute-start | bytes 73736 | tf_op jit(solution)/shard_map/ppermute | solution.py:510
  89.4 0.0 collective-permute-done.7.refs_4_.refs_2_
  89.4 0.8 collective-permute-done.6.refs_3_.refs_1_
  90.2 1.1 %all-to-all-done.1.refs_0_ = bf16[32,24,128]{2,1,0:T(8,128)(2,1)S(1)} async-done(((bf16[32,24,128]{2,1,0:T(8,128)(2,1)}), bf16[32,24,128]{2,1,0:T(8,128)(2,1)S(1)}, u32[]{:S(2)}, u32[]{:S(2)}) %all-to-all-start.1) | async-done | bytes 196640 | tf_op jit(solution)/shard_map/all_to_all | solution.py:626
  91.3 0.7 shard_map.145
  92.0 3.5 %all-to-all-start.2 = ((f32[16,24,128]{2,1,0:T(8,128)}), f32[16,24,128]{2,1,0:T(8,128)S(1)}, u32[]{:S(2)}, u32[]{:S(2)}) async-start(f32[16,24,128]{2,1,0:T(8,128)} %shard_map.145), calls=%async_computation.2 | async-start | bytes 393216 | tf_op jit(solution)/shard_map/all_to_all | solution.py:630
  95.6 5.8 %shard_map.143 = bf16[96,8,256]{2,1,0:T(8,128)(2,1)} custom-call(f32[8,96,256]{2,1,0:T(8,128)S(1)} %shard_map.142.refs_0_.refs_1_, bf16[3,96,256]{2,1,0:T(8,128)(2,1)S(1)} %get-tuple-element.48.refs_1_, bf16[3,96,256]{2,1,0:T(8,128)(2,1)S(1)} %get-tuple-element.49.refs_2_, bf16[96,128]{1,0:T(8,128)(2,1)S(1)} %collective-permute-done.6.refs_3_.refs_1_, ...), custom_call_target="tpu_custom_call" | custom-call | tf_op jit(solution)/shard_map/pallas_call | solution.py:48
  101.3 4.2 %all-to-all-done.2 = f32[16,24,128]{2,1,0:T(8,128)S(1)} async-done(((f32[16,24,128]{2,1,0:T(8,128)}), f32[16,24,128]{2,1,0:T(8,128)S(1)}, u32[]{:S(2)}, u32[]{:S(2)}) %all-to-all-start.2) | async-done | bytes 196640 | tf_op jit(solution)/shard_map/all_to_all | solution.py:630
  105.6 0.8 shard_map.146
Async XLA Ops:
  2.6 11.8 %collective-permute-start = (bf16[3,96,256]{2,1,0:T(8,128)(2,1)S(1)}, bf16[3,96,256]{2,1,0:T(8,128)(2,1)S(1)}, u32[]{:S(2)}, u32[]{:S(2)}) collective-permute-start(bf16[3,96,256]{2,1,0:T(8,128)(2,1)S(1)} %get-tuple-element.33), channel_id=1, source_target_pairs={{1,2},{2,1},{3,4},{4,3},{5,6},{6,5},{7,8},{8,7},{9,10},{10,9},{11,... | collective-permute-start | bytes 442376 | tf_op jit(solution)/shard_map/ppermute | solution.py:502
  3.2 11.2 %collective-permute-start.1 = (bf16[3,96,256]{2,1,0:T(8,128)(2,1)S(1)}, bf16[3,96,256]{2,1,0:T(8,128)(2,1)S(1)}, u32[]{:S(2)}, u32[]{:S(2)}) collective-permute-start(bf16[3,96,256]{2,1,0:T(8,128)(2,1)S(1)} %get-tuple-element.34), channel_id=1, source_target_pairs={{0,1},{1,0},{2,3},{3,2},{4,5},{5,4},{6,7},{7,6},{8,9},{9,8},{10,11... | collective-permute-start | bytes 442376 | tf_op jit(solution)/shard_map/ppermute | solution.py:503
  15.4 17.0 %collective-permute-start.2 = (bf16[96,128]{1,0:T(8,128)(2,1)S(1)}, bf16[96,128]{1,0:T(8,128)(2,1)S(1)}, u32[]{:S(2)}, u32[]{:S(2)}) collective-permute-start(bf16[96,128]{1,0:T(8,128)(2,1)S(1)} %get-tuple-element.39), channel_id=1, source_target_pairs={{0,496},{16,32},{32,16},{48,64},{64,48},{80,96},{96,80},{112,128},... | collective-permute-start | bytes 73736 | tf_op jit(solution)/shard_map/ppermute | solution.py:509
  19.6 12.8 %collective-permute-start.3 = (bf16[96,128]{1,0:T(8,128)(2,1)S(1)}, bf16[96,128]{1,0:T(8,128)(2,1)S(1)}, u32[]{:S(2)}, u32[]{:S(2)}) collective-permute-start(bf16[96,128]{1,0:T(8,128)(2,1)S(1)} %get-tuple-element.40), channel_id=1, source_target_pairs={{0,16},{16,0},{32,48},{48,32},{64,80},{80,64},{96,112},{112,96},{1... | collective-permute-start | bytes 73736 | tf_op jit(solution)/shard_map/ppermute | solution.py:510
  41.3 12.6 %collective-permute-start.4 = (bf16[3,96,256]{2,1,0:T(8,128)(2,1)S(1)}, bf16[3,96,256]{2,1,0:T(8,128)(2,1)S(1)}, u32[]{:S(2)}, u32[]{:S(2)}) collective-permute-start(bf16[3,96,256]{2,1,0:T(8,128)(2,1)S(1)} %get-tuple-element.43), channel_id=1, source_target_pairs={{1,2},{2,1},{3,4},{4,3},{5,6},{6,5},{7,8},{8,7},{9,10},{10,9},{11,... | collective-permute-start | bytes 442376 | tf_op jit(solution)/shard_map/ppermute | solution.py:502
  42.0 11.9 %collective-permute-start.5 = (bf16[3,96,256]{2,1,0:T(8,128)(2,1)S(1)}, bf16[3,96,256]{2,1,0:T(8,128)(2,1)S(1)}, u32[]{:S(2)}, u32[]{:S(2)}) collective-permute-start(bf16[3,96,256]{2,1,0:T(8,128)(2,1)S(1)} %get-tuple-element.44), channel_id=1, source_target_pairs={{0,1},{1,0},{2,3},{3,2},{4,5},{5,4},{6,7},{7,6},{8,9},{9,8},{10,11... | collective-permute-start | bytes 442376 | tf_op jit(solution)/shard_map/ppermute | solution.py:503
  55.4 17.4 %all-to-all-start = ((bf16[16,24,128]{2,1,0:T(8,128)(2,1)}), bf16[16,24,128]{2,1,0:T(8,128)(2,1)S(1)}, u32[]{:S(2)}, u32[]{:S(2)}) async-start(bf16[16,24,128]{2,1,0:T(8,128)(2,1)} %bitcast.6), calls=%async_computation | async-start | bytes 196608 | tf_op jit(solution)/shard_map/all_to_all | solution.py:617
  73.5 17.8 %all-to-all-start.1 = ((bf16[32,24,128]{2,1,0:T(8,128)(2,1)}), bf16[32,24,128]{2,1,0:T(8,128)(2,1)S(1)}, u32[]{:S(2)}, u32[]{:S(2)}) async-start(bf16[32,24,128]{2,1,0:T(8,128)(2,1)} %shard_map.144), calls=%async_computation.1 | async-start | bytes 393216 | tf_op jit(solution)/shard_map/all_to_all | solution.py:626
  79.5 9.9 %collective-permute-start.7 = (bf16[96,128]{1,0:T(8,128)(2,1)S(1)}, bf16[96,128]{1,0:T(8,128)(2,1)S(1)}, u32[]{:S(2)}, u32[]{:S(2)}) collective-permute-start(bf16[96,128]{1,0:T(8,128)(2,1)S(1)} %get-tuple-element.50), channel_id=1, source_target_pairs={{0,496},{16,32},{32,16},{48,64},{64,48},{80,96},{96,80},{112,128},... | collective-permute-start | bytes 73736 | tf_op jit(solution)/shard_map/ppermute | solution.py:509
  83.0 7.2 %collective-permute-start.6 = (bf16[96,128]{1,0:T(8,128)(2,1)S(1)}, bf16[96,128]{1,0:T(8,128)(2,1)S(1)}, u32[]{:S(2)}, u32[]{:S(2)}) collective-permute-start(bf16[96,128]{1,0:T(8,128)(2,1)S(1)} %get-tuple-element.47.refs_2_), channel_id=1, source_target_pairs={{0,16},{16,0},{32,48},{48,32},{64,80},{80,64},{96,112},{112,96},{1... | collective-permute-start | bytes 73736 | tf_op jit(solution)/shard_map/ppermute | solution.py:510
  92.0 13.5 %all-to-all-start.2 = ((f32[16,24,128]{2,1,0:T(8,128)}), f32[16,24,128]{2,1,0:T(8,128)S(1)}, u32[]{:S(2)}, u32[]{:S(2)}) async-start(f32[16,24,128]{2,1,0:T(8,128)} %shard_map.145), calls=%async_computation.2 | async-start | bytes 393216 | tf_op jit(solution)/shard_map/all_to_all | solution.py:630

commit v7 on v6

--- a/solution.py
+++ b/solution.py
@@ -619,13 +619,13 @@
         functools.partial(first_body, True), [sums_grid], [grads], [taps],
         scratch=[tap_grid, sums_grid], waits=[near],
     )
+    near, far = lon_halo(near, far)
     (pieces,) = call(
-        spread_body, [pltpu.VMEM((n_lon, size, 128), BF16)], [pieces], waits=[conv]
-    )
-    near, far = lon_halo(near, far)
+        spread_body, [pltpu.VMEM((n_lon, size, 128), BF16)], [pieces], waits=[conv, near]
+    )
     pieces = lax.all_to_all(pieces, "lon", 0, 0, tiled=True)
     (pieces,) = call(
-        spread_body, [pltpu.VMEM((n_lat, size, 128), F32)], [pieces], waits=[near, far]
+        spread_body, [pltpu.VMEM((n_lat, size, 128), F32)], [pieces], waits=[far]
     )
     pieces = lax.all_to_all(pieces, "lat", 0, 0, tiled=True)
     (input_grad,) = call(

time: 107 us -> 109 us (1.019)
  waiting for transfers between devices: 9.64 us -> 13.2 us
  starting transfers between devices: 57.5 us -> 55.8 us
    all_to_all x1, waiting for transfers between devices: 1.08 us -> 6.38 us  [shards(): pieces = lax.all_to_all(pieces, 'lon', 0, 0, tiled=True)]
    ppermute x2, starting transfers between devices: 17.3 us -> 13.7 us  [lon_halo(): near = lax.ppermute(near, 'lon', [(i, i ^ 1) for i in range(n_lon)])]
    all_to_all x1, waiting for transfers between devices: 3.51 us -> 0.72 us  [shards(): lax.all_to_all(sums.reshape(n_lat, size, 128), 'lat', 0, 0, tiled=True)]
    ppermute x2, waiting for transfers between devices: 0.01 us -> 1.9 us  [lon_halo(): lax.ppermute(far, 'lon', [(i, (i - 1 + 2 * (i % 2)) % n_lon) for i in ran...]
    all_to_all x1, starting transfers between devices: 3.52 us -> 5.38 us  [shards(): pieces = lax.all_to_all(pieces, 'lat', 0, 0, tiled=True)]
  transfers between devices with their start and end apart: 11 -> 11, of which waited for: 4 -> 4; matrix products, arithmetic and copies ran while one was open for 0% -> 0% of each run, Pallas kernels for 22% -> 21%
where the time goes in v7:
time: 109 us; the launch traced here: 108 us
  starting transfers between devices  55.8 us (51%)
  Pallas kernels  38.3 us (35%)
  waiting for transfers between devices  13.2 us (12%)
    pallas_call x12, Pallas kernels, call(): pl.pallas_call(run, out_shape=outs, in_specs=specs, out_specs=[pl.BlockSp...  38.3 us
    ppermute x2, starting transfers between devices, lon_halo(): near = lax.ppermute(near, 'lon', [(i, i ^ 1) for i in range(n_lon)])  13.7 us
    ppermute x2, starting transfers between devices, lat_halo(): inner = lax.ppermute(inner, 'lat', [(i, i ^ 1) for i in range(n_lat)])  12.5 us
    all_to_all x1, starting transfers between devices, shards(): lax.all_to_all(sums.reshape(n_lat, size, 128), 'lat', 0, 0, tiled=True)  9.16 us
    ppermute x2, starting transfers between devices, lon_halo(): lax.ppermute(far, 'lon', [(i, (i - 1 + 2 * (i % 2)) % n_lon) for i in ran...  7.78 us
    all_to_all x1, waiting for transfers between devices, shards(): pieces = lax.all_to_all(pieces, 'lon', 0, 0, tiled=True)  6.38 us
    all_to_all x1, starting transfers between devices, shards(): pieces = lax.all_to_all(pieces, 'lon', 0, 0, tiled=True)  5.97 us
    all_to_all x1, starting transfers between devices, shards(): pieces = lax.all_to_all(pieces, 'lat', 0, 0, tiled=True)  5.38 us
  transfers between devices with their start and end apart: 11, of which 4 were waited for; matrix products, arithmetic and copies ran while one was open for 0% of the time, Pallas kernels for 21%

profile of v7, /device:TPU:1, one launch (start us, length us, event | category | flops | bytes accessed | tf_op | source)
XLA Modules:
  0.0 108.1 jit_solution(1680705707544303105)
XLA Ops:
  0.7 0.1 pad_add_fusion.refs_2_.refs_3_.refs_11_.refs_8_.refs_4_
  0.7 1.8 %shard_map.135 = (bf16[8,96,256]{2,1,0:T(8,128)(2,1)S(1)}, bf16[3,96,256]{2,1,0:T(8,128)(2,1)S(1)}, bf16[3,96,256]{2,1,0:T(8,128)(2,1)S(1)}) custom-call(bf16[96,8,256]{2,1,0:T(8,128)(2,1)} %refs_0_.1, s32[8,256]{1,0:T(8,128)} %refs_6_.3, s32[3]{0:T(128)S(1)} %pad_add_fusion.refs_2_.refs_3_.refs_11_.refs_8_.refs_4_), custom_call_target="tpu_custom_call" | custom-call | tf_op jit(solution)/shard_map/pallas_call | solution.py:48
  2.6 0.7 collective-permute-start
  3.2 6.5 %collective-permute-start.1 = (bf16[3,96,256]{2,1,0:T(8,128)(2,1)S(1)}, bf16[3,96,256]{2,1,0:T(8,128)(2,1)S(1)}, u32[]{:S(2)}, u32[]{:S(2)}) collective-permute-start(bf16[3,96,256]{2,1,0:T(8,128)(2,1)S(1)} %get-tuple-element.34), channel_id=1, source_target_pairs={{0,1},{1,0},{2,3},{3,2},{4,5},{5,4},{6,7},{7,6},{8,9},{9,8},{10,11... | collective-permute-start | bytes 442376 | tf_op jit(solution)/shard_map/ppermute | solution.py:503
  9.7 4.7 %shard_map.136 = (f32[8,96,256]{2,1,0:T(8,128)S(1)}, f32[49,96,128]{2,1,0:T(8,128)S(1)}) custom-call(bf16[8,96,256]{2,1,0:T(8,128)(2,1)S(1)} %get-tuple-element.32.refs_0_, f32[7,7,96]{2,1,0:T(8,128)} %bitcast.12), custom_call_target="tpu_custom_call" | custom-call | tf_op jit(solution)/shard_map/pallas_call | solution.py:48
  14.4 0.0 collective-permute-done.refs_1_
  14.4 0.0 collective-permute-done.1.refs_2_
  14.4 0.9 shard_map.137
  15.4 4.2 %collective-permute-start.2 = (bf16[96,128]{1,0:T(8,128)(2,1)S(1)}, bf16[96,128]{1,0:T(8,128)(2,1)S(1)}, u32[]{:S(2)}, u32[]{:S(2)}) collective-permute-start(bf16[96,128]{1,0:T(8,128)(2,1)S(1)} %get-tuple-element.39), channel_id=1, source_target_pairs={{0,496},{16,32},{32,16},{48,64},{64,48},{80,96},{96,80},{112,128},... | collective-permute-start | bytes 73736 | tf_op jit(solution)/shard_map/ppermute | solution.py:509
  19.6 10.9 %collective-permute-start.3 = (bf16[96,128]{1,0:T(8,128)(2,1)S(1)}, bf16[96,128]{1,0:T(8,128)(2,1)S(1)}, u32[]{:S(2)}, u32[]{:S(2)}) collective-permute-start(bf16[96,128]{1,0:T(8,128)(2,1)S(1)} %get-tuple-element.40), channel_id=1, source_target_pairs={{0,16},{16,0},{32,48},{48,32},{64,80},{80,64},{96,112},{112,96},{1... | collective-permute-start | bytes 73736 | tf_op jit(solution)/shard_map/ppermute | solution.py:510
  30.5 1.8 %shard_map.138.refs_1_ = f32[8,96,256]{2,1,0:T(8,128)S(1)} custom-call(bf16[3,96,256]{2,1,0:T(8,128)(2,1)S(1)} %get-tuple-element.36.refs_0_.refs_1_, bf16[3,96,256]{2,1,0:T(8,128)(2,1)S(1)} %get-tuple-element.37.refs_1_.refs_2_, f32[8,96,256]{2,1,0:T(8,128)S(1)} %get-tuple-element.35.refs_4_.refs_2_, f32[49,96,128]{2,1,0:T(8,128)S(1)} %get-tuple-element.38.refs_3_.refs_4_), custom_call_target="tpu_custom_call" | custom-call | tf_op jit(solution)/shard_map/pallas_call | solution.py:48
  32.4 0.0 collective-permute-done.2.refs_2_.refs_4_
  32.4 0.0 collective-permute-done.3.refs_3_
  32.4 8.9 %shard_map.139 = (bf16[96,8,256]{2,1,0:T(8,128)(2,1)}, bf16[8,96,256]{2,1,0:T(8,128)(2,1)S(1)}, bf16[3,96,256]{2,1,0:T(8,128)(2,1)S(1)}, bf16[3,96,256]{2,1,0:T(...) custom-call(bf16[8,96,256]{2,1,0:T(8,128)(2,1)S(1)} %get-tuple-element.32.refs_0_, ...), custom_call_target="tpu_custom_call" | custom-call | tf_op jit(solution)/shard_map/pallas_call | solution.py:48
  41.3 0.7 collective-permute-start.4
  42.0 6.0 %collective-permute-start.5 = (bf16[3,96,256]{2,1,0:T(8,128)(2,1)S(1)}, bf16[3,96,256]{2,1,0:T(8,128)(2,1)S(1)}, u32[]{:S(2)}, u32[]{:S(2)}) collective-permute-start(bf16[3,96,256]{2,1,0:T(8,128)(2,1)S(1)} %get-tuple-element.44), channel_id=1, source_target_pairs={{0,1},{1,0},{2,3},{3,2},{4,5},{5,4},{6,7},{7,6},{8,9},{9,8},{10,11... | collective-permute-start | bytes 442376 | tf_op jit(solution)/shard_map/ppermute | solution.py:503
  48.0 5.9 %shard_map.140.refs_3_ = bf16[384,128]{1,0:T(8,128)(2,1)S(1)} custom-call(bf16[8,96,256]{2,1,0:T(8,128)(2,1)S(1)} %get-tuple-element.32.refs_0_, bf16[3,96,256]{2,1,0:T(8,128)(2,1)S(1)} %get-tuple-element.36.refs_0_.refs_1_, bf16[3,96,256]{2,1,0:T(8,128)(2,1)S(1)} %get-tuple-element.37.refs_1_.refs_2_, bf16[96,128]{1,0:T(8,128)(2,1)S(1)} %collective-permute-done.3.refs_3_, ...), custom_call_target="tpu_custom_call" | custom-call | tf_op jit(solution)/shard_map/pallas_call | solution.py:48
  53.9 0.0 collective-permute-done.4.refs_1_
  53.9 0.0 collective-permute-done.5.refs_2_
  53.9 1.5 %shard_map.141 = (bf16[3,96,256]{2,1,0:T(8,128)(2,1)S(1)}, bf16[3,96,256]{2,1,0:T(8,128)(2,1)S(1)}, bf16[96,128]{1,0:T(8,128)(2,1)S(1)}, bf16[96,128]{1,0:T(8,128)(2,1)S(1)}, bf16[384,128]{1,0:T(8,128)(2,1)}) custom-call(bf16[8,96,256]{2,1,0:T(8,128)(2,1)S(1)} %get-tuple-element.42.refs_5_.refs_0_, bf16[3,96,256]{2,1,0:T(8,128)(2,1)S(1)} %collective-permute-done.4.refs_1_, ...), custom_call_target="tpu_custom_call" | custom-call | tf_op jit(solution)/shard_map/pallas_call | solution.py:48
  55.4 9.2 %all-to-all-start = ((bf16[16,24,128]{2,1,0:T(8,128)(2,1)}), bf16[16,24,128]{2,1,0:T(8,128)(2,1)S(1)}, u32[]{:S(2)}, u32[]{:S(2)}) async-start(bf16[16,24,128]{2,1,0:T(8,128)(2,1)} %bitcast.6), calls=%async_computation | async-start | bytes 196608 | tf_op jit(solution)/shard_map/all_to_all | solution.py:617
  64.6 2.8 %collective-permute-start.6 = (bf16[96,128]{1,0:T(8,128)(2,1)S(1)}, bf16[96,128]{1,0:T(8,128)(2,1)S(1)}, u32[]{:S(2)}, u32[]{:S(2)}) collective-permute-start(bf16[96,128]{1,0:T(8,128)(2,1)S(1)} %get-tuple-element.47.refs_2_), channel_id=1, source_target_pairs={{0,16},{16,0},{32,48},{48,32},{64,80},{80,64},{96,112},{112,96},{1... | collective-permute-start | bytes 73736 | tf_op jit(solution)/shard_map/ppermute | solution.py:510
  67.4 4.7 %shard_map.142.refs_0_.refs_1_ = f32[8,96,256]{2,1,0:T(8,128)S(1)} custom-call(bf16[8,96,256]{2,1,0:T(8,128)(2,1)S(1)} %get-tuple-element.42.refs_5_.refs_0_, f32[7,7,96]{2,1,0:T(8,128)} %bitcast.13, bf16[96,128]{1,0:T(8,128)(2,1)S(1)} %get-tuple-element.47.refs_2_), custom_call_target="tpu_custom_call" | custom-call | tf_op jit(solution)/shard_map/pallas_call | solution.py:48
  72.1 0.0 collective-permute-done.6.refs_3_.refs_2_
  72.1 0.7 all-to-all-done.refs_0_
  72.8 0.7 shard_map.144
  73.5 6.0 %all-to-all-start.1 = ((bf16[32,24,128]{2,1,0:T(8,128)(2,1)}), bf16[32,24,128]{2,1,0:T(8,128)(2,1)S(1)}, u32[]{:S(2)}, u32[]{:S(2)}) async-start(bf16[32,24,128]{2,1,0:T(8,128)(2,1)} %shard_map.144), calls=%async_computation.1 | async-start | bytes 393216 | tf_op jit(solution)/shard_map/all_to_all | solution.py:626
  79.5 3.5 %collective-permute-start.7 = (bf16[96,128]{1,0:T(8,128)(2,1)S(1)}, bf16[96,128]{1,0:T(8,128)(2,1)S(1)}, u32[]{:S(2)}, u32[]{:S(2)}) collective-permute-start(bf16[96,128]{1,0:T(8,128)(2,1)S(1)} %get-tuple-element.50), channel_id=1, source_target_pairs={{0,496},{16,32},{32,16},{48,64},{64,48},{80,96},{96,80},{112,128},... | collective-permute-start | bytes 73736 | tf_op jit(solution)/shard_map/ppermute | solution.py:509
  83.0 1.9 %collective-permute-done.7.refs_4_.refs_1_ = bf16[96,128]{1,0:T(8,128)(2,1)S(1)} collective-permute-done((bf16[96,128]{1,0:T(8,128)(2,1)S(1)}, bf16[96,128]{1,0:T(8,128)(2,1)S(1)}, u32[]{:S(2)}, u32[]{:S(2)}) %collective-permute-start.7) | collective-permute-done | bytes 24608 | tf_op jit(solution)/shard_map/ppermute | solution.py:509
  84.9 6.4 %all-to-all-done.1.refs_0_ = bf16[32,24,128]{2,1,0:T(8,128)(2,1)S(1)} async-done(((bf16[32,24,128]{2,1,0:T(8,128)(2,1)}), bf16[32,24,128]{2,1,0:T(8,128)(2,1)S(1)}, u32[]{:S(2)}, u32[]{:S(2)}) %all-to-all-start.1) | async-done | bytes 196640 | tf_op jit(solution)/shard_map/all_to_all | solution.py:626
  91.3 0.7 shard_map.145
  92.0 5.4 %all-to-all-start.2 = ((f32[16,24,128]{2,1,0:T(8,128)}), f32[16,24,128]{2,1,0:T(8,128)S(1)}, u32[]{:S(2)}, u32[]{:S(2)}) async-start(f32[16,24,128]{2,1,0:T(8,128)} %shard_map.145), calls=%async_computation.2 | async-start | bytes 393216 | tf_op jit(solution)/shard_map/all_to_all | solution.py:630
  97.4 5.8 %shard_map.143 = bf16[96,8,256]{2,1,0:T(8,128)(2,1)} custom-call(f32[8,96,256]{2,1,0:T(8,128)S(1)} %shard_map.142.refs_0_.refs_1_, bf16[3,96,256]{2,1,0:T(8,128)(2,1)S(1)} %get-tuple-element.48.refs_1_, bf16[3,96,256]{2,1,0:T(8,128)(2,1)S(1)} %get-tuple-element.49.refs_2_, bf16[96,128]{1,0:T(8,128)(2,1)S(1)} %collective-permute-done.6.refs_3_.refs_2_, ...), custom_call_target="tpu_custom_call" | custom-call | tf_op jit(solution)/shard_map/pallas_call | solution.py:48
  103.2 4.2 %all-to-all-done.2 = f32[16,24,128]{2,1,0:T(8,128)S(1)} async-done(((f32[16,24,128]{2,1,0:T(8,128)}), f32[16,24,128]{2,1,0:T(8,128)S(1)}, u32[]{:S(2)}, u32[]{:S(2)}) %all-to-all-start.2) | async-done | bytes 196640 | tf_op jit(solution)/shard_map/all_to_all | solution.py:630
  107.4 0.8 shard_map.146
Async XLA Ops:
  2.6 11.8 %collective-permute-start = (bf16[3,96,256]{2,1,0:T(8,128)(2,1)S(1)}, bf16[3,96,256]{2,1,0:T(8,128)(2,1)S(1)}, u32[]{:S(2)}, u32[]{:S(2)}) collective-permute-start(bf16[3,96,256]{2,1,0:T(8,128)(2,1)S(1)} %get-tuple-element.33), channel_id=1, source_target_pairs={{1,2},{2,1},{3,4},{4,3},{5,6},{6,5},{7,8},{8,7},{9,10},{10,9},{11,... | collective-permute-start | bytes 442376 | tf_op jit(solution)/shard_map/ppermute | solution.py:502
  3.2 11.2 %collective-permute-start.1 = (bf16[3,96,256]{2,1,0:T(8,128)(2,1)S(1)}, bf16[3,96,256]{2,1,0:T(8,128)(2,1)S(1)}, u32[]{:S(2)}, u32[]{:S(2)}) collective-permute-start(bf16[3,96,256]{2,1,0:T(8,128)(2,1)S(1)} %get-tuple-element.34), channel_id=1, source_target_pairs={{0,1},{1,0},{2,3},{3,2},{4,5},{5,4},{6,7},{7,6},{8,9},{9,8},{10,11... | collective-permute-start | bytes 442376 | tf_op jit(solution)/shard_map/ppermute | solution.py:503
  15.4 17.0 %collective-permute-start.2 = (bf16[96,128]{1,0:T(8,128)(2,1)S(1)}, bf16[96,128]{1,0:T(8,128)(2,1)S(1)}, u32[]{:S(2)}, u32[]{:S(2)}) collective-permute-start(bf16[96,128]{1,0:T(8,128)(2,1)S(1)} %get-tuple-element.39), channel_id=1, source_target_pairs={{0,496},{16,32},{32,16},{48,64},{64,48},{80,96},{96,80},{112,128},... | collective-permute-start | bytes 73736 | tf_op jit(solution)/shard_map/ppermute | solution.py:509
  19.6 12.8 %collective-permute-start.3 = (bf16[96,128]{1,0:T(8,128)(2,1)S(1)}, bf16[96,128]{1,0:T(8,128)(2,1)S(1)}, u32[]{:S(2)}, u32[]{:S(2)}) collective-permute-start(bf16[96,128]{1,0:T(8,128)(2,1)S(1)} %get-tuple-element.40), channel_id=1, source_target_pairs={{0,16},{16,0},{32,48},{48,32},{64,80},{80,64},{96,112},{112,96},{1... | collective-permute-start | bytes 73736 | tf_op jit(solution)/shard_map/ppermute | solution.py:510
  41.3 12.6 %collective-permute-start.4 = (bf16[3,96,256]{2,1,0:T(8,128)(2,1)S(1)}, bf16[3,96,256]{2,1,0:T(8,128)(2,1)S(1)}, u32[]{:S(2)}, u32[]{:S(2)}) collective-permute-start(bf16[3,96,256]{2,1,0:T(8,128)(2,1)S(1)} %get-tuple-element.43), channel_id=1, source_target_pairs={{1,2},{2,1},{3,4},{4,3},{5,6},{6,5},{7,8},{8,7},{9,10},{10,9},{11,... | collective-permute-start | bytes 442376 | tf_op jit(solution)/shard_map/ppermute | solution.py:502
  42.0 11.9 %collective-permute-start.5 = (bf16[3,96,256]{2,1,0:T(8,128)(2,1)S(1)}, bf16[3,96,256]{2,1,0:T(8,128)(2,1)S(1)}, u32[]{:S(2)}, u32[]{:S(2)}) collective-permute-start(bf16[3,96,256]{2,1,0:T(8,128)(2,1)S(1)} %get-tuple-element.44), channel_id=1, source_target_pairs={{0,1},{1,0},{2,3},{3,2},{4,5},{5,4},{6,7},{7,6},{8,9},{9,8},{10,11... | collective-permute-start | bytes 442376 | tf_op jit(solution)/shard_map/ppermute | solution.py:503
  55.4 17.4 %all-to-all-start = ((bf16[16,24,128]{2,1,0:T(8,128)(2,1)}), bf16[16,24,128]{2,1,0:T(8,128)(2,1)S(1)}, u32[]{:S(2)}, u32[]{:S(2)}) async-start(bf16[16,24,128]{2,1,0:T(8,128)(2,1)} %bitcast.6), calls=%async_computation | async-start | bytes 196608 | tf_op jit(solution)/shard_map/all_to_all | solution.py:617
  64.6 7.5 %collective-permute-start.6 = (bf16[96,128]{1,0:T(8,128)(2,1)S(1)}, bf16[96,128]{1,0:T(8,128)(2,1)S(1)}, u32[]{:S(2)}, u32[]{:S(2)}) collective-permute-start(bf16[96,128]{1,0:T(8,128)(2,1)S(1)} %get-tuple-element.47.refs_2_), channel_id=1, source_target_pairs={{0,16},{16,0},{32,48},{48,32},{64,80},{80,64},{96,112},{112,96},{1... | collective-permute-start | bytes 73736 | tf_op jit(solution)/shard_map/ppermute | solution.py:510
  73.5 17.8 %all-to-all-start.1 = ((bf16[32,24,128]{2,1,0:T(8,128)(2,1)}), bf16[32,24,128]{2,1,0:T(8,128)(2,1)S(1)}, u32[]{:S(2)}, u32[]{:S(2)}) async-start(bf16[32,24,128]{2,1,0:T(8,128)(2,1)} %shard_map.144), calls=%async_computation.1 | async-start | bytes 393216 | tf_op jit(solution)/shard_map/all_to_all | solution.py:626
  79.5 5.4 %collective-permute-start.7 = (bf16[96,128]{1,0:T(8,128)(2,1)S(1)}, bf16[96,128]{1,0:T(8,128)(2,1)S(1)}, u32[]{:S(2)}, u32[]{:S(2)}) collective-permute-start(bf16[96,128]{1,0:T(8,128)(2,1)S(1)} %get-tuple-element.50), channel_id=1, source_target_pairs={{0,496},{16,32},{32,16},{48,64},{64,48},{80,96},{96,80},{112,128},... | collective-permute-start | bytes 73736 | tf_op jit(solution)/shard_map/ppermute | solution.py:509
  92.0 15.3 %all-to-all-start.2 = ((f32[16,24,128]{2,1,0:T(8,128)}), f32[16,24,128]{2,1,0:T(8,128)S(1)}, u32[]{:S(2)}, u32[]{:S(2)}) async-start(f32[16,24,128]{2,1,0:T(8,128)} %shard_map.145), calls=%async_computation.2 | async-start | bytes 393216 | tf_op jit(solution)/shard_map/all_to_all | solution.py:630
